TPU v7x, 32 devices: a whole 2x2x4 slice. The times are simulated.
32 devices in a mesh: dp: 8 (over y, x, core), mp: 4 (over z).
Axes of the slice: x: 2, y: 2, z: 4, core: 2. Of those that a mesh axis runs over, the one named last changes fastest.
Arguments:
- inputs: bfloat16 [10240, 768], P(('dp', 'mp')), may hold values from -6 to 6
- encoded: bfloat16 [16384, 768], P(('dp', 'mp')), may hold values from -6 to 6
- cotangent: bfloat16 [10240, 768], P(('dp', 'mp')), may hold values from -6 to 6
- lengths: int32 [16], P('dp'), may hold values from 224 to 640, as said below
- buckets: int32 [640], replicated, may hold values from 0 to 31
- self_gain: float32 [768], replicated, may hold values from 0.5 to 1.5
- self_query: bfloat16 [768, 768], P(None, 'mp'), may hold values from -0.078125 to 0.078125
- self_key: bfloat16 [768, 768], P(None, 'mp'), may hold values from -0.078125 to 0.078125
- self_value: bfloat16 [768, 768], P(None, 'mp'), may hold values from -0.21875 to 0.21875
- self_output: bfloat16 [768, 768], P('mp'), may hold values from -3 to 3
- bias_table: float32 [32, 12], P(None, 'mp'), may hold values from -4 to 4
- cross_gain: float32 [768], replicated, may hold values from 0.5 to 1.5
- cross_query: bfloat16 [768, 768], P(None, 'mp'), may hold values from -0.078125 to 0.078125
- cross_key: bfloat16 [768, 768], P(None, 'mp'), may hold values from -0.078125 to 0.078125
- cross_value: bfloat16 [768, 768], P(None, 'mp'), may hold values from -0.21875 to 0.21875
- cross_output: bfloat16 [768, 768], P('mp'), may hold values from -3.5 to 3.5
- feed_gain: float32 [768], replicated, may hold values from 0.5 to 1.5
- feed_inner: bfloat16 [768, 3072], P(None, 'mp'), may hold values from -0.21875 to 0.21875
- feed_output_weight: bfloat16 [3072, 768], P('mp'), may hold values from -0.15625 to 0.15625
Outputs:
- result: bfloat16 [10240, 768], P(('dp', 'mp'))
- input_grad: bfloat16 [10240, 768], P(('dp', 'mp'))
- encoder_grad: bfloat16 [16384, 768], P(('dp', 'mp'))
- grad_self_gain: float32 [768], replicated
- grad_self_query: float32 [768, 768], P('dp', 'mp')
- grad_self_key: float32 [768, 768], P('dp', 'mp')
- grad_self_value: float32 [768, 768], P('dp', 'mp')
- grad_self_output: float32 [768, 768], P('mp', 'dp')
- grad_bias_table: float32 [32, 12], P(None, 'mp')
- grad_cross_gain: float32 [768], replicated
- grad_cross_query: float32 [768, 768], P('dp', 'mp')
- grad_cross_key: float32 [768, 768], P('dp', 'mp')
- grad_cross_value: float32 [768, 768], P('dp', 'mp')
- grad_cross_output: float32 [768, 768], P('mp', 'dp')
- grad_feed_gain: float32 [768], replicated
- grad_feed_inner: float32 [768, 3072], P('dp', 'mp')
- grad_feed_outer: float32 [3072, 768], P('mp', 'dp')
Inputs may be any that keep to these rules, and one draw needn't show every extreme that they name: `lengths`: each length is 640 or 224; both occur.
All inputs are finite; a program needn't handle non-finite values.
Results may differ from a plain program's by a relative error of at most 0.024.
Values may be sent and summed in bfloat16 or wider, within the bound.
A program may use at most 384 MiB of HBM per device.

v0:
```python
import jax
import jax.numpy as jnp
from jax import lax
from jax.sharding import PartitionSpec as P

eps_norm = 1e-06
masked_value = -1e30


def norm_rows(values, gain):
    inv_root = lax.rsqrt(jnp.mean(values * values, axis=-1, keepdims=True) + eps_norm)
    normal = values * inv_root
    return (normal * gain, normal, inv_root)


def norm_back(grad, normal, inv_root, gain):
    scaled_grad = grad * gain
    grad_in = inv_root * (
        scaled_grad - normal * jnp.mean(scaled_grad * normal, axis=-1, keepdims=True)
    )
    return (grad_in, jnp.sum(grad * normal, axis=0))


def matmul(left_side, right_side):
    return jnp.dot(left_side, right_side, preferred_element_type=jnp.float32)


def transposed_left_product(left_side, right_side):
    return lax.dot_general(
        left_side, right_side, (((0,), (0,)), ((), ())), preferred_element_type=jnp.float32
    )


def matmul_nt(left_side, right_side):
    return lax.dot_general(
        left_side, right_side, (((1,), (1,)), ((), ())), preferred_element_type=jnp.float32
    )


def low16(values):
    return values.astype(jnp.bfloat16)


def smooth_act(values):
    return jax.nn.gelu(values, approximate=True)


def split_heads(values, seq_count, head_count):
    return values.reshape(
        seq_count, values.shape[0] // seq_count, head_count, values.shape[1] // head_count
    )


def join_heads(values):
    return values.reshape(values.shape[0] * values.shape[1], values.shape[2] * values.shape[3])


def row_terms(pairs):
    summed = None
    for left_side, right_side, contract in pairs:
        partial_value = lax.dot_general(
            left_side,
            right_side,
            (((1,), (contract,)), ((), ())),
            preferred_element_type=jnp.float32,
        )
        summed = partial_value if summed is None else summed + partial_value
    return summed


def reduce_rows(pairs):
    return lax.psum_scatter(row_terms(pairs), "mp", scatter_dimension=0, tiled=True)


def gather_rows(normed):
    return lax.all_gather(low16(normed), "mp", axis=0, tiled=True)


def gather_grad(grad):
    return lax.all_gather(low16(grad), "mp", axis=0, tiled=True)


def attend_scores(query_rows, key_rows, bias_grid, valid_mask):
    scores = jnp.einsum("qhd,khd->hqk", query_rows, key_rows, preferred_element_type=jnp.float32)
    if bias_grid is not None:
        scores = jnp.where(valid_mask[None], scores + bias_grid, masked_value)
    return scores


def attend_forward(query_rows, key_rows, value_rows, bias_grid, valid_mask):
    scores = attend_scores(query_rows, key_rows, bias_grid, valid_mask)
    largest = jnp.max(scores, axis=-1, keepdims=True)
    shifted = jnp.exp(scores - largest)
    summed = jnp.sum(shifted, axis=-1, keepdims=True)
    weights = low16(shifted / summed)
    mixed = low16(
        jnp.einsum("hqk,khd->qhd", weights, value_rows, preferred_element_type=jnp.float32)
    )
    return (mixed, (largest + jnp.log(summed))[..., 0])


def attend_back(query_rows, key_rows, value_rows, grad_rows, log_total, bias_grid, valid_mask):
    scores = attend_scores(query_rows, key_rows, bias_grid, valid_mask)
    weights = jnp.exp(scores - log_total[..., None])
    weights_low = low16(weights)
    mixed = low16(
        jnp.einsum("hqk,khd->qhd", weights_low, value_rows, preferred_element_type=jnp.float32)
    )
    grad_weights = jnp.einsum(
        "qhd,khd->hqk", grad_rows, value_rows, preferred_element_type=jnp.float32
    )
    centre = jnp.sum(weights * grad_weights, axis=-1, keepdims=True)
    grad_scores = low16(weights * (grad_weights - centre))
    grad_query = low16(
        jnp.einsum("hqk,khd->qhd", grad_scores, key_rows, preferred_element_type=jnp.float32)
    )
    grad_key = low16(
        jnp.einsum("hqk,qhd->khd", grad_scores, query_rows, preferred_element_type=jnp.float32)
    )
    grad_value = low16(
        jnp.einsum("hqk,qhd->khd", weights_low, grad_rows, preferred_element_type=jnp.float32)
    )
    return (mixed, grad_query, grad_key, grad_value, grad_scores)


def body(
    inputs,
    encoded,
    cotangent,
    lengths,
    buckets,
    self_gain,
    self_query,
    self_key,
    self_value,
    self_output,
    bias_table,
    cross_gain,
    cross_query,
    cross_key,
    cross_value,
    cross_output,
    feed_gain,
    feed_inner,
    feed_output_weight,
):
    seq_here = lengths.shape[0]
    slots = buckets.shape[0]
    bucket_count = bias_table.shape[0]
    heads_here = bias_table.shape[1]
    positions = lax.iota(jnp.int32, slots)
    offsets = jnp.maximum(positions[:, None] - positions[None, :], 0)
    bucket_grid = jnp.take(buckets, offsets)
    bucket_onehot = (buckets[:, None] == lax.iota(jnp.int32, bucket_count)[None, :]).astype(
        jnp.float32
    )
    by_offset = jnp.dot(bucket_onehot, bias_table, precision=lax.Precision.HIGHEST)
    bias_grid = jnp.transpose(jnp.take(by_offset, offsets, axis=0), (2, 0, 1))
    causal = positions[None, :] <= positions[:, None]

    def self_mask(length):
        return causal & (positions[None, :] < length)

    def self_project(normed):
        gathered = gather_rows(normed)
        query_all = split_heads(low16(matmul(gathered, self_query)), seq_here, heads_here)
        key_all = split_heads(low16(matmul(gathered, self_key)), seq_here, heads_here)
        value_all = split_heads(low16(matmul(gathered, self_value)), seq_here, heads_here)
        return (gathered, query_all, key_all, value_all)

    def self_forward(sequence_in):
        query_rows, key_rows, value_rows, length = sequence_in
        return attend_forward(query_rows, key_rows, value_rows, bias_grid, self_mask(length))

    def cross_forward(sequence_in):
        query_rows, key_rows, value_rows = sequence_in
        return attend_forward(query_rows, key_rows, value_rows, None, None)

    resid_in = inputs.astype(jnp.float32)
    normed_one = norm_rows(resid_in, self_gain)[0]
    first_gathered_rows, query_one, key_one, value_one = self_project(normed_one)
    mixed_one, logs_one = lax.map(self_forward, (query_one, key_one, value_one, lengths))
    resid_one = resid_in + reduce_rows(((join_heads(mixed_one), self_output, 0),))
    enc_whole = lax.all_gather(encoded, "mp", axis=0, tiled=True)
    cross_keys = low16(matmul(enc_whole, cross_key))
    cross_values = low16(matmul(enc_whole, cross_value))
    key_two = split_heads(cross_keys, seq_here, heads_here)
    value_two = split_heads(cross_values, seq_here, heads_here)
    normed_two = norm_rows(resid_one, cross_gain)[0]
    gathered_two = gather_rows(normed_two)
    query_two = split_heads(low16(matmul(gathered_two, cross_query)), seq_here, heads_here)
    mixed_two, logs_two = lax.map(cross_forward, (query_two, key_two, value_two))
    resid_two = resid_one + reduce_rows(((join_heads(mixed_two), cross_output, 0),))
    normed_three = norm_rows(resid_two, feed_gain)[0]
    gathered_three = gather_rows(normed_three)
    hidden = low16(smooth_act(matmul(gathered_three, feed_inner)))
    outcome = resid_two + reduce_rows(((hidden, feed_output_weight, 0),))
    grad_out = cotangent.astype(jnp.float32)
    normed_three, hat_three, root_three = norm_rows(resid_two, feed_gain)
    gathered_three = gather_rows(normed_three)
    before_act = matmul(gathered_three, feed_inner)
    activated, act_pull = jax.vjp(smooth_act, before_act)
    hidden = low16(activated)
    grad_rows = gather_grad(grad_out)
    grad_outer = transposed_left_product(hidden, grad_rows)
    grad_hidden = low16(matmul_nt(grad_rows, feed_output_weight))
    grad_pre = low16(act_pull(grad_hidden.astype(jnp.float32))[0])
    grad_inner = transposed_left_product(gathered_three, grad_pre)
    grad_normed = reduce_rows(((grad_pre, feed_inner, 1),))
    grad_resid, gain_three = norm_back(grad_normed, hat_three, root_three, feed_gain)
    grad_two = grad_out + grad_resid
    normed_two, hat_two, root_two = norm_rows(resid_one, cross_gain)
    gathered_two = gather_rows(normed_two)
    query_two = split_heads(low16(matmul(gathered_two, cross_query)), seq_here, heads_here)
    grad_rows = gather_grad(grad_two)
    grad_mixed = split_heads(low16(matmul_nt(grad_rows, cross_output)), seq_here, heads_here)

    def cross_back(sequence_in):
        query_rows, key_rows, value_rows, grad_seq, log_total = sequence_in
        mixed, grad_query, grad_key, grad_value, unused_scores = attend_back(
            query_rows, key_rows, value_rows, grad_seq, log_total, None, None
        )
        return (mixed, grad_query, grad_key, grad_value)

    mixed_two, gq_two, gk_two, gv_two = lax.map(
        cross_back, (query_two, key_two, value_two, grad_mixed, logs_two)
    )
    mixed_two = join_heads(mixed_two)
    gq_two = join_heads(gq_two)
    gk_two = join_heads(gk_two)
    gv_two = join_heads(gv_two)
    grad_cout = transposed_left_product(mixed_two, grad_rows)
    grad_cquery = transposed_left_product(gathered_two, gq_two)
    grad_normed = reduce_rows(((gq_two, cross_query, 1),))
    grad_ckey = transposed_left_product(enc_whole, gk_two)
    grad_cvalue = transposed_left_product(enc_whole, gv_two)
    encoder_grad = lax.psum_scatter(
        row_terms(((gk_two, cross_key, 1), (gv_two, cross_value, 1))).astype(jnp.bfloat16),
        "mp",
        scatter_dimension=0,
        tiled=True,
    ).astype(jnp.float32)
    grad_resid, gain_two = norm_back(grad_normed, hat_two, root_two, cross_gain)
    grad_one = grad_two + grad_resid
    normed_one, hat_one, root_one = norm_rows(resid_in, self_gain)
    first_gathered_rows, query_one, key_one, value_one = self_project(normed_one)
    grad_rows = gather_grad(grad_one)
    grad_mixed = split_heads(low16(matmul_nt(grad_rows, self_output)), seq_here, heads_here)

    def self_back(score_sum, sequence_in):
        query_rows, key_rows, value_rows, grad_seq, log_total, length = sequence_in
        mixed, grad_query, grad_key, grad_value, grad_scores = attend_back(
            query_rows, key_rows, value_rows, grad_seq, log_total, bias_grid, self_mask(length)
        )
        return (
            score_sum + grad_scores.astype(jnp.float32),
            (mixed, grad_query, grad_key, grad_value),
        )

    score_start = jnp.zeros((heads_here, slots, slots), jnp.float32)
    score_sum, (mixed_one, gq_one, first_key_gradient, gv_one) = lax.scan(
        self_back, score_start, (query_one, key_one, value_one, grad_mixed, logs_one, lengths)
    )
    mixed_one = join_heads(mixed_one)
    gq_one = join_heads(gq_one)
    first_key_gradient = join_heads(first_key_gradient)
    gv_one = join_heads(gv_one)
    grad_sout = transposed_left_product(mixed_one, grad_rows)
    grad_squery = transposed_left_product(first_gathered_rows, gq_one)
    self_key_gradient = transposed_left_product(first_gathered_rows, first_key_gradient)
    grad_svalue = transposed_left_product(first_gathered_rows, gv_one)
    grad_normed = reduce_rows(
        ((gq_one, self_query, 1), (first_key_gradient, self_key, 1), (gv_one, self_value, 1))
    )
    grad_resid, gain_one = norm_back(grad_normed, hat_one, root_one, self_gain)
    input_grad = grad_one + grad_resid
    (
        grad_squery,
        self_key_gradient,
        grad_svalue,
        grad_sout,
        grad_cquery,
        grad_ckey,
        grad_cvalue,
        grad_cout,
        grad_inner,
        grad_outer,
    ) = (
        lax.psum_scatter(grad_squery, "dp", scatter_dimension=0, tiled=True),
        lax.psum_scatter(self_key_gradient, "dp", scatter_dimension=0, tiled=True),
        lax.psum_scatter(grad_svalue, "dp", scatter_dimension=0, tiled=True),
        lax.psum_scatter(grad_sout, "dp", scatter_dimension=1, tiled=True),
        lax.psum_scatter(grad_cquery, "dp", scatter_dimension=0, tiled=True),
        lax.psum_scatter(grad_ckey, "dp", scatter_dimension=0, tiled=True),
        lax.psum_scatter(grad_cvalue, "dp", scatter_dimension=0, tiled=True),
        lax.psum_scatter(grad_cout, "dp", scatter_dimension=1, tiled=True),
        lax.psum_scatter(grad_inner, "dp", scatter_dimension=0, tiled=True),
        lax.psum_scatter(grad_outer, "dp", scatter_dimension=1, tiled=True),
    )
    block_count = 4
    block_rows = slots // block_count
    sums_blocked = jnp.transpose(
        score_sum.reshape(heads_here, block_count, block_rows * slots), (1, 0, 2)
    )
    grid_blocked = bucket_grid.reshape(block_count, block_rows * slots)

    def bucket_block(block_in):
        sums_part, grid_part = block_in
        one_hot = (grid_part[:, None] == lax.iota(jnp.int32, bucket_count)[None, :]).astype(
            jnp.float32
        )
        return jnp.dot(sums_part, one_hot, precision=lax.Precision.HIGHEST)

    table_local = jnp.transpose(
        jnp.sum(lax.map(bucket_block, (sums_blocked, grid_blocked)), axis=0)
    )
    column_start = lax.axis_index("mp") * heads_here
    table_full = lax.dynamic_update_slice(
        jnp.zeros((bucket_count, heads_here * lax.axis_size("mp")), jnp.float32),
        table_local,
        (jnp.int32(0), column_start),
    )
    gain_one, gain_two, gain_three, table_all = lax.psum(
        (gain_one, gain_two, gain_three, table_full), ("dp", "mp")
    )
    table_mine = lax.dynamic_slice_in_dim(table_all, column_start, heads_here, 1)
    return (
        low16(outcome),
        low16(input_grad),
        low16(encoder_grad),
        gain_one,
        grad_squery,
        self_key_gradient,
        grad_svalue,
        grad_sout,
        table_mine,
        gain_two,
        grad_cquery,
        grad_ckey,
        grad_cvalue,
        grad_cout,
        gain_three,
        grad_inner,
        grad_outer,
    )


def solution(mesh):
    return jax.shard_map(
        body,
        mesh=mesh,
        in_specs=(
            P(("dp", "mp"), None),
            P(("dp", "mp"), None),
            P(("dp", "mp"), None),
            P("dp"),
            P(),
            P(),
            P(None, "mp"),
            P(None, "mp"),
            P(None, "mp"),
            P("mp", None),
            P(None, "mp"),
            P(),
            P(None, "mp"),
            P(None, "mp"),
            P(None, "mp"),
            P("mp", None),
            P(),
            P(None, "mp"),
            P("mp", None),
        ),
        out_specs=(
            P(("dp", "mp"), None),
            P(("dp", "mp"), None),
            P(("dp", "mp"), None),
            P(),
            P("dp", "mp"),
            P("dp", "mp"),
            P("dp", "mp"),
            P("mp", "dp"),
            P(None, "mp"),
            P(),
            P("dp", "mp"),
            P("dp", "mp"),
            P("dp", "mp"),
            P("mp", "dp"),
            P(),
            P("dp", "mp"),
            P("mp", "dp"),
        ),
        check_vma=False,
    )
```

profile of v0, /device:TPU:0, one launch (start us, length us, event | category | flops | bytes accessed | tf_op | source)
XLA Modules:
  0.0 5771.9 jit_solution(10008595993746313695)
XLA Ops:
  14.7 1352.2 %gather_fusion = f32[409600,3]{1,0:T(8,128)} fusion(f32[640,3]{1,0:T(8,128)S(1)} %fusion.148, s32[409600]{0:T(1024)S(1)} %broadcast_clamp_fusion), kind=kCustom, calls=%fused_computation | custom fusion | bytes 11468800 | tf_op jit(solution)/shard_map/jit(_take)/gather | solution.py:158
  1366.9 109.1 %copy.135 = f32[640,640,3]{0,1,2:T(8,128)} copy(f32[640,640,3]{2,1,0:T(8,128)} %bitcast.22) | data formatting | bytes 9830400 | tf_op jit(solution)/shard_map/jit(_take)/gather | solution.py:158
  1489.2 13.4 while.73
  1506.8 74.7 %reduce-scatter.26.cloned.1.call-done = f32[320,768]{1,0:T(8,128)} async-done(((f32[1280,768]{1,0:T(8,128)}), f32[320,768]{1,0:T(8,128)}) %reduce-scatter.26.cloned.1.call-update) | async-done | bytes 983056 | tf_op jit(solution)/shard_map/reduce_scatter | solution.py:72
  1585.1 61.9 %all-gather.10.cloned.1.call-done = bf16[2048,768]{1,0:T(8,128)(2,1)} async-done(((bf16[512,768]{1,0:T(8,128)(2,1)}), bf16[2048,768]{1,0:T(8,128)(2,1)}) %all-gather.10.cloned.1.call-update) | async-done | bytes 3145744 | tf_op jit(solution)/shard_map/all_gather | solution.py:184
  1656.8 34.4 all-gather.12.cloned.1.call-done
  1697.0 13.0 while.70
  1714.2 72.1 %reduce-scatter.28.cloned.1.call-done = f32[320,768]{1,0:T(8,128)} async-done(((f32[1280,768]{1,0:T(8,128)}), f32[320,768]{1,0:T(8,128)}) %reduce-scatter.28.cloned.1.call-update) | async-done | bytes 983056 | tf_op jit(solution)/shard_map/reduce_scatter | solution.py:72
  1791.2 42.9 all-gather.14.cloned.1.call-done
  1839.2 38.8 all-gather.16.cloned.1.call-done
  1889.7 71.6 %reduce-scatter.32.cloned.1.call-done = f32[320,768]{1,0:T(8,128)} async-done(((f32[1280,768]{1,0:T(8,128)}), f32[320,768]{1,0:T(8,128)}) %reduce-scatter.32.cloned.1.call-update) | async-done | bytes 983056 | tf_op jit(solution)/shard_map/reduce_scatter | solution.py:72
  1966.1 43.8 all-gather.18.cloned.1.call-done
  2013.4 25.8 while.71
  2050.4 65.0 %reduce-scatter.34.cloned.1.call-done = f32[320,768]{1,0:T(8,128)} async-done(((f32[1280,768]{1,0:T(8,128)}), f32[320,768]{1,0:T(8,128)}) %reduce-scatter.34.cloned.1.call-update) | async-done | bytes 983056 | tf_op jit(solution)/shard_map/reduce_scatter | solution.py:72
  2117.5 73.2 %reduce-scatter.30.cloned.1.call-done = f32[320,768]{1,0:T(8,128)} async-done(((f32[1280,768]{1,0:T(8,128)}), f32[320,768]{1,0:T(8,128)}) %reduce-scatter.30.cloned.1.call-update) | async-done | bytes 983056 | tf_op jit(solution)/shard_map/reduce_scatter | solution.py:72
  2199.7 38.6 all-gather.20.cloned.1.call-done
  2243.4 39.4 while.74
  2251.3 7.2 select_add_fusion.2
  2270.4 8.6 select_add_fusion.2
  2331.5 3311.4 %gather_fusion.1 = s32[409600]{0:T(1024)} fusion(s32[640]{0:T(1024)S(1)} %copy-done.3, s32[409600]{0:T(1024)S(1)} %copy-done.18), kind=kCustom, calls=%fused_computation.1 | custom fusion | bytes 4915200 | tf_op jit(solution)/shard_map/jit(_take)/gather | solution.py:153
  5659.2 7.1 copy.159
  5666.3 6.8 reshape.287
  5676.4 41.7 while.72
  5721.7 39.6 all-reduce
  (438 shorter events, 296.3 us)
Async XLA Ops:
  7.2 1474.3 %all-gather.8.cloned.1.call-start = ((), (), s32[]{:S(2)}) async-start(), calls=%async_computation.17 | async-start | bytes 2457600 | tf_op jit(solution)/shard_map/all_gather | solution.py:76
  11.2 1570.3 %reduce-scatter.26.cloned.1.call-start = ((), (), s32[]{:S(2)}) async-start(), calls=%async_computation.18 | async-start | bytes 4915200 | tf_op jit(solution)/shard_map/reduce_scatter | solution.py:72
  1506.0 141.0 %all-gather.10.cloned.1.call-start = ((), (), s32[]{:S(2)}) async-start(), calls=%async_computation.19 | async-start | bytes 3932160 | tf_op jit(solution)/shard_map/all_gather | solution.py:184
  1506.7 184.5 %all-gather.12.cloned.1.call-start = ((), (), s32[]{:S(2)}) async-start(), calls=%async_computation.20 | async-start | bytes 2457600 | tf_op jit(solution)/shard_map/all_gather | solution.py:76
  1584.8 201.5 %reduce-scatter.28.cloned.1.call-start = ((), (), s32[]{:S(2)}) async-start(), calls=%async_computation.21 | async-start | bytes 4915200 | tf_op jit(solution)/shard_map/reduce_scatter | solution.py:72
  1714.2 119.9 %all-gather.14.cloned.1.call-start = ((), (), s32[]{:S(2)}) async-start(), calls=%async_computation.22 | async-start | bytes 2457600 | tf_op jit(solution)/shard_map/all_gather | solution.py:76
  1790.0 88.1 %all-gather.16.cloned.1.call-start = ((), (), s32[]{:S(2)}) async-start(), calls=%async_computation.24 | async-start | bytes 2457600 | tf_op jit(solution)/shard_map/all_gather | solution.py:80
  1790.7 170.6 %reduce-scatter.32.cloned.1.call-start = ((), (), s32[]{:S(2)}) async-start(), calls=%async_computation.25 | async-start | bytes 4915200 | tf_op jit(solution)/shard_map/reduce_scatter | solution.py:72
  1889.6 120.3 %all-gather.18.cloned.1.call-start = ((), (), s32[]{:S(2)}) async-start(), calls=%async_computation.26 | async-start | bytes 2457600 | tf_op jit(solution)/shard_map/all_gather | solution.py:80
  1965.9 149.4 %reduce-scatter.34.cloned.1.call-start = ((), (), s32[]{:S(2)}) async-start(), calls=%async_computation.27 | async-start | bytes 4915200 | tf_op jit(solution)/shard_map/reduce_scatter | solution.py:72
  2043.7 147.0 %reduce-scatter.30.cloned.1.call-start = ((), (), s32[]{:S(2)}) async-start(), calls=%async_computation.23 | async-start | bytes 4915200 | tf_op jit(solution)/shard_map/reduce_scatter | solution.py:72
  2050.3 188.0 %all-gather.20.cloned.1.call-start = ((), (), s32[]{:S(2)}) async-start(), calls=%async_computation.28 | async-start | bytes 2457600 | tf_op jit(solution)/shard_map/all_gather | solution.py:80
  2194.2 3463.4 %reduce-scatter.58.cloned.1.call-start = ((), (), s32[]{:S(2)}) async-start(), calls=%async_computation.40 | async-start | bytes 884736
  2199.7 3518.6 %reduce-scatter.52.cloned.1.call-start = ((), (), s32[]{:S(2)}) async-start(), calls=%async_computation.37 | async-start | bytes 884736
  2292.1 3427.9 %reduce-scatter.36.cloned.1.call-start = ((), (), s32[]{:S(2)}) async-start(), calls=%async_computation.29 | async-start | bytes 4915200 | tf_op jit(solution)/shard_map/reduce_scatter | solution.py:72
  2298.0 3466.5 %reduce-scatter.48.cloned.1.call-start = ((), (), s32[]{:S(2)}) async-start(), calls=%async_computation.35 | async-start | bytes 2654208 | tf_op jit(solution)/shard_map/reduce_scatter | solution.py:297
  2304.4 3460.1 %reduce-scatter.50.cloned.1.call-start = ((), (), s32[]{:S(2)}) async-start(), calls=%async_computation.36 | async-start | bytes 2654208 | tf_op jit(solution)/shard_map/reduce_scatter | solution.py:298
  2310.8 3453.7 %reduce-scatter.46.cloned.1.call-start = ((), (), s32[]{:S(2)}) async-start(), calls=%async_computation.34 | async-start | bytes 884736 | tf_op jit(solution)/shard_map/reduce_scatter | solution.py:293
  2314.1 3450.3 %reduce-scatter.54.cloned.1.call-start = ((), (), s32[]{:S(2)}) async-start(), calls=%async_computation.38 | async-start | bytes 884736
  2319.2 3445.3 %reduce-scatter.56.cloned.1.call-start = ((), (), s32[]{:S(2)}) async-start(), calls=%async_computation.39 | async-start | bytes 884736
  2324.2 3440.3 %reduce-scatter.38.cloned.1.call-start = ((), (), s32[]{:S(2)}) async-start(), calls=%async_computation.30 | async-start | bytes 3932160 | tf_op jit(solution)/shard_map/reduce_scatter | solution.py:237
  2328.1 3436.5 %reduce-scatter.40.cloned.1.call-start = ((), (), s32[]{:S(2)}) async-start(), calls=%async_computation.31 | async-start | bytes 884736 | tf_op jit(solution)/shard_map/reduce_scatter | solution.py:289
  2331.4 3433.2 %reduce-scatter.42.cloned.1.call-start = ((), (), s32[]{:S(2)}) async-start(), calls=%async_computation.32 | async-start | bytes 884736 | tf_op jit(solution)/shard_map/reduce_scatter | solution.py:290
  5654.0 110.6 %reduce-scatter.44.cloned.1.call-start = ((), (), s32[]{:S(2)}) async-start(), calls=%async_computation.33 | async-start | bytes 884736 | tf_op jit(solution)/shard_map/reduce_scatter | solution.py:291
  (93 other events, 5042.5 us)
Sparse Core Ops, SparseCore 0:
  11.3 46.2 all-gather.7
  1506.1 75.3 reduce-scatter.25
  1583.1 63.8 all-gather.9
  1648.9 42.1 all-gather.11
  1714.3 72.0 reduce-scatter.27
  1790.1 43.8 all-gather.13
  1835.6 42.3 all-gather.15
  1889.8 71.5 reduce-scatter.31
  1966.0 43.8 all-gather.17
  2043.8 71.5 reduce-scatter.33
  2117.7 73.0 reduce-scatter.29
  2194.3 43.9 all-gather.19
  2241.4 33.8 reduce-scatter.57
  2292.2 33.9 reduce-scatter.51
  2328.4 72.6 reduce-scatter.35
  2404.9 42.8 reduce-scatter.47
  2451.9 42.4 reduce-scatter.49
  2498.0 34.9 reduce-scatter.45
  2536.7 34.9 reduce-scatter.53
  2575.3 34.9 reduce-scatter.55
  2613.2 60.2 reduce-scatter.37
  2677.2 35.0 reduce-scatter.39
  5654.1 33.9 reduce-scatter.41
  5691.7 34.9 reduce-scatter.43
where the time goes:
time: 5780 us; the launch traced here: 5770 us
  local copies, waits for them, and re-layouts  4860 us (84%)
  waiting for transfers between devices  619 us (11%)
  matrix products  174 us (3%)
  other arithmetic  65 us (1%)
    gather x2, local copies, waits for them, and re-layouts, body(): bucket_grid = jnp.take(buckets, offsets)  3310 us
    gather x2, local copies, waits for them, and re-layouts, body(): bias_grid = jnp.transpose(jnp.take(by_offset, offsets, axis=0), (2, 0, 1))  1460 us
    reduce_scatter x6, waiting for transfers between devices, reduce_rows(): lax.psum_scatter(row_terms(pairs), 'mp', scatter_dimension=0, tiled=True)  357 us
    all_gather x3, waiting for transfers between devices, gather_grad(): return lax.all_gather(low16(grad), 'mp', axis=0, tiled=True)  121 us
  transfers between devices with their start and end apart: 24, of which 11 were waited for; matrix products, arithmetic and copies ran while one was open for 86% of the time, Pallas kernels for 0%

commit v1 on v0

v1 whole, which is shorter than its diff:
```python
import functools

import jax
import jax.numpy as jnp
from jax import lax
from jax.experimental import pallas as pl
from jax.experimental.pallas import tpu as pltpu
from jax.sharding import PartitionSpec as P

EPS = 1e-06
MASKED = -1e30
DH = 64
F32 = jnp.float32
BF16 = jnp.bfloat16
VMEM_BYTES = 62 << 20
ROOT = 0.7978845608028654
CUBE = 0.044715


def mm(a, b):
    return jnp.dot(a, b, preferred_element_type=F32)


def mm_nt(a, b):
    return lax.dot_general(a, b, (((1,), (1,)), ((), ())), preferred_element_type=F32)


def low(v):
    return v.astype(BF16)


def flip(v):
    return jnp.transpose(v.astype(F32)).astype(BF16)


def norm_rows(v, gain):
    root = lax.rsqrt(jnp.mean(v * v, axis=-1, keepdims=True) + EPS)
    unit = v * root
    return unit * gain, unit, root


def norm_back(grad, v, gain):
    _, unit, root = norm_rows(v, gain)
    scaled = grad * gain
    back = root * (scaled - unit * jnp.mean(scaled * unit, axis=-1, keepdims=True))
    return back, jnp.sum(grad * unit, axis=0, keepdims=True)


def half_of_sequence(halves):
    return lax.rem(lax.axis_index("mp"), halves)


def chunks(rows, step):
    return [(r, min(step, rows - r)) for r in range(0, rows, step)]


def forward_kernel(
    halves,
    len_ref,
    x_ref,
    xa_ref,
    enc_hbm,
    gains_ref,
    diag_ref,
    w_hbm,
    result_ref,
    n1_out,
    q1_out,
    kv1_out,
    p1_out,
    o1_out,
    l1_out,
    x1_out,
    n2_out,
    q2_out,
    kv2_out,
    p2_out,
    o2_out,
    l2_out,
    x2_out,
    n3_out,
    hid_out,
    slope_out,
    w,
    enc,
    mask,
    s_buf,
    n1,
    q1,
    kv1,
    p1,
    o1,
    x1,
    n2,
    q2,
    kv2,
    p2,
    o2,
    x2,
    n3,
    hid,
    slope,
    l1,
    l2,
    acc,
    w_sem,
    enc_sem,
    out_sem,
):
    rows = x_ref.shape[0]
    parts = w.shape[1]
    half = half_of_sequence(halves)

    def fetch(g, z):
        return pltpu.make_async_copy(w_hbm.at[g, z], w.at[g, z], w_sem.at[g, z])

    enc_copy = pltpu.make_async_copy(enc_hbm, enc, enc_sem)
    for g in range(4):
        for z in range(parts):
            fetch(g, z).start()
        if g == 0:
            enc_copy.start()

    saves = []

    def save(src, dst):
        copy = pltpu.make_async_copy(src, dst, out_sem.at[len(saves)])
        copy.start()
        saves.append(copy)

    n1[0:rows, :] = low(norm_rows(xa_ref[...].astype(F32), gains_ref[0:1, :])[0])
    n1[rows : 2 * rows, :] = low(norm_rows(x_ref[...].astype(F32), gains_ref[0:1, :])[0])
    save(n1, n1_out)

    length = len_ref[0]
    i = lax.broadcasted_iota(jnp.int32, mask.shape, 0)
    c = lax.broadcasted_iota(jnp.int32, mask.shape, 1)
    own = c - rows
    limit = jnp.where(half > 0, length, 0)
    ok = ((own < 0) & (c < limit)) | ((own >= 0) & (own <= i) & (own + half * rows < length))
    mask[...] = jnp.where(ok, 0.0, MASKED)

    def heads(z, q, kv, p, o, l, keys, with_bias):
        outs = []
        for j in range(3):
            h = z * 3 + j
            q_h = q[z, :, DH * j : DH * (j + 1)]
            k_h = kv[z, :, DH * j : DH * (j + 1)]
            v_h = kv[z, :, DH * (3 + j) : DH * (4 + j)]
            s_buf[j, :, 0:keys] = mm_nt(q_h, k_h)
            for r, n in chunks(rows, 32):
                s = s_buf[j, r : r + n, 0:keys]
                if with_bias:
                    line = jnp.broadcast_to(diag_ref[pl.ds(h, 1), :], (n, diag_ref.shape[1]))
                    grid = pltpu.roll(line, r, 1, stride=1, stride_axis=0)
                    s = s + grid[:, 0:keys] + mask[r : r + n, :]
                top = jnp.max(s, axis=1, keepdims=True)
                p[h, r : r + n, :] = low(jnp.exp(s - top))
            wide = jnp.concatenate([v_h, jnp.ones_like(v_h)], axis=1)
            mixed = mm(p[h], wide)
            outs.append(low(mixed[:, 0:DH] / mixed[:, DH : 2 * DH]))
            l[z, :, 32 * j : 32 * (j + 1)] = mixed[:, DH : DH + 32]
        o[z] = jnp.concatenate(outs, axis=1)

    acc[...] = x_ref[...].astype(F32)

    def self_step(z, carry):
        fetch(0, z).wait()
        kv1[z] = low(mm(n1[...], w[0, z, :, 0:384]))
        q1[z] = low(mm(n1[rows : 2 * rows, :], w[0, z, :, 384:576]))
        heads(z, q1, kv1, p1, o1, l1, 2 * rows, True)
        acc[...] += mm_nt(o1[z], w[0, z, :, 576:768])
        return carry

    lax.fori_loop(0, parts, self_step, 0)
    for src, dst in ((q1, q1_out), (kv1, kv1_out), (p1, p1_out), (o1, o1_out), (l1, l1_out)):
        save(src, dst)
    x1[...] = acc[...]
    n2[...] = low(norm_rows(acc[...], gains_ref[1:2, :])[0])
    save(x1, x1_out)
    save(n2, n2_out)
    enc_copy.wait()
    keys = enc.shape[0]

    def cross_step(z, carry):
        fetch(1, z).wait()
        kv2[z] = low(mm(enc[...], w[1, z, :, 0:384]))
        q2[z] = low(mm(n2[...], w[1, z, :, 384:576]))
        heads(z, q2, kv2, p2, o2, l2, keys, False)
        acc[...] += mm_nt(o2[z], w[1, z, :, 576:768])
        return carry

    lax.fori_loop(0, parts, cross_step, 0)
    for src, dst in ((q2, q2_out), (kv2, kv2_out), (p2, p2_out), (o2, o2_out), (l2, l2_out)):
        save(src, dst)
    x2[...] = acc[...]
    n3[...] = low(norm_rows(acc[...], gains_ref[2:3, :])[0])
    save(x2, x2_out)
    save(n3, n3_out)

    def feed_step(z, carry):
        fetch(2, z).wait()
        fetch(3, z).wait()
        for r, n in chunks(rows, 64):
            a = mm(n3[r : r + n, :], w[2, z])
            sq = a * a
            t = jnp.tanh(a * (ROOT + ROOT * CUBE * sq))
            cdf = 0.5 + 0.5 * t
            hid[z, r : r + n, :] = low(a * cdf)
            slope[z, r : r + n, :] = low(
                cdf + 0.5 * a * (1.0 - t * t) * (ROOT + 3.0 * ROOT * CUBE * sq)
            )
        acc[...] += mm_nt(hid[z], w[3, z])
        return carry

    lax.fori_loop(0, parts, feed_step, 0)
    save(hid, hid_out)
    save(slope, slope_out)
    result_ref[...] = low(acc[...])
    for copy in saves:
        copy.wait()


def backward_kernel(
    x_ref,
    xa_ref,
    cot_ref,
    gains_ref,
    onehot_ref,
    enc_hbm,
    w_hbm,
    n1_hbm,
    q1_hbm,
    kv1_hbm,
    p1_hbm,
    o1_hbm,
    l1_hbm,
    x1_hbm,
    n2_hbm,
    q2_hbm,
    kv2_hbm,
    p2_hbm,
    o2_hbm,
    l2_hbm,
    x2_hbm,
    n3_hbm,
    hid_hbm,
    slope_hbm,
    dx_ref,
    dxa_ref,
    denc_ref,
    small_ref,
    table_ref,
    g_hbm,
    w,
    enc,
    n1,
    q1,
    kv1,
    p1,
    o1,
    l1,
    n2,
    q2,
    kv2,
    p2,
    o2,
    l2,
    x2,
    n3,
    hid,
    slope,
    g_buf,
    rows_t,
    rows_t2,
    keys_t,
    dp_buf,
    ds_buf,
    dkv_t,
    dn,
    acc,
    enc_acc,
    diag_acc,
    w_sem,
    in_sem,
    p_sem,
    g_sem,
):
    rows = x_ref.shape[0]
    parts = w.shape[0]

    order = [(3, 2), (1,), (0,)]
    seq = [g for gs in order for g in gs]

    def fetch(slot, g, z):
        return pltpu.make_async_copy(w_hbm.at[g, z], w.at[z, slot], w_sem.at[z, slot])

    loads = {}
    names = [
        (n3_hbm, n3), (hid_hbm, hid), (slope_hbm, slope), (x2_hbm, x2),
        (o2_hbm, o2), (l2_hbm, l2), (q2_hbm, q2), (kv2_hbm, kv2),
        (n2_hbm, n2), (enc_hbm, enc),
        (o1_hbm, o1), (l1_hbm, l1), (q1_hbm, q1), (kv1_hbm, kv1), (n1_hbm, n1),
    ]

    for z in range(parts):
        fetch(0, 3, z).start()
        fetch(1, 2, z).start()
    for k, (src, dst) in enumerate(names):
        loads[id(dst)] = pltpu.make_async_copy(src, dst, in_sem.at[k])
        loads[id(dst)].start()

    def need(*refs):
        for ref in refs:
            loads[id(ref)].wait()

    def fetch_p(src, dst, k, z):
        slot = lax.rem(z, 2)
        return pltpu.make_async_copy(src.at[pl.ds(3 * z, 3)], dst.at[slot], p_sem.at[k, slot])

    def turn_p(src, dst, k, z):
        fetch_p(src, dst, k, z).wait()

        @pl.when(z + 1 < parts)
        def _():
            fetch_p(src, dst, k, z + 1).start()

    fetch_p(p2_hbm, p2, 0, 0).start()
    fetch_p(p1_hbm, p1, 1, 0).start()

    def store(slot, g, z):
        return pltpu.make_async_copy(g_buf.at[slot], g_hbm.at[g, z], g_sem.at[slot])

    e3 = cot_ref[...]
    rows_t[...] = flip(e3)
    need(n3, hid, slope)
    rows_t2[...] = flip(n3[...])
    acc[...] = jnp.zeros_like(acc)

    def feed_step(z, carry):
        fetch(0, 3, z).wait()
        fetch(1, 2, z).wait()
        dh = low(mm(cot_ref[...], w[z, 0]))
        da = low(dh.astype(F32) * slope[z].astype(F32))
        hid_z = hid[z]
        slope[z] = da
        acc[...] += mm_nt(slope[z], w[z, 1])

        @pl.when(z > 0)
        def _():
            store(0, 3, z - 1).wait()
            store(1, 2, z - 1).wait()

        g_buf[0] = low(mm(rows_t[...], hid_z))
        store(0, 3, z).start()
        g_buf[1] = low(mm(rows_t2[...], slope[z]))
        store(1, 2, z).start()
        fetch(0, 1, z).start()
        fetch(1, 0, z).start()
        return carry

    lax.fori_loop(0, parts, feed_step, 0)
    store(0, 3, parts - 1).wait()
    store(1, 2, parts - 1).wait()
    need(x2)
    back, gain3 = norm_back(acc[...], x2[...], gains_ref[2:3, :])
    x1_copy = pltpu.make_async_copy(x1_hbm, x2, in_sem.at[len(names)])
    gx = cot_ref[...].astype(F32) + back
    dn[...] = gx
    x1_copy.start()
    small_ref[2:3, :] = gain3

    def heads_back(z, do, q, kv, p, o, l, keys, with_diag):
        do_all = []
        delta_all = []
        for j in range(3):
            do_h = do[:, DH * j : DH * (j + 1)]
            inv = 1.0 / l[z, :, 32 * j : 32 * j + 1]
            o_h = o[z, :, DH * j : DH * (j + 1)].astype(F32)
            delta_all.append(jnp.sum(do_h * o_h * inv, axis=1, keepdims=True))
            do_all.append(do_h * inv)
        do_z = jnp.concatenate(do_all, axis=1)
        do_t = low(jnp.transpose(do_z))
        q_t = flip(q[z])
        dq = []
        for j in range(3):
            h = z * 3 + j
            p_h = p.at[lax.rem(z, 2), j]
            k_h = kv[z, :, DH * j : DH * (j + 1)]
            v_h = kv[z, :, DH * (3 + j) : DH * (4 + j)]
            dp_buf[j % 2, :, 0:keys] = mm_nt(low(do_all[j]), v_h)
            total = None
            for r, n in chunks(rows, 32):
                ds = low(
                    p_h[r : r + n, :].astype(F32)
                    * (dp_buf[j % 2, r : r + n, 0:keys] - delta_all[j][r : r + n, :])
                )
                ds_buf[j % 2, r : r + n, 0:keys] = ds
                if with_diag:
                    width = diag_acc.shape[2]
                    wide = jnp.concatenate(
                        [ds.astype(F32), jnp.zeros((n, width - keys), F32)], axis=1
                    )
                    for b in range(0, n, 8):
                        turned = pltpu.roll(wide[b : b + 8, :], (width - r - b) % width, 1)
                        total = turned if total is None else total + turned
            if with_diag:
                diag_acc[h] = total
            ds_h = ds_buf[j % 2, :, 0:keys]
            dq.append(low(mm(ds_h, k_h)))
            dkv_t[DH * j : DH * (j + 1), 0:keys] = mm(q_t[DH * j : DH * (j + 1), :], ds_h)
            dkv_t[DH * (3 + j) : DH * (4 + j), 0:keys] = mm(do_t[DH * j : DH * (j + 1), :], p_h[...])
        dkv = low(jnp.transpose(dkv_t[:, 0:keys]))
        return jnp.concatenate(dq, axis=1), dkv

    e2 = low(dn[...])
    rows_t[...] = flip(e2)
    need(o2, l2, q2, kv2, n2, enc)
    rows_t2[...] = flip(n2[...])
    keys_t[...] = flip(enc[...])
    keys = enc.shape[0]
    acc[...] = jnp.zeros_like(acc)
    enc_acc[...] = jnp.zeros_like(enc_acc)

    def cross_step(z, carry):
        fetch(0, 1, z).wait()
        turn_p(p2_hbm, p2, 0, z)
        do = low(mm(low(dn[...]), w[z, 0, :, 576:768])).astype(F32)
        dq, dkv = heads_back(z, do, q2, kv2, p2, o2, l2, keys, False)

        @pl.when(z > 0)
        def _():
            store(0, 1, z - 1).wait()

        g_buf[0, :, 0:384] = low(mm(keys_t[...], dkv))
        g_buf[0, :, 384:768] = jnp.concatenate(
            [low(mm(rows_t2[...], dq)), low(mm(rows_t[...], o2[z]))], axis=1
        )
        store(0, 1, z).start()
        acc[...] += mm_nt(dq, w[z, 0, :, 384:576])
        enc_acc[...] += mm_nt(dkv, w[z, 0, :, 0:384])
        return carry

    lax.fori_loop(0, parts, cross_step, 0)
    store(0, 1, parts - 1).wait()
    denc_ref[...] = low(enc_acc[...])
    x1_copy.wait()
    back, gain2 = norm_back(acc[...], x2[...], gains_ref[1:2, :])
    dn[...] += back
    small_ref[1:2, :] = gain2

    rows_t[...] = flip(low(dn[...]))
    need(o1, l1, q1, kv1, n1)
    rows_t2[...] = flip(n1[rows : 2 * rows, :])
    keys_t[:, 0 : 2 * rows] = flip(n1[...])
    acc[...] = jnp.zeros_like(acc)
    enc_acc[0 : 2 * rows, :] = jnp.zeros((2 * rows, enc_acc.shape[1]), F32)

    def self_step(z, carry):
        fetch(1, 0, z).wait()
        turn_p(p1_hbm, p1, 1, z)
        do = low(mm(low(dn[...]), w[z, 1, :, 576:768])).astype(F32)
        dq, dkv = heads_back(z, do, q1, kv1, p1, o1, l1, 2 * rows, True)

        @pl.when(z > 0)
        def _():
            store(0, 0, z - 1).wait()

        g_buf[0, :, 0:384] = low(mm(keys_t[:, 0 : 2 * rows], dkv))
        g_buf[0, :, 384:768] = jnp.concatenate(
            [low(mm(rows_t2[...], dq)), low(mm(rows_t[...], o1[z]))], axis=1
        )
        store(0, 0, z).start()
        acc[...] += mm_nt(dq, w[z, 1, :, 384:576])
        enc_acc[0 : 2 * rows, :] += mm_nt(dkv, w[z, 1, :, 0:384])
        return carry

    lax.fori_loop(0, parts, self_step, 0)
    store(0, 0, parts - 1).wait()
    gain = gains_ref[0:1, :]
    back, gain1 = norm_back(
        acc[...] + enc_acc[rows : 2 * rows, :], x_ref[...].astype(F32), gain
    )
    dx_ref[...] = dn[...] + back
    back, gain1a = norm_back(enc_acc[0:rows, :], xa_ref[...].astype(F32), gain)
    dxa_ref[...] = low(back)
    small_ref[0:1, :] = gain1 + gain1a
    small_ref[3:8, :] = jnp.zeros((5, small_ref.shape[1]), F32)
    width = diag_acc.shape[2]
    lines = []
    for h in range(diag_acc.shape[0]):
        block = diag_acc[h]
        line = block[0:1, :]
        for b in range(1, 8):
            line = line + pltpu.roll(block[b : b + 1, :], width - b, 1)
        lines.append(line)
    lines.append(jnp.zeros((16 - len(lines), width), F32))
    table_ref[...] = jnp.dot(
        jnp.concatenate(lines, axis=0), onehot_ref[...], precision=lax.Precision.HIGHEST, preferred_element_type=F32
    )


def body(
    inputs, encoded, cotangent, lengths, buckets,
    self_gain, self_query, self_key, self_value, self_output, bias_table,
    cross_gain, cross_query, cross_key, cross_value, cross_output,
    feed_gain, feed_inner, feed_output_weight,
):
    rows, width = inputs.shape
    parts = lax.axis_size("mp")
    n_dp = lax.axis_size("dp")
    halves = parts // lengths.shape[0]
    assert halves == 2 and buckets.shape[0] == 2 * rows and parts == 4
    z = lax.axis_index("mp")
    enc_rows = encoded.shape[0]
    vmem = pl.BlockSpec(memory_space=pltpu.VMEM)
    smem = pl.BlockSpec(memory_space=pltpu.SMEM)
    hbm = pl.BlockSpec(memory_space=pl.ANY)
    sds = jax.ShapeDtypeStruct

    packed = jnp.stack(
        [
            jnp.concatenate([self_key, self_value, self_query, self_output.T], axis=1),
            jnp.concatenate([cross_key, cross_value, cross_query, cross_output.T], axis=1),
            feed_inner,
            feed_output_weight.T,
        ]
    )
    share = width // n_dp
    piece = lax.dynamic_slice_in_dim(packed, lax.axis_index("dp") * share, share, 1)
    gathered = lax.all_gather(piece, ("dp", "mp"), axis=0, tiled=False)
    weights = jnp.transpose(
        gathered.reshape(n_dp, parts, 4, share, width), (2, 1, 0, 3, 4)
    ).reshape(4, parts, width, width)
    table = jnp.transpose(lax.all_gather(bias_table, "mp", axis=1, tiled=True))
    swap = [(s, s ^ 1) for s in range(parts)]
    both = lax.ppermute(encoded, "mp", swap)
    other = lax.ppermute(inputs, "mp", swap)
    half = lax.rem(z, 2)
    enc_all = jnp.where(
        half == 0,
        jnp.concatenate([encoded, both], axis=0),
        jnp.concatenate([both, encoded], axis=0),
    )
    length = lax.dynamic_slice_in_dim(lengths, z // 2, 1)
    gains = jnp.concatenate(
        [jnp.stack([self_gain, cross_gain, feed_gain]), jnp.zeros((5, width), F32)]
    )
    diag = 1024
    line = jnp.concatenate(
        [
            buckets[0 : rows + 1][::-1],
            jnp.full((diag - 2 * rows,), -1, jnp.int32),
            buckets[rows + 1 :][::-1],
        ]
    )
    onehot = (line[:, None] == lax.iota(jnp.int32, 128)[None, :]).astype(F32)
    heads = table.shape[0]
    table_pad = jnp.pad(table, ((0, 16 - heads), (0, 128 - table.shape[1])))
    diag_rows = lax.dot_general(
        table_pad, onehot, (((1,), (1,)), ((), ())), precision=lax.Precision.HIGHEST
    )

    keys = enc_all.shape[0]
    saved = [
        ((2 * rows, width), BF16),
        ((parts, rows, 192), BF16),
        ((parts, 2 * rows, 384), BF16),
        ((heads, rows, 2 * rows), BF16),
        ((parts, rows, 192), BF16),
        ((parts, rows, 128), F32),
        ((rows, width), F32),
        ((rows, width), BF16),
        ((parts, rows, 192), BF16),
        ((parts, keys, 384), BF16),
        ((heads, rows, keys), BF16),
        ((parts, rows, 192), BF16),
        ((parts, rows, 128), F32),
        ((rows, width), F32),
        ((rows, width), BF16),
        ((parts, rows, width), BF16),
        ((parts, rows, width), BF16),
    ]
    n1s, q1s, kv1s, p1s, o1s, l1s, x1s, n2s, q2s, kv2s, p2s, o2s, l2s, x2s, n3s, hids, slopes = [
        pltpu.VMEM(*s) for s in saved
    ]
    result, *kept = pl.pallas_call(
        functools.partial(forward_kernel, halves),
        out_shape=[sds((rows, width), BF16)] + [sds(*s) for s in saved],
        in_specs=[smem, vmem, vmem, hbm, vmem, vmem, hbm],
        out_specs=[vmem] + [hbm] * len(saved),
        scratch_shapes=[
            pltpu.VMEM((4, parts, width, width), BF16),
            pltpu.VMEM((keys, width), BF16),
            pltpu.VMEM((rows, 2 * rows), F32),
            pltpu.VMEM((3, rows, keys), F32),
            n1s, q1s, kv1s, p1s, o1s, x1s, n2s, q2s, kv2s, p2s, o2s, x2s, n3s, hids, slopes,
            l1s, l2s,
            pltpu.VMEM((rows, width), F32),
            pltpu.SemaphoreType.DMA((4, parts)),
            pltpu.SemaphoreType.DMA,
            pltpu.SemaphoreType.DMA((len(saved),)),
        ],
        compiler_params=pltpu.CompilerParams(vmem_limit_bytes=VMEM_BYTES),
        name="forward",
    )(length, inputs, other, enc_all, gains, diag_rows, weights)

    dx, dxa, denc, small, table_grad, grads = pl.pallas_call(
        backward_kernel,
        out_shape=[
            sds((rows, width), F32),
            sds((rows, width), BF16),
            sds((keys, width), BF16),
            sds((8, width), F32),
            sds((16, 128), F32),
            sds((4, parts, width, width), BF16),
        ],
        in_specs=[vmem, vmem, vmem, vmem, vmem] + [hbm] * 19,
        out_specs=[vmem] * 5 + [hbm],
        scratch_shapes=[
            pltpu.VMEM((parts, 2, width, width), BF16),
            pltpu.VMEM((keys, width), BF16),
            n1s, q1s, kv1s, pltpu.VMEM((2, 3, rows, 2 * rows), BF16), o1s, l1s, n2s, q2s, kv2s, pltpu.VMEM((2, 3, rows, keys), BF16), o2s, l2s, x2s, n3s,
            hids, slopes,
            pltpu.VMEM((2, width, width), BF16),
            pltpu.VMEM((width, rows), BF16),
            pltpu.VMEM((width, rows), BF16),
            pltpu.VMEM((width, keys), BF16),
            pltpu.VMEM((2, rows, keys), F32),
            pltpu.VMEM((2, rows, keys), BF16),
            pltpu.VMEM((384, keys), F32),
            pltpu.VMEM((rows, width), F32),
            pltpu.VMEM((rows, width), F32),
            pltpu.VMEM((keys, width), F32),
            pltpu.VMEM((heads, 8, diag), F32),
            pltpu.SemaphoreType.DMA((parts, 2)),
            pltpu.SemaphoreType.DMA((18,)),
            pltpu.SemaphoreType.DMA((2, 2)),
            pltpu.SemaphoreType.DMA((2,)),
        ],
        compiler_params=pltpu.CompilerParams(vmem_limit_bytes=VMEM_BYTES),
        name="backward",
    )(inputs, other, cotangent, gains, onehot, enc_all, weights, *kept)

    input_grad = dx + lax.ppermute(dxa, "mp", swap).astype(F32)
    mine = lax.dynamic_slice_in_dim(denc, half * enc_rows, enc_rows)
    theirs = lax.dynamic_slice_in_dim(denc, (1 - half) * enc_rows, enc_rows)
    encoder_grad = mine.astype(F32) + lax.ppermute(theirs, "mp", swap).astype(F32)
    shares = jnp.transpose(
        grads.reshape(4, parts, n_dp, share, width), (2, 1, 0, 3, 4)
    ).reshape(n_dp * parts, 4 * share, width)
    summed = (
        lax.psum_scatter(shares, ("dp", "mp"), scatter_dimension=0, tiled=True)
        .astype(F32)
        .reshape(4, share, width)
    )
    small, table_grad = lax.psum((small, table_grad), ("dp", "mp"))
    table_mine = lax.dynamic_slice_in_dim(
        jnp.transpose(table_grad[0:heads, 0 : bias_table.shape[0]]), z * 3, 3, 1
    )
    gs, gc = summed[0], summed[1]
    return (
        result,
        low(input_grad),
        low(encoder_grad),
        small[0],
        gs[:, 384:576],
        gs[:, 0:192],
        gs[:, 192:384],
        gs[:, 576:768].T,
        table_mine,
        small[1],
        gc[:, 384:576],
        gc[:, 0:192],
        gc[:, 192:384],
        gc[:, 576:768].T,
        small[2],
        summed[2],
        summed[3].T,
    )


def solution(mesh):
    rows = P(("dp", "mp"), None)
    across, down = P(None, "mp"), P("mp", None)
    return jax.shard_map(
        body,
        mesh=mesh,
        in_specs=(
            rows, rows, rows, P("dp"), P(),
            P(), across, across, across, down, across,
            P(), across, across, across, down,
            P(), across, down,
        ),
        out_specs=(
            rows, rows, rows,
            P(), P("dp", "mp"), P("dp", "mp"), P("dp", "mp"), P("mp", "dp"), P(None, "mp"),
            P(), P("dp", "mp"), P("dp", "mp"), P("dp", "mp"), P("mp", "dp"),
            P(), P("dp", "mp"), P("mp", "dp"),
        ),
        check_vma=False,
    )
```

time: 5780 us -> 513 us (0.09)
  local copies, waits for them, and re-layouts: 4860 us -> 51.6 us
  waiting for transfers between devices: 619 us -> 231 us
  matrix products: 174 us -> 1.09 us
  Pallas kernels: 0 us -> 101 us
    gather x4 -> x0, local copies, waits for them, and re-layouts: 4780 us -> none  [the longest x2 3310 us: body(): bucket_grid = jnp.take(buckets, offsets)]
    reduce_scatter x13 -> x1, waiting for transfers between devices: 357 us -> 149 us  [body(): lax.psum_scatter(shares, ('dp', 'mp'), scatter_dimension=0, tiled=True)]
    all_gather x7 -> x1, waiting for transfers between devices: 260 us -> 82.6 us  [body(): gathered = lax.all_gather(piece, ('dp', 'mp'), axis=0, tiled=False)]
    dot_general x65 -> x1, matrix products: 169 us -> 1.09 us  [body(): lax.dot_general(table_pad, onehot, (((1,), (1,)), ((), ())), precision=la...]
    pallas_call x0 -> x2, Pallas kernels: none -> 101 us  [the longest x1 62 us: body(): pl.pallas_call(backward_kernel, out_shape=[sds((rows, width), F32), sds((...]
  transfers between devices with their start and end apart: 24 -> 6, of which waited for: 11 -> 2; matrix products, arithmetic and copies ran while one was open for 86% -> 5% of each run, Pallas kernels for 0% -> 0%
where the time goes in v1:
time: 513 us; the launch traced here: 512 us
  waiting for transfers between devices  231 us (45%)
  Pallas kernels  101 us (20%)
  blocking collectives  95.9 us (19%)
  local copies, waits for them, and re-layouts  51.6 us (10%)
  between operations  14.4 us (3%)
  other arithmetic  11.2 us (2%)
  starting transfers between devices  5.57 us (1%)
    reduce_scatter x1, waiting for transfers between devices, body(): lax.psum_scatter(shares, ('dp', 'mp'), scatter_dimension=0, tiled=True)  149 us
    all_gather x1, waiting for transfers between devices, body(): gathered = lax.all_gather(piece, ('dp', 'mp'), axis=0, tiled=False)  82.6 us
    pallas_call x1, Pallas kernels, body(): pl.pallas_call(backward_kernel, out_shape=[sds((rows, width), F32), sds((...  62 us
    all_gather x1, blocking collectives, body(): table = jnp.transpose(lax.all_gather(bias_table, 'mp', axis=1, tiled=True))  48.1 us
    psum x1, blocking collectives, body(): small, table_grad = lax.psum((small, table_grad), ('dp', 'mp'))  47.8 us
    pallas_call x1, Pallas kernels, body(): pl.pallas_call(functools.partial(forward_kernel, halves), out_shape=[sds(...  38.6 us
    transpose x1, local copies, waits for them, and re-layouts, body(): jnp.transpose(grads.reshape(4, parts, n_dp, share, width), (2, 1, 0, 3, 4))  17.2 us
    reshape x1, local copies, waits for them, and re-layouts, body(): gathered.reshape(n_dp, parts, 4, share, width)  17.2 us
  transfers between devices with their start and end apart: 6, of which 2 were waited for; matrix products, arithmetic and copies ran while one was open for 5% of the time, Pallas kernels for 0%

profile of v1, /device:TPU:0, one launch (start us, length us, event | category | flops | bytes accessed | tf_op | source)
XLA Modules:
  0.0 511.7 jit_solution(16206628089984604316)
XLA Ops:
  7.3 1.6 copy.54
  10.2 1.1 copy.53
  11.4 1.9 copy.52
  13.3 1.9 copy.51
  15.1 2.7 maximum_bitcast_fusion
  18.9 3.1 collective-permute-start
  22.8 48.1 %all-gather.1 = f32[4,3,32]{2,1,0:T(4,128)S(1)} all-gather(f32[1,3,32]{2,1,0:T(4,128)S(1)} %bitcast.51), channel_id=1, replica_groups=mesh['dp'=8,'mp'=4] {'mp'}, dimensions={0}, use_global_device_ids=true | all-gather | bytes 1920 | tf_op jit(solution)/shard_map/all_gather | solution.py:535
  71.1 1.1 fusion.4.diag_ref
  73.5 1.0 fusion.3.onehot_ref
  74.4 1.8 maximum_select_fusion.enc_hbm
  76.3 82.6 %all-gather.4.cloned.1.call-done = bf16[128,96,768]{2,1,0:T(8,128)(2,1)} async-done(((bf16[4,96,768]{2,1,0:T(8,128)(2,1)}), bf16[128,96,768]{2,1,0:T(8,128)(2,1)}) %all-gather.4.cloned.1.call-update) | async-done | bytes 18874384 | tf_op jit(solution)/shard_map/all_gather | solution.py:531
  158.9 17.2 %copy.55 = bf16[8,4,4,96,768]{4,3,0,1,2:T(8,128)(2,1)} copy(bf16[8,4,4,96,768]{4,3,2,1,0:T(8,128)(2,1)} %bitcast.43) | data formatting | bytes 37748736 | tf_op jit(solution)/shard_map/reshape | solution.py:533
  176.9 38.6 %forward.1 = (bf16[320,768]{1,0:T(8,128)(2,1)}, bf16[640,768]{1,0:T(8,128)(2,1)}, bf16[4,320,192]{2,1,0:T(8,128)(2,1)}, bf16[4,640,384]{2,1,0:T(8,128)(2,1)}, bf...) custom-call(s32[1]{0:T(128)} %dynamic_slice.15.len_ref, ...), custom_call_target="tpu_custom_call" | custom-call | tf_op jit(solution)/shard_map/forward/pallas_call | solution.py:587
  215.5 62.0 %backward.1 = (f32[320,768]{1,0:T(8,128)}, bf16[320,768]{1,0:T(8,128)(2,1)}, bf16[1024,768]{1,0:T(8,128)(2,1)}, f32[8,768]{1,0:T(8,128)}, f32[16,128]{1,0:T(8,128)}, /*index=5*/bf16[4,4,768,768]{3,2,1,0:T(8,128)(2,1)}) custom-call(bf16[320,768]{1,0:T(8,128)(2,1)} %x_ref.3, bf16[320,768]{1,0:T(8,128)(2,1)} %copy-done.1, bf16[320,768]{1,0:T(8,128)(2,1)} %cot_ref.1, ...), custom_call_target="tpu_custom_call" | custom-call | tf_op jit(solution)/shard_map/backward/pallas_call | solution.py:608
  277.5 17.2 %copy.56 = bf16[8,4,4,96,768]{4,3,2,1,0:T(8,128)(2,1)} copy(bf16[8,4,4,96,768]{4,3,0,1,2:T(8,128)(2,1)} %bitcast.44) | data formatting | bytes 37748736 | tf_op jit(solution)/shard_map/transpose | solution.py:649
  294.8 1.3 copy-done.2
  296.1 0.9 constant_dynamic-slice_fusion
  297.2 1.9 collective-permute-start.2
  299.1 47.8 %all-reduce.1 = (f32[8,768]{1,0:T(8,128)S(1)}, f32[16,128]{1,0:T(8,128)S(1)}) all-reduce(f32[8,768]{1,0:T(8,128)S(1)} %copy-done.11, f32[16,128]{1,0:T(8,128)S(1)} %copy-done.13), channel_id=1, replica_groups=mesh['dp'=8,'mp'=4] {'dp','mp'}, use_global_device_ids=true, to_apply=%region_0.1 | all-reduce | flops 8192 | bytes 65536 | tf_op jit(solution)/shard_map/psum | solution.py:657
  348.1 1.9 add_convert_fusion.1
  350.0 1.1 add_convert_fusion
  351.1 148.8 %reduce-scatter.2.cloned.1.call-done = bf16[1,384,768]{2,1,0:T(8,128)(2,1)} async-done(((bf16[32,384,768]{2,1,0:T(8,128)(2,1)}), bf16[1,384,768]{2,1,0:T(8,128)(2,1)}) %reduce-scatter.2.cloned.1.call-update) | async-done | bytes 589840 | tf_op jit(solution)/shard_map/reduce_scatter | solution.py:653
  499.9 1.1 convert_element_type.29
  501.0 0.9 slice_bitcast_fusion
  (76 shorter events, 9.7 us)
Async XLA Ops:
  7.2 1.7 copy-start.6
  7.2 1.9 copy-start.7
  7.2 151.7 %all-gather.4.cloned.1.call-start = ((), (), s32[]{:S(2)}) async-start(), calls=%async_computation.2 | async-start | bytes 19464192 | tf_op jit(solution)/shard_map/all_gather | solution.py:531
  7.3 2.0 copy-start.8
  8.9 1.1 copy-start.10
  15.1 2.7 copy-start.3
  17.8 1.0 copy-start
  17.8 4.1 copy-start.5
  17.9 4.5 copy-start.12
  17.9 4.6 copy-start.14
  17.9 4.6 copy-start.15
  17.9 4.6 copy-start.16
  17.9 4.8 slice-start
  17.9 4.9 copy-start.17
  17.9 55.0 %copy-start.18 = (s32[2]{0:T(128)S(1)}, s32[2]{0:T(128)}, u32[]{:S(2)}) copy-start(s32[2]{0:T(128)} %param.22) | copy-start | bytes 28
  18.8 481.0 %reduce-scatter.2.cloned.1.call-start = ((), (), s32[]{:S(2)}) async-start(), calls=%async_computation.1 | async-start | bytes 19464192 | tf_op jit(solution)/shard_map/reduce_scatter | solution.py:653
  18.9 157.2 %collective-permute-start = (bf16[320,768]{1,0:T(8,128)(2,1)S(1)}, bf16[320,768]{1,0:T(8,128)(2,1)S(1)}, u32[]{:S(2)}, u32[]{:S(2)}) collective-permute-start(bf16[320,768]{1,0:T(8,128)(2,1)S(1)} %copy-done), channel_id=1, source_target_pairs={{0,1},{1,0},{2,3},{3,2},{4,5},{5,4},{6,7},{7,6},{8,9},{9,8},{10,11... | collective-permute-start | bytes 1474568 | tf_op jit(solution)/shard_map/ppermute | solution.py:538
  22.0 52.5 %collective-permute-start.1 = (bf16[512,768]{1,0:T(8,128)(2,1)S(1)}, bf16[512,768]{1,0:T(8,128)(2,1)S(1)}, u32[]{:S(2)}, u32[]{:S(2)}) collective-permute-start(bf16[512,768]{1,0:T(8,128)(2,1)S(1)} %copy-done.5), channel_id=1, source_target_pairs={{0,1},{1,0},{2,3},{3,2},{4,5},{5,4},{6,7},{7,6},{8,9},{9,8},{10,11... | collective-permute-start | bytes 2359304 | tf_op jit(solution)/shard_map/ppermute | solution.py:537
  294.7 1.4 copy-start.2
  294.7 4.3 copy-start.11
  294.8 4.3 copy-start.13
  294.8 53.3 %copy-start.4 = (f32[320,768]{1,0:T(8,128)S(1)}, f32[320,768]{1,0:T(8,128)}, u32[]{:S(2)}) copy-start(f32[320,768]{1,0:T(8,128)} %get-tuple-element.59) | copy-start | bytes 2949124
  297.1 53.0 %collective-permute-start.3 = (bf16[512,768]{1,0:T(8,128)(2,1)}, bf16[512,768]{1,0:T(8,128)(2,1)S(1)}, u32[]{:S(2)}, u32[]{:S(2)}) collective-permute-start(bf16[512,768]{1,0:T(8,128)(2,1)} %constant_dynamic-slice_fusion), channel_id=1, source_target_pairs={{0,1},{1,0},{2,3},{3,2},{4,5},{5,4},{6,7},{7,6},{8,9},{9,8},{10,11... | collective-permute-start | bytes 2359304 | tf_op jit(solution)/shard_map/ppermute | solution.py:648
  297.2 50.9 %collective-permute-start.2 = (bf16[320,768]{1,0:T(8,128)(2,1)}, bf16[320,768]{1,0:T(8,128)(2,1)}, u32[]{:S(2)}, u32[]{:S(2)}) collective-permute-start(bf16[320,768]{1,0:T(8,128)(2,1)} %get-tuple-element.60), channel_id=1, source_target_pairs={{0,1},{1,0},{2,3},{3,2},{4,5},{5,4},{6,7},{7,6},{8,9},{9,8},{10,11... | collective-permute-start | bytes 1474568 | tf_op jit(solution)/shard_map/ppermute | solution.py:645
  (2 other events, 1.7 us)
Sparse Core Ops, SparseCore 0:
  18.9 139.9 all-gather.3
  294.9 204.9 reduce-scatter.1

commit v2 on v1

--- a/solution.py
+++ b/solution.py
@@ -46,12 +46,444 @@
     return back, jnp.sum(grad * unit, axis=0, keepdims=True)
 
 
+def block(w, i, j, start=0, stop=None):
+    part = w[i, j, :, :, :, start:stop]
+    return part.reshape(part.shape[0] * part.shape[1] * part.shape[2], part.shape[3])
+
+
 def half_of_sequence(halves):
     return lax.rem(lax.axis_index("mp"), halves)
 
 
 def chunks(rows, step):
     return [(r, min(step, rows - r)) for r in range(0, rows, step)]
+
+
+MESH_ID = pl.DeviceIdType.MESH
+
+
+def places():
+    d = lax.axis_index("dp")
+    z = lax.axis_index("mp")
+    lo = lax.rem(d, 8)
+    core = lax.rem(lo, 2)
+    x = lax.rem(lax.div(lo, 2), 2)
+    y = lax.div(lo, 4)
+    d_core = d + 1 - 2 * core
+    d_x = d + 2 - 4 * x
+    d_y = d + 4 - 8 * y
+    return d, z, core, x, y, d_core, d_x, d_y
+
+
+def greet(z_parts):
+    d, z, _, _, _, d_core, d_x, d_y = places()
+    barrier = pltpu.get_barrier_semaphore()
+    for who in (d_core, d_x, d_y):
+        pl.semaphore_signal(barrier, inc=1, device_id=(who, z), device_id_type=MESH_ID)
+    for step in range(1, z_parts):
+        pl.semaphore_signal(
+            barrier, inc=1, device_id=(d, lax.rem(z + step, z_parts)), device_id_type=MESH_ID
+        )
+    pl.semaphore_wait(barrier, 2 + z_parts)
+
+
+def remote(src, dst, send, recv, who):
+    return pltpu.make_async_remote_copy(
+        src_ref=src, dst_ref=dst, send_sem=send, recv_sem=recv, device_id=who, device_id_type=MESH_ID
+    )
+
+
+class Gather:
+    def __init__(self, packed, wg, z_send, z_recv, s_send, s_recv):
+        self.packed, self.wg = packed, wg
+        self.z_sems, self.s_sems = (z_send, z_recv), (s_send, s_recv)
+        self.parts = wg.shape[1]
+        self.place = places()
+
+    def z_copy(self, g, step):
+        d, z, core, x, y, *_ = self.place
+        yx = 2 * y + x
+        return remote(
+            self.packed.at[g, yx, core],
+            self.wg.at[g, self.parts - step, yx, core],
+            self.z_sems[0].at[g, step - 1],
+            self.z_sems[1].at[g, step - 1],
+            (d, lax.rem(z + step, self.parts)),
+        )
+
+    def s_copy(self, g, k):
+        d, z, core, x, y, d_core, d_x, d_y = self.place
+        rest = pl.ds(1, self.parts - 1)
+        share = self.wg.shape[4]
+        first, second = pl.ds(0, share // 2), pl.ds(share // 2, share // 2)
+        if k < 2:
+            ref = self.wg.at[g, rest, 2 * y + x, core]
+            who = (d_x, d_y)[k]
+        elif k == 2:
+            ref = self.wg.at[g, rest, 2 * y + 1 - x, core, first]
+            who = d_y
+        elif k == 3:
+            ref = self.wg.at[g, rest, 2 * (1 - y) + x, core, second]
+            who = d_x
+        else:
+            ref = self.wg.at[g, rest, :, core]
+            who = d_core
+        return remote(ref, ref, self.s_sems[0].at[g, k], self.s_sems[1].at[g, k], (who, z))
+
+    def z_start(self, g):
+        for step in range(1, self.parts):
+            self.z_copy(g, step).start()
+
+    def xy_start(self, g):
+        for step in range(1, self.parts):
+            self.z_copy(g, step).wait_recv()
+        self.s_copy(g, 0).start()
+        self.s_copy(g, 1).start()
+
+    def corner_start(self, g):
+        self.s_copy(g, 0).wait_recv()
+        self.s_copy(g, 2).start()
+        self.s_copy(g, 1).wait_recv()
+        self.s_copy(g, 3).start()
+
+    def core_start(self, g):
+        self.s_copy(g, 2).wait_recv()
+        self.s_copy(g, 3).wait_recv()
+        self.s_copy(g, 4).start()
+
+    def arrived(self, g):
+        self.s_copy(g, 4).wait_recv()
+
+    def sent(self):
+        for g in range(4):
+            for step in range(1, self.parts):
+                self.z_copy(g, step).wait_send()
+            for k in range(5):
+                self.s_copy(g, k).wait_send()
+
+
+def gather_kernel(
+    packed, x_in, enc_in, table_in, wg, x_out, enc_out, table_out,
+    z_send, z_recv, s_send, s_recv, e_send, e_recv,
+):
+    parts = wg.shape[1]
+    d, z = places()[:2]
+    mate = z + 1 - 2 * lax.rem(z, 2)
+    greet(parts)
+    gather = Gather(packed, wg, z_send, z_recv, s_send, s_recv)
+    x_copy = remote(x_in, x_out, e_send.at[0], e_recv.at[0], (d, mate))
+    enc_copy = remote(enc_in, enc_out, e_send.at[1], e_recv.at[1], (d, mate))
+    tables = [
+        remote(
+            table_in, table_out.at[parts - step], e_send.at[1 + step], e_recv.at[1 + step],
+            (d, lax.rem(z + step, parts)),
+        )
+        for step in range(1, parts)
+    ]
+    gather.z_start(0)
+    for copy in tables:
+        copy.start()
+    x_copy.start()
+    for t in range(7):
+        if t >= 3:
+            gather.arrived(t - 3)
+        if 2 <= t < 6:
+            gather.core_start(t - 2)
+        if 1 <= t < 5:
+            gather.corner_start(t - 1)
+        if t < 4:
+            gather.xy_start(t)
+        if t < 3:
+            gather.z_start(t + 1)
+        if t == 0:
+            enc_copy.start()
+    for copy in tables + [x_copy, enc_copy]:
+        copy.wait()
+    gather.sent()
+
+
+C_RING = 4
+TICKS = 16
+
+
+class Scatter:
+    def __init__(self, bufs, sems, credit):
+        (
+            self.c_in, self.a_in, self.b_in, self.z_in,
+            self.a_out, self.a_keep, self.b_out, self.b_keep, self.z_out, self.total,
+        ) = bufs
+        self.sems, self.credit = sems, credit
+        self.parts = 4
+        self.share = self.z_out.shape[1]
+        self.place = places()
+
+    def block(self, t):
+        feed = 1 - lax.div(t, 8)
+        r = feed * lax.div(t, 2) + (1 - feed) * lax.rem(t, 4)
+        g = feed * (3 - lax.rem(t, 2)) + (1 - feed) * (3 - lax.div(t, 4))
+        return g, r
+
+    def copy(self, k, t, src, dst, who):
+        return remote(src, dst, self.sems.at[0, k, t], self.sems.at[1, k, t], who)
+
+    def c_copy(self, t, src):
+        z, d_core = self.place[1], self.place[5]
+        return self.copy(0, t, src, self.c_in.at[lax.rem(t, C_RING)], (d_core, z))
+
+    def a_copy(self, t, q):
+        _, z, *_, d_x, d_y = self.place
+        src, dst = self.a_out.at[lax.rem(t, 2), q], self.a_in.at[t, q]
+        return self.copy(1 + q, t, src, dst, ((d_x, d_y)[q], z))
+
+    def b_copy(self, t, q):
+        _, z, *_, d_x, d_y = self.place
+        src, dst = self.b_out.at[lax.rem(t, 2), q], self.b_in.at[t, q]
+        return self.copy(3 + q, t, src, dst, ((d_y, d_x)[q], z))
+
+    def z_copy(self, t):
+        d, z = self.place[:2]
+        who = (d, lax.rem(z + self.block(t)[1], self.parts))
+        return self.copy(5, t, self.z_out.at[lax.rem(t, 2)], self.z_in.at[t], who)
+
+    def rows(self, q):
+        return pl.ds(q * (self.share // 2), self.share // 2)
+
+    def c_start(self, t, src):
+        @pl.when(t >= C_RING)
+        def _():
+            pl.semaphore_wait(self.credit, 1)
+
+        self.c_copy(t, src).start()
+
+    def a_start(self, t, mine, src):
+        _, z, _, x, y, d_core, *_ = self.place
+        slot, ring = lax.rem(t, 2), lax.rem(t, C_RING)
+
+        @pl.when(t >= 2)
+        def _():
+            self.a_copy(t - 2, 0).wait_send()
+            self.a_copy(t - 2, 1).wait_send()
+
+        self.c_copy(t, src).wait_recv()
+        for q in range(2):
+            rows = self.rows(q)
+            for k in range(2):
+                send = (2 * k + 1 - x, 2 * (1 - y) + k)[q]
+                keep = (2 * k + x, 2 * y + k)[q]
+                self.a_out[slot, q, k] = low(
+                    mine[send, rows].astype(F32) + self.c_in[ring, send, rows].astype(F32)
+                )
+                self.a_keep[slot, q, k] = mine[keep, rows].astype(F32) + self.c_in[
+                    ring, keep, rows
+                ].astype(F32)
+            self.a_copy(t, q).start()
+
+        @pl.when(t < TICKS - C_RING)
+        def _():
+            pl.semaphore_signal(
+                self.credit, inc=1, device_id=(d_core, z), device_id_type=MESH_ID
+            )
+
+    def b_start(self, t):
+        _, _, _, x, y, *_ = self.place
+        slot = lax.rem(t, 2)
+
+        @pl.when(t >= 2)
+        def _():
+            self.b_copy(t - 2, 0).wait_send()
+            self.b_copy(t - 2, 1).wait_send()
+
+        for q in range(2):
+            keep = (y, x)[q]
+            send = 1 - keep
+            self.a_copy(t, q).wait_recv()
+            self.b_out[slot, q] = low(
+                self.a_keep[slot, q, send] + self.a_in[t, q, send].astype(F32)
+            )
+            self.b_keep[slot, q] = self.a_keep[slot, q, keep] + self.a_in[t, q, keep].astype(F32)
+            self.b_copy(t, q).start()
+
+    def z_start(self, t):
+        slot = lax.rem(t, 2)
+        g, r = self.block(t)
+
+        @pl.when((t >= 2) & (self.block(t - 2)[1] > 0))
+        def _():
+            self.z_copy(t - 2).wait_send()
+
+        for q in range(2):
+            self.b_copy(t, q).wait_recv()
+            done = self.b_keep[slot, q] + self.b_in[t, q].astype(F32)
+
+            @pl.when(r == 0)
+            def _():
+                self.total[g, self.rows(q)] = done
+
+            @pl.when(r > 0)
+            def _():
+                self.z_out[slot, self.rows(q)] = low(done)
+
+        @pl.when(r > 0)
+        def _():
+            self.z_copy(t).start()
+
+    def step(self, t, mine, src):
+        @pl.when((t >= 1) & (t < TICKS + 1))
+        def _():
+            self.a_start(t - 1, mine, src)
+
+        @pl.when((t >= 2) & (t < TICKS + 2))
+        def _():
+            self.b_start(t - 2)
+
+        @pl.when((t >= 3) & (t < TICKS + 3))
+        def _():
+            self.z_start(t - 3)
+
+    def finish(self):
+        def drain(t, carry):
+            self.a_copy(t, 0).wait_send()
+            self.a_copy(t, 1).wait_send()
+            self.b_copy(t, 0).wait_send()
+            self.b_copy(t, 1).wait_send()
+            self.z_copy(t).wait_send()
+            return carry
+
+        lax.fori_loop(TICKS - 2, TICKS, drain, 0)
+
+        def add(t, carry):
+            g, r = self.block(t)
+
+            @pl.when(r > 0)
+            def _():
+                self.z_copy(t).wait_recv()
+                self.total[g] += self.z_in[t].astype(F32)
+
+            return carry
+
+        lax.fori_loop(0, TICKS, add, 0)
+
+
+class Sum:
+    def __init__(self, out, into, ring, send, recv):
+        self.out, self.into, self.ring = out, into, ring
+        self.send, self.recv = send, recv
+        self.place = places()
+
+    def pair(self, k):
+        z, who = self.place[1], self.place[5 + k]
+        return remote(
+            self.out.at[k], self.into.at[k], self.send.at[k], self.recv.at[k], (who, z)
+        )
+
+    def along(self, step):
+        d, z = self.place[:2]
+        parts = self.ring.shape[0]
+        return remote(
+            self.ring.at[z], self.ring.at[z], self.send.at[2 + step], self.recv.at[2 + step],
+            (d, lax.rem(z + step, parts)),
+        )
+
+    def start(self, value):
+        self.out[0] = value
+        self.pair(0).start()
+
+    def turn(self, k):
+        self.pair(k).wait()
+        value = self.out[k] + self.into[k]
+        if k < 2:
+            self.out[k + 1] = value
+            self.pair(k + 1).start()
+            return
+        self.ring[self.place[1]] = value
+        for step in range(1, self.ring.shape[0]):
+            self.along(step).start()
+
+    def result(self):
+        parts = self.ring.shape[0]
+        z = self.place[1]
+        for step in range(1, parts):
+            self.along(step).wait_send()
+            sender = lax.rem(z + parts - step, parts)
+            remote(
+                self.ring.at[sender], self.ring.at[sender],
+                self.send.at[2 + step], self.recv.at[2 + step], (self.place[0], sender),
+            ).wait_recv()
+        value = self.ring[0]
+        for k in range(1, parts):
+            value = value + self.ring[k]
+        return value
+
+
+def scatter_kernel(
+    g_hbm, small_ref, dx_ref, dxa_ref, denc_ref,
+    total_out, small_out, dx_out, denc_out,
+    g_buf, c_in, a_in, b_in, z_in, a_out, a_keep, b_out, b_keep, z_out,
+    s_out, s_in, s_ring, dxa_in, denc_in,
+    sems, credit, s_send, s_recv, e_send, e_recv, g_sem,
+):
+    parts = s_ring.shape[0]
+    place = places()
+    d, z, core = place[:3]
+    half = lax.rem(z, 2)
+    mate = z + 1 - 2 * half
+    enc_rows = denc_out.shape[0]
+    greet(parts)
+    scatter = Scatter(
+        (c_in, a_in, b_in, z_in, a_out, a_keep, b_out, b_keep, z_out, total_out), sems, credit
+    )
+    sums = Sum(s_out, s_in, s_ring, s_send, s_recv)
+    dxa_copy = remote(dxa_ref, dxa_in, e_send.at[0], e_recv.at[0], (d, mate))
+    denc_copy = remote(
+        denc_ref.at[1 - half], denc_in, e_send.at[1], e_recv.at[1], (d, mate)
+    )
+
+    def load(t):
+        slot = lax.rem(t, 2)
+        return pltpu.make_async_copy(g_hbm.at[t, :, core], g_buf.at[slot], g_sem.at[slot])
+
+    def tick(t, carry):
+        @pl.when(t < TICKS)
+        def _():
+            scatter.c_start(t, g_hbm.at[t, :, 1 - core])
+
+        @pl.when((t >= 1) & (t < TICKS + 1))
+        def _():
+            load(t - 1).wait()
+
+        @pl.when(t < TICKS)
+        def _():
+            load(t).start()
+
+        scatter.step(t, g_buf.at[lax.rem(t + 1, 2)], g_hbm.at[lax.rem(t + 15, 16), :, 1 - core])
+
+        @pl.when(t == 4)
+        def _():
+            denc_copy.start()
+            dxa_copy.start()
+            sums.start(small_ref[...])
+
+        for k in range(3):
+
+            @pl.when(t == 6 + k)
+            def _():
+                sums.turn(k)
+
+        return carry
+
+    lax.fori_loop(0, TICKS + 3, tick, 0)
+    scatter.finish()
+    small_out[...] = sums.result()
+    denc_copy.wait()
+    dxa_copy.wait()
+    denc_out[...] = low(denc_ref[half].astype(F32) + denc_in[...].astype(F32))
+    dx_out[...] = low(dx_ref[...] + dxa_in[...].astype(F32))
+
+    def drain(t, carry):
+        scatter.c_copy(t, g_hbm.at[t, :, 1 - core]).wait_send()
+        return carry
+
+    lax.fori_loop(0, TICKS, drain, 0)
 
 
 def forward_kernel(
@@ -59,9 +491,13 @@
     len_ref,
     x_ref,
     xa_ref,
-    enc_hbm,
+    enc_own,
+    enc_other,
     gains_ref,
-    diag_ref,
+    table_own,
+    table_ref,
+    onehot_ref,
+    packed,
     w_hbm,
     result_ref,
     n1_out,
@@ -83,6 +519,7 @@
     slope_out,
     w,
     enc,
+    diag,
     mask,
     s_buf,
     n1,
@@ -111,15 +548,26 @@
     parts = w.shape[1]
     half = half_of_sequence(halves)
 
-    def fetch(g, z):
-        return pltpu.make_async_copy(w_hbm.at[g, z], w.at[g, z], w_sem.at[g, z])
-
-    enc_copy = pltpu.make_async_copy(enc_hbm, enc, enc_sem)
+    def fetch(g, r, src=w_hbm):
+        src = packed.at[g] if src is packed else src.at[g, r]
+        return pltpu.make_async_copy(src, w.at[g, r], w_sem.at[g, r])
+
+    enc_copies = [
+        pltpu.make_async_copy(enc_own, enc.at[half], enc_sem.at[0]),
+        pltpu.make_async_copy(enc_other, enc.at[1 - half], enc_sem.at[1]),
+    ]
     for g in range(4):
-        for z in range(parts):
-            fetch(g, z).start()
+        fetch(g, 0, packed).start()
+        for r in range(1, parts):
+            fetch(g, r).start()
         if g == 0:
-            enc_copy.start()
+            for copy in enc_copies:
+                copy.start()
+    for r in range(parts):
+        lines = table_own[...] if r == 0 else table_ref[r]
+        diag[r] = jnp.dot(
+            lines, onehot_ref[...], precision=lax.Precision.HIGHEST, preferred_element_type=F32
+        )
 
     saves = []
 
@@ -151,7 +599,7 @@
             for r, n in chunks(rows, 32):
                 s = s_buf[j, r : r + n, 0:keys]
                 if with_bias:
-                    line = jnp.broadcast_to(diag_ref[pl.ds(h, 1), :], (n, diag_ref.shape[1]))
+                    line = jnp.broadcast_to(diag[z, j : j + 1, :], (n, diag.shape[2]))
                     grid = pltpu.roll(line, r, 1, stride=1, stride_axis=0)
                     s = s + grid[:, 0:keys] + mask[r : r + n, :]
                 top = jnp.max(s, axis=1, keepdims=True)
@@ -166,10 +614,10 @@
 
     def self_step(z, carry):
         fetch(0, z).wait()
-        kv1[z] = low(mm(n1[...], w[0, z, :, 0:384]))
-        q1[z] = low(mm(n1[rows : 2 * rows, :], w[0, z, :, 384:576]))
+        kv1[z] = low(mm(n1[...], block(w, 0, z, 0, 384)))
+        q1[z] = low(mm(n1[rows : 2 * rows, :], block(w, 0, z, 384, 576)))
         heads(z, q1, kv1, p1, o1, l1, 2 * rows, True)
-        acc[...] += mm_nt(o1[z], w[0, z, :, 576:768])
+        acc[...] += mm_nt(o1[z], block(w, 0, z, 576, 768))
         return carry
 
     lax.fori_loop(0, parts, self_step, 0)
@@ -179,15 +627,16 @@
     n2[...] = low(norm_rows(acc[...], gains_ref[1:2, :])[0])
     save(x1, x1_out)
     save(n2, n2_out)
-    enc_copy.wait()
-    keys = enc.shape[0]
+    for copy in enc_copies:
+        copy.wait()
+    keys = 2 * enc.shape[1]
 
     def cross_step(z, carry):
         fetch(1, z).wait()
-        kv2[z] = low(mm(enc[...], w[1, z, :, 0:384]))
-        q2[z] = low(mm(n2[...], w[1, z, :, 384:576]))
+        kv2[z] = low(mm(enc[...].reshape(keys, enc.shape[2]), block(w, 1, z, 0, 384)))
+        q2[z] = low(mm(n2[...], block(w, 1, z, 384, 576)))
         heads(z, q2, kv2, p2, o2, l2, keys, False)
-        acc[...] += mm_nt(o2[z], w[1, z, :, 576:768])
+        acc[...] += mm_nt(o2[z], block(w, 1, z, 576, 768))
         return carry
 
     lax.fori_loop(0, parts, cross_step, 0)
@@ -202,7 +651,7 @@
         fetch(2, z).wait()
         fetch(3, z).wait()
         for r, n in chunks(rows, 64):
-            a = mm(n3[r : r + n, :], w[2, z])
+            a = mm(n3[r : r + n, :], block(w, 2, z))
             sq = a * a
             t = jnp.tanh(a * (ROOT + ROOT * CUBE * sq))
             cdf = 0.5 + 0.5 * t
@@ -210,7 +659,7 @@
             slope[z, r : r + n, :] = low(
                 cdf + 0.5 * a * (1.0 - t * t) * (ROOT + 3.0 * ROOT * CUBE * sq)
             )
-        acc[...] += mm_nt(hid[z], w[3, z])
+        acc[...] += mm_nt(hid[z], block(w, 3, z))
         return carry
 
     lax.fori_loop(0, parts, feed_step, 0)
@@ -227,7 +676,9 @@
     cot_ref,
     gains_ref,
     onehot_ref,
-    enc_hbm,
+    enc_own,
+    enc_other,
+    packed,
     w_hbm,
     n1_hbm,
     q1_hbm,
@@ -250,7 +701,6 @@
     dxa_ref,
     denc_ref,
     small_ref,
-    table_ref,
     g_hbm,
     w,
     enc,
@@ -286,29 +736,41 @@
     p_sem,
     g_sem,
 ):
-    rows = x_ref.shape[0]
+    rows, width_all = x_ref.shape
     parts = w.shape[0]
 
     order = [(3, 2), (1,), (0,)]
     seq = [g for gs in order for g in gs]
 
-    def fetch(slot, g, z):
-        return pltpu.make_async_copy(w_hbm.at[g, z], w.at[z, slot], w_sem.at[z, slot])
+    half = lax.rem(lax.axis_index("mp"), 2)
+
+    def fetch(slot, g, z, src=w_hbm):
+        src = packed.at[g] if src is packed else src.at[g, z]
+        return pltpu.make_async_copy(src, w.at[z, slot], w_sem.at[z, slot])
+
+    def refetch(slot, g, z):
+        @pl.when(z == 0)
+        def _():
+            fetch(slot, g, z, packed).start()
+
+        @pl.when(z > 0)
+        def _():
+            fetch(slot, g, z).start()
 
     loads = {}
     names = [
         (n3_hbm, n3), (hid_hbm, hid), (slope_hbm, slope), (x2_hbm, x2),
         (o2_hbm, o2), (l2_hbm, l2), (q2_hbm, q2), (kv2_hbm, kv2),
-        (n2_hbm, n2), (enc_hbm, enc),
+        (n2_hbm, n2), (enc_own, enc.at[half]), (enc_other, enc.at[1 - half]),
         (o1_hbm, o1), (l1_hbm, l1), (q1_hbm, q1), (kv1_hbm, kv1), (n1_hbm, n1),
     ]
 
     for z in range(parts):
-        fetch(0, 3, z).start()
-        fetch(1, 2, z).start()
+        fetch(0, 3, z, packed if z == 0 else w_hbm).start()
+        fetch(1, 2, z, packed if z == 0 else w_hbm).start()
     for k, (src, dst) in enumerate(names):
-        loads[id(dst)] = pltpu.make_async_copy(src, dst, in_sem.at[k])
-        loads[id(dst)].start()
+        loads[id(src)] = pltpu.make_async_copy(src, dst, in_sem.at[k])
+        loads[id(src)].start()
 
     def need(*refs):
         for ref in refs:
@@ -329,46 +791,52 @@
     fetch_p(p1_hbm, p1, 1, 0).start()
 
     def store(slot, g, z):
-        return pltpu.make_async_copy(g_buf.at[slot], g_hbm.at[g, z], g_sem.at[slot])
+        t = 2 * z + (3 - g) if g >= 2 else 12 - 4 * g + z
+        return pltpu.make_async_copy(g_buf.at[slot], g_hbm.at[t], g_sem.at[slot])
+
+    def put(slot, value, start=0):
+        shape = g_buf.shape[1:4] + (value.shape[1],)
+        g_buf[slot, :, :, :, start : start + value.shape[1]] = value.reshape(shape)
 
     e3 = cot_ref[...]
     rows_t[...] = flip(e3)
-    need(n3, hid, slope)
+    need(n3_hbm, hid_hbm, slope_hbm)
     rows_t2[...] = flip(n3[...])
     acc[...] = jnp.zeros_like(acc)
 
     def feed_step(z, carry):
         fetch(0, 3, z).wait()
         fetch(1, 2, z).wait()
-        dh = low(mm(cot_ref[...], w[z, 0]))
+        dh = low(mm(cot_ref[...], block(w, z, 0)))
         da = low(dh.astype(F32) * slope[z].astype(F32))
         hid_z = hid[z]
         slope[z] = da
-        acc[...] += mm_nt(slope[z], w[z, 1])
+        acc[...] += mm_nt(slope[z], block(w, z, 1))
 
         @pl.when(z > 0)
         def _():
             store(0, 3, z - 1).wait()
             store(1, 2, z - 1).wait()
 
-        g_buf[0] = low(mm(rows_t[...], hid_z))
+        put(0, low(mm(rows_t[...], hid_z)))
         store(0, 3, z).start()
-        g_buf[1] = low(mm(rows_t2[...], slope[z]))
+        put(1, low(mm(rows_t2[...], slope[z])))
         store(1, 2, z).start()
-        fetch(0, 1, z).start()
-        fetch(1, 0, z).start()
+        refetch(0, 1, z)
+        refetch(1, 0, z)
         return carry
 
     lax.fori_loop(0, parts, feed_step, 0)
     store(0, 3, parts - 1).wait()
     store(1, 2, parts - 1).wait()
-    need(x2)
+    need(x2_hbm)
     back, gain3 = norm_back(acc[...], x2[...], gains_ref[2:3, :])
     x1_copy = pltpu.make_async_copy(x1_hbm, x2, in_sem.at[len(names)])
     gx = cot_ref[...].astype(F32) + back
     dn[...] = gx
     x1_copy.start()
-    small_ref[2:3, :] = gain3
+    small_ref[...] = jnp.zeros_like(small_ref)
+    small_ref[2:3, 0:width_all] = gain3
 
     def heads_back(z, do, q, kv, p, o, l, keys, with_diag):
         do_all = []
@@ -415,42 +883,46 @@
 
     e2 = low(dn[...])
     rows_t[...] = flip(e2)
-    need(o2, l2, q2, kv2, n2, enc)
+    need(o2_hbm, l2_hbm, q2_hbm, kv2_hbm, n2_hbm, enc_own, enc_other)
     rows_t2[...] = flip(n2[...])
-    keys_t[...] = flip(enc[...])
-    keys = enc.shape[0]
+    keys = 2 * enc.shape[1]
+    keys_t[...] = flip(enc[...].reshape(keys, enc.shape[2]))
     acc[...] = jnp.zeros_like(acc)
     enc_acc[...] = jnp.zeros_like(enc_acc)
 
     def cross_step(z, carry):
         fetch(0, 1, z).wait()
         turn_p(p2_hbm, p2, 0, z)
-        do = low(mm(low(dn[...]), w[z, 0, :, 576:768])).astype(F32)
+        do = low(mm(low(dn[...]), block(w, z, 0, 576, 768))).astype(F32)
         dq, dkv = heads_back(z, do, q2, kv2, p2, o2, l2, keys, False)
 
         @pl.when(z > 0)
         def _():
             store(0, 1, z - 1).wait()
 
-        g_buf[0, :, 0:384] = low(mm(keys_t[...], dkv))
-        g_buf[0, :, 384:768] = jnp.concatenate(
-            [low(mm(rows_t2[...], dq)), low(mm(rows_t[...], o2[z]))], axis=1
+        put(0, low(mm(keys_t[...], dkv)))
+        put(
+            0,
+            jnp.concatenate(
+                [low(mm(rows_t2[...], dq)), low(mm(rows_t[...], o2[z]))], axis=1
+            ),
+            384,
         )
         store(0, 1, z).start()
-        acc[...] += mm_nt(dq, w[z, 0, :, 384:576])
-        enc_acc[...] += mm_nt(dkv, w[z, 0, :, 0:384])
+        acc[...] += mm_nt(dq, block(w, z, 0, 384, 576))
+        enc_acc[...] += mm_nt(dkv, block(w, z, 0, 0, 384))
         return carry
 
     lax.fori_loop(0, parts, cross_step, 0)
     store(0, 1, parts - 1).wait()
-    denc_ref[...] = low(enc_acc[...])
+    denc_ref[...] = low(enc_acc[...]).reshape(denc_ref.shape)
     x1_copy.wait()
     back, gain2 = norm_back(acc[...], x2[...], gains_ref[1:2, :])
     dn[...] += back
-    small_ref[1:2, :] = gain2
+    small_ref[1:2, 0:width_all] = gain2
 
     rows_t[...] = flip(low(dn[...]))
-    need(o1, l1, q1, kv1, n1)
+    need(o1_hbm, l1_hbm, q1_hbm, kv1_hbm, n1_hbm)
     rows_t2[...] = flip(n1[rows : 2 * rows, :])
     keys_t[:, 0 : 2 * rows] = flip(n1[...])
     acc[...] = jnp.zeros_like(acc)
@@ -459,20 +931,24 @@
     def self_step(z, carry):
         fetch(1, 0, z).wait()
         turn_p(p1_hbm, p1, 1, z)
-        do = low(mm(low(dn[...]), w[z, 1, :, 576:768])).astype(F32)
+        do = low(mm(low(dn[...]), block(w, z, 1, 576, 768))).astype(F32)
         dq, dkv = heads_back(z, do, q1, kv1, p1, o1, l1, 2 * rows, True)
 
         @pl.when(z > 0)
         def _():
             store(0, 0, z - 1).wait()
 
-        g_buf[0, :, 0:384] = low(mm(keys_t[:, 0 : 2 * rows], dkv))
-        g_buf[0, :, 384:768] = jnp.concatenate(
-            [low(mm(rows_t2[...], dq)), low(mm(rows_t[...], o1[z]))], axis=1
+        put(0, low(mm(keys_t[:, 0 : 2 * rows], dkv)))
+        put(
+            0,
+            jnp.concatenate(
+                [low(mm(rows_t2[...], dq)), low(mm(rows_t[...], o1[z]))], axis=1
+            ),
+            384,
         )
         store(0, 0, z).start()
-        acc[...] += mm_nt(dq, w[z, 1, :, 384:576])
-        enc_acc[0 : 2 * rows, :] += mm_nt(dkv, w[z, 1, :, 0:384])
+        acc[...] += mm_nt(dq, block(w, z, 1, 384, 576))
+        enc_acc[0 : 2 * rows, :] += mm_nt(dkv, block(w, z, 1, 0, 384))
         return carry
 
     lax.fori_loop(0, parts, self_step, 0)
@@ -484,20 +960,46 @@
     dx_ref[...] = dn[...] + back
     back, gain1a = norm_back(enc_acc[0:rows, :], xa_ref[...].astype(F32), gain)
     dxa_ref[...] = low(back)
-    small_ref[0:1, :] = gain1 + gain1a
-    small_ref[3:8, :] = jnp.zeros((5, small_ref.shape[1]), F32)
+    small_ref[0:1, 0:width_all] = gain1 + gain1a
     width = diag_acc.shape[2]
     lines = []
-    for h in range(diag_acc.shape[0]):
-        block = diag_acc[h]
-        line = block[0:1, :]
-        for b in range(1, 8):
-            line = line + pltpu.roll(block[b : b + 1, :], width - b, 1)
-        lines.append(line)
+    for r in range(parts):
+        for j in range(3):
+            part = diag_acc[3 * r + j]
+            line = part[0:1, :]
+            for k in range(1, 8):
+                line = line + pltpu.roll(part[k : k + 1, :], width - k, 1)
+            lines.append(line)
     lines.append(jnp.zeros((16 - len(lines), width), F32))
-    table_ref[...] = jnp.dot(
-        jnp.concatenate(lines, axis=0), onehot_ref[...], precision=lax.Precision.HIGHEST, preferred_element_type=F32
+    table = lax.dot_general(
+        jnp.concatenate(lines, axis=0),
+        onehot_ref[...],
+        (((1,), (1,)), ((), ())),
+        precision=lax.Precision.HIGHEST,
+        preferred_element_type=F32,
     )
+    me = lax.axis_index("mp")
+    for r in range(parts):
+        at = lax.rem(me + r, parts)
+        for p in range(parts):
+
+            @pl.when(at == p)
+            def _(r=r, p=p):
+                small_ref[3 + p : 4 + p, width_all : width_all + 128] = table[3 * r : 3 * r + 1]
+                small_ref[3 + p : 4 + p, width_all + 128 :] = table[3 * r + 1 : 3 * r + 2]
+                small_ref[3 + p : 4 + p, 0:128] = table[3 * r + 2 : 3 * r + 3]
+
+
+def across_groups(summed, small, n_dp):
+    groups = n_dp // 8
+    d = lax.axis_index("dp")
+    whole = lax.all_gather(summed, "dp", axis=0, tiled=False)
+    share, width = summed.shape[1:]
+    whole = whole.reshape(groups, 8, 4, share, width).sum(0)
+    whole = jnp.transpose(whole, (1, 0, 2, 3)).reshape(4, 8 * share, width)
+    rows = 8 * share // n_dp
+    small = lax.all_gather(small, "dp", axis=0, tiled=False).reshape(groups, 8, *small.shape)[:, 0]
+    return lax.dynamic_slice_in_dim(whole, d * rows, rows, 1), small.sum(0)
 
 
 def body(
@@ -518,6 +1020,7 @@
     hbm = pl.BlockSpec(memory_space=pl.ANY)
     sds = jax.ShapeDtypeStruct
 
+    share = width // 8
     packed = jnp.stack(
         [
             jnp.concatenate([self_key, self_value, self_query, self_output.T], axis=1),
@@ -525,24 +1028,31 @@
             feed_inner,
             feed_output_weight.T,
         ]
-    )
-    share = width // n_dp
-    piece = lax.dynamic_slice_in_dim(packed, lax.axis_index("dp") * share, share, 1)
-    gathered = lax.all_gather(piece, ("dp", "mp"), axis=0, tiled=False)
-    weights = jnp.transpose(
-        gathered.reshape(n_dp, parts, 4, share, width), (2, 1, 0, 3, 4)
-    ).reshape(4, parts, width, width)
-    table = jnp.transpose(lax.all_gather(bias_table, "mp", axis=1, tiled=True))
-    swap = [(s, s ^ 1) for s in range(parts)]
-    both = lax.ppermute(encoded, "mp", swap)
-    other = lax.ppermute(inputs, "mp", swap)
+    ).reshape(4, 4, 2, share, width)
+    table_own = jnp.pad(bias_table.T, ((0, 8 - bias_table.shape[1]), (0, 128 - bias_table.shape[0])))
+    weights, other, enc_other, table_all = pl.pallas_call(
+        gather_kernel,
+        out_shape=[
+            sds((4, parts, 4, 2, share, width), BF16),
+            sds((rows, width), BF16),
+            sds((enc_rows, width), BF16),
+            sds((parts, 8, 128), F32),
+        ],
+        in_specs=[hbm] * 4,
+        out_specs=[hbm] * 4,
+        scratch_shapes=[
+            pltpu.SemaphoreType.DMA((4, parts - 1)),
+            pltpu.SemaphoreType.DMA((4, parts - 1)),
+            pltpu.SemaphoreType.DMA((4, 5)),
+            pltpu.SemaphoreType.DMA((4, 5)),
+            pltpu.SemaphoreType.DMA((5,)),
+            pltpu.SemaphoreType.DMA((5,)),
+        ],
+        compiler_params=pltpu.CompilerParams(collective_id=1, has_side_effects=True),
+        name="gather",
+    )(packed, inputs, encoded, table_own)
     half = lax.rem(z, 2)
-    enc_all = jnp.where(
-        half == 0,
-        jnp.concatenate([encoded, both], axis=0),
-        jnp.concatenate([both, encoded], axis=0),
-    )
-    length = lax.dynamic_slice_in_dim(lengths, z // 2, 1)
+    length = lax.dynamic_slice_in_dim(lengths, lax.div(z, 2), 1)
     gains = jnp.concatenate(
         [jnp.stack([self_gain, cross_gain, feed_gain]), jnp.zeros((5, width), F32)]
     )
@@ -554,14 +1064,9 @@
             buckets[rows + 1 :][::-1],
         ]
     )
-    onehot = (line[:, None] == lax.iota(jnp.int32, 128)[None, :]).astype(F32)
-    heads = table.shape[0]
-    table_pad = jnp.pad(table, ((0, 16 - heads), (0, 128 - table.shape[1])))
-    diag_rows = lax.dot_general(
-        table_pad, onehot, (((1,), (1,)), ((), ())), precision=lax.Precision.HIGHEST
-    )
-
-    keys = enc_all.shape[0]
+    onehot = (line[None, :] == lax.iota(jnp.int32, 128)[:, None]).astype(F32)
+    heads = 3 * parts
+    keys = 2 * enc_rows
     saved = [
         ((2 * rows, width), BF16),
         ((parts, rows, 192), BF16),
@@ -587,42 +1092,44 @@
     result, *kept = pl.pallas_call(
         functools.partial(forward_kernel, halves),
         out_shape=[sds((rows, width), BF16)] + [sds(*s) for s in saved],
-        in_specs=[smem, vmem, vmem, hbm, vmem, vmem, hbm],
+        in_specs=[smem, vmem, vmem, hbm, hbm, vmem, vmem, vmem, vmem, hbm, hbm],
         out_specs=[vmem] + [hbm] * len(saved),
         scratch_shapes=[
-            pltpu.VMEM((4, parts, width, width), BF16),
-            pltpu.VMEM((keys, width), BF16),
+            pltpu.VMEM((4, parts, 4, 2, share, width), BF16),
+            pltpu.VMEM((2, enc_rows, width), BF16),
+            pltpu.VMEM((parts, 8, diag), F32),
             pltpu.VMEM((rows, 2 * rows), F32),
             pltpu.VMEM((3, rows, keys), F32),
             n1s, q1s, kv1s, p1s, o1s, x1s, n2s, q2s, kv2s, p2s, o2s, x2s, n3s, hids, slopes,
             l1s, l2s,
             pltpu.VMEM((rows, width), F32),
             pltpu.SemaphoreType.DMA((4, parts)),
-            pltpu.SemaphoreType.DMA,
+            pltpu.SemaphoreType.DMA((2,)),
             pltpu.SemaphoreType.DMA((len(saved),)),
         ],
         compiler_params=pltpu.CompilerParams(vmem_limit_bytes=VMEM_BYTES),
         name="forward",
-    )(length, inputs, other, enc_all, gains, diag_rows, weights)
-
-    dx, dxa, denc, small, table_grad, grads = pl.pallas_call(
+    )(
+        length, inputs, other, encoded, enc_other, gains, table_own, table_all, onehot, packed, weights
+    )
+
+    dx, dxa, denc, small, grads = pl.pallas_call(
         backward_kernel,
         out_shape=[
             sds((rows, width), F32),
             sds((rows, width), BF16),
-            sds((keys, width), BF16),
-            sds((8, width), F32),
-            sds((16, 128), F32),
-            sds((4, parts, width, width), BF16),
+            sds((2, enc_rows, width), BF16),
+            sds((8, diag), F32),
+            sds((TICKS, 4, 2, share, width), BF16),
         ],
-        in_specs=[vmem, vmem, vmem, vmem, vmem] + [hbm] * 19,
-        out_specs=[vmem] * 5 + [hbm],
+        in_specs=[vmem, vmem, vmem, vmem, vmem] + [hbm] * 21,
+        out_specs=[vmem] * 4 + [hbm],
         scratch_shapes=[
-            pltpu.VMEM((parts, 2, width, width), BF16),
-            pltpu.VMEM((keys, width), BF16),
+            pltpu.VMEM((parts, 2, 4, 2, share, width), BF16),
+            pltpu.VMEM((2, enc_rows, width), BF16),
             n1s, q1s, kv1s, pltpu.VMEM((2, 3, rows, 2 * rows), BF16), o1s, l1s, n2s, q2s, kv2s, pltpu.VMEM((2, 3, rows, keys), BF16), o2s, l2s, x2s, n3s,
             hids, slopes,
-            pltpu.VMEM((2, width, width), BF16),
+            pltpu.VMEM((2, 4, 2, share, width), BF16),
             pltpu.VMEM((width, rows), BF16),
             pltpu.VMEM((width, rows), BF16),
             pltpu.VMEM((width, keys), BF16),
@@ -634,47 +1141,78 @@
             pltpu.VMEM((keys, width), F32),
             pltpu.VMEM((heads, 8, diag), F32),
             pltpu.SemaphoreType.DMA((parts, 2)),
-            pltpu.SemaphoreType.DMA((18,)),
+            pltpu.SemaphoreType.DMA((20,)),
             pltpu.SemaphoreType.DMA((2, 2)),
             pltpu.SemaphoreType.DMA((2,)),
         ],
         compiler_params=pltpu.CompilerParams(vmem_limit_bytes=VMEM_BYTES),
         name="backward",
-    )(inputs, other, cotangent, gains, onehot, enc_all, weights, *kept)
-
-    input_grad = dx + lax.ppermute(dxa, "mp", swap).astype(F32)
-    mine = lax.dynamic_slice_in_dim(denc, half * enc_rows, enc_rows)
-    theirs = lax.dynamic_slice_in_dim(denc, (1 - half) * enc_rows, enc_rows)
-    encoder_grad = mine.astype(F32) + lax.ppermute(theirs, "mp", swap).astype(F32)
-    shares = jnp.transpose(
-        grads.reshape(4, parts, n_dp, share, width), (2, 1, 0, 3, 4)
-    ).reshape(n_dp * parts, 4 * share, width)
-    summed = (
-        lax.psum_scatter(shares, ("dp", "mp"), scatter_dimension=0, tiled=True)
-        .astype(F32)
-        .reshape(4, share, width)
-    )
-    small, table_grad = lax.psum((small, table_grad), ("dp", "mp"))
-    table_mine = lax.dynamic_slice_in_dim(
-        jnp.transpose(table_grad[0:heads, 0 : bias_table.shape[0]]), z * 3, 3, 1
+    )(inputs, other, cotangent, gains, onehot, encoded, enc_other, packed, weights, *kept)
+
+    summed, small, input_grad, encoder_grad = pl.pallas_call(
+        scatter_kernel,
+        out_shape=[
+            sds((4, share, width), F32),
+            sds((8, diag), F32),
+            sds((rows, width), BF16),
+            sds((enc_rows, width), BF16),
+        ],
+        in_specs=[hbm, vmem, vmem, vmem, vmem],
+        out_specs=[vmem] * 4,
+        scratch_shapes=[
+            pltpu.VMEM((2, 4, share, width), BF16),
+            pltpu.VMEM((C_RING, 4, share, width), BF16),
+            pltpu.VMEM((TICKS, 2, 2, share // 2, width), BF16),
+            pltpu.VMEM((TICKS, 2, share // 2, width), BF16),
+            pltpu.VMEM((TICKS, share, width), BF16),
+            pltpu.VMEM((2, 2, 2, share // 2, width), BF16),
+            pltpu.VMEM((2, 2, 2, share // 2, width), F32),
+            pltpu.VMEM((2, 2, share // 2, width), BF16),
+            pltpu.VMEM((2, 2, share // 2, width), F32),
+            pltpu.VMEM((2, share, width), BF16),
+            pltpu.VMEM((3, 8, diag), F32),
+            pltpu.VMEM((3, 8, diag), F32),
+            pltpu.VMEM((parts, 8, diag), F32),
+            pltpu.VMEM((rows, width), BF16),
+            pltpu.VMEM((enc_rows, width), BF16),
+            pltpu.SemaphoreType.DMA((2, 6, TICKS)),
+            pltpu.SemaphoreType.REGULAR,
+            pltpu.SemaphoreType.DMA((6,)),
+            pltpu.SemaphoreType.DMA((6,)),
+            pltpu.SemaphoreType.DMA((2,)),
+            pltpu.SemaphoreType.DMA((2,)),
+            pltpu.SemaphoreType.DMA((2,)),
+        ],
+        compiler_params=pltpu.CompilerParams(
+            collective_id=2, has_side_effects=True, vmem_limit_bytes=VMEM_BYTES
+        ),
+        name="scatter",
+    )(grads, small, dx, dxa, denc)
+    if n_dp > 8:
+        summed, small = across_groups(summed, small, n_dp)
+    buckets_here = bias_table.shape[0]
+    mine = lax.dynamic_slice_in_dim(small, 3 + z, 1, 0)[0]
+    table_mine = jnp.stack(
+        [mine[width : width + buckets_here], mine[width + 128 :][:buckets_here], mine[:buckets_here]],
+        axis=1,
     )
     gs, gc = summed[0], summed[1]
     return (
         result,
         low(input_grad),
         low(encoder_grad),
-        small[0],
+        small[0, :width],
         gs[:, 384:576],
         gs[:, 0:192],
         gs[:, 192:384],
         gs[:, 576:768].T,
         table_mine,
-        small[1],
+        small[1, :width],
         gc[:, 384:576],
         gc[:, 0:192],
         gc[:, 192:384],
         gc[:, 576:768].T,
-        small[2],
+        small[2, :width],
         summed[2],
         summed[3].T,
     )

time: 513 us -> 341 us (0.66)
  waiting for transfers between devices: 231 us -> 0 us
  Pallas kernels: 101 us -> 317 us
  blocking collectives: 95.9 us -> 0 us
  local copies, waits for them, and re-layouts: 51.6 us -> 14.7 us
  between operations: 14.4 us -> 0.89 us
  starting transfers between devices: 5.57 us -> 0 us
    pallas_call x0 -> x2, Pallas kernels: none -> 215 us  [the longest x1 114 us: body(): pl.pallas_call(scatter_kernel, out_shape=[sds((4, share, width), F32), sd...]
    reduce_scatter x1 -> x0, waiting for transfers between devices: 149 us -> none  [body(): lax.psum_scatter(shares, ('dp', 'mp'), scatter_dimension=0, tiled=True)]
    all_gather x1 -> x0, waiting for transfers between devices: 82.6 us -> none  [body(): gathered = lax.all_gather(piece, ('dp', 'mp'), axis=0, tiled=False)]
    all_gather x1 -> x0, blocking collectives: 48.1 us -> none  [body(): table = jnp.transpose(lax.all_gather(bias_table, 'mp', axis=1, tiled=True))]
    psum x1 -> x0, blocking collectives: 47.8 us -> none  [body(): small, table_grad = lax.psum((small, table_grad), ('dp', 'mp'))]
    reshape x1 -> x0, local copies, waits for them, and re-layouts: 17.2 us -> none  [body(): gathered.reshape(n_dp, parts, 4, share, width)]
    transpose x3 -> x1, local copies, waits for them, and re-layouts: 18 us -> 1.56 us  [body(): packed = jnp.stack([jnp.concatenate([self_key, self_value, self_query, se...]
    unnamed x53 -> x30, local copies, waits for them, and re-layouts: 11.8 us -> 3.52 us
  transfers between devices with their start and end apart: 6 -> 0, of which waited for: 2 -> 0; matrix products, arithmetic and copies ran while one was open for 5% -> 0% of each run, Pallas kernels for 0% -> 0%
where the time goes in v2:
time: 341 us
  Pallas kernels  317 us (93%)
  local copies, waits for them, and re-layouts  14.7 us (4%)
  other arithmetic  8.24 us (2%)
    pallas_call x1, Pallas kernels, body(): pl.pallas_call(scatter_kernel, out_shape=[sds((4, share, width), F32), sd...  114 us
    pallas_call x1, Pallas kernels, body(): pl.pallas_call(gather_kernel, out_shape=[sds((4, parts, 4, 2, share, widt...  101 us
    pallas_call x1, Pallas kernels, body(): pl.pallas_call(backward_kernel, out_shape=[sds((rows, width), F32), sds((...  63.4 us
    pallas_call x1, Pallas kernels, body(): pl.pallas_call(functools.partial(forward_kernel, halves), out_shape=[sds(...  38.9 us

profile of v2, /device:TPU:0, one launch (start us, length us, event | category | flops | bytes accessed | tf_op | source)
XLA Modules:
  0.0 340.9 jit_solution(4971833627156610152)
XLA Ops:
  0.7 1.3 dynamic_slice.6.len_ref
  2.0 1.6 copy.38
  3.7 0.6 copy.37
  4.4 2.3 pad_maximum_fusion.1
  6.7 1.6 copy.36
  8.3 3.6 %pad_maximum_fusion.packed = bf16[4,4,2,96,768]{4,3,2,1,0:T(8,128)(2,1)} fusion(bf16[1,4,2,96,768]{4,3,2,1,0:T(8,128)(2,1)S(1)} %bitcast.30, bf16[1,4,2,96,768]{4,3,2,1,0:T(8,128)(2,1)} %bitcast.33, bf16[1,4,2,96,768]{4,3,2,1,0:T(8,128)(2,1)S(1)} %bitcast.31, bf16[1,4,2,96,768]{4,3,2,1,0:T(8,128)(2,1)S(1)} %bitcast.32), kind=kLoop, calls=%fused_computation | loop fusion | flops 7077888 | bytes 9437184 | tf_op jit(solution)/shard_map/stack | solution.py:1024
  11.9 0.6 pad.4.table_in.table_own
  12.5 100.5 %gather.1 = (bf16[4,4,4,2,96,768]{5,4,3,2,1,0:T(8,128)(2,1)}, bf16[320,768]{1,0:T(8,128)(2,1)}, bf16[512,768]{1,0:T(8,128)(2,1)}, f32[4,8,128]{2,1,0:T(8,128)}) custom-call(bf16[4,4,2,96,768]{4,3,2,1,0:T(8,128)(2,1)} %pad_maximum_fusion.packed, bf16[320,768]{1,0:T(8,128)(2,1)} %x_ref.3, bf16[512,768]{1,0:T(8,128)(2,1)} %enc_own.3, ...), custom_call_target="tpu_custom_call" | custom-call | tf_op jit(solution)/shard_map/gather/pallas_call | solution.py:1033
  113.2 0.7 maximum_maximum_fusion.gains_ref
  114.0 0.1 reverse
  114.2 0.1 reverse.1
  114.4 0.9 fusion.onehot_ref
  115.3 38.9 %forward.1 = (bf16[320,768]{1,0:T(8,128)(2,1)}, bf16[640,768]{1,0:T(8,128)(2,1)}, bf16[4,320,192]{2,1,0:T(8,128)(2,1)}, bf16[4,640,384]{2,1,0:T(8,128)(2,1)}, bf...) custom-call(s32[1]{0:T(128)} %dynamic_slice.6.len_ref, ...), custom_call_target="tpu_custom_call" | custom-call | tf_op jit(solution)/shard_map/forward/pallas_call | solution.py:1092
  154.2 63.4 %backward.1 = (f32[320,768]{1,0:T(8,128)}, bf16[320,768]{1,0:T(8,128)(2,1)}, bf16[2,512,768]{2,1,0:T(8,128)(2,1)}, f32[8,1024]{1,0:T(8,128)}, bf16[16,4,2,96,768]{4,3,2,1,0:T(8,128)(2,1)}) custom-call(bf16[320,768]{1,0:T(8,128)(2,1)} %x_ref.3, bf16[320,768]{1,0:T(8,128)(2,1)} %get-tuple-element.48.xa_ref, bf16[320,768]{1,0:T(8,128)(2,1)} %cot_ref.1, ...), custom_call_target="tpu_custom_call" | custom-call | tf_op jit(solution)/shard_map/backward/pallas_call | solution.py:1116
  217.6 114.2 %scatter.1 = (f32[4,96,768]{2,1,0:T(8,128)}, f32[8,1024]{1,0:T(8,128)}, bf16[320,768]{1,0:T(8,128)(2,1)}, bf16[512,768]{1,0:T(8,128)(2,1)}) custom-call(bf16[16,4,2,96,768]{4,3,2,1,0:T(8,128)(2,1)} %get-tuple-element.70.g_hbm, f32[8,1024]{1,0:T(8,128)} %get-tuple-element.71.small_ref, f32[320,768]{1,0:T(8,128)} %get-tuple-element.72.dx_ref, ...), custom_call_target="tpu_custom_call" | custom-call | tf_op jit(solution)/shard_map/scatter/pallas_call | solution.py:1152
  331.9 1.5 slice_reduce_fusion
  333.4 2.2 slice_bitcast_fusion
  335.6 0.9 slice_bitcast_fusion.4
  336.4 0.7 copy.39
  337.2 0.8 dynamic-slice_bitcast_fusion.2
  337.9 0.6 pad_maximum_fusion.3
  338.5 0.7 copy.40
  339.3 0.8 copy.43
  340.0 0.9 copy.44
  (35 shorter events, 0.5 us)
Async XLA Ops:
  0.7 3.0 copy-start.2
  0.7 3.0 copy-start.3
  0.7 3.0 copy-start.4
  0.7 3.0 copy-start.5
  8.3 3.6 %copy-start.10 = (f32[32,3]{0,1:T(4,128)S(1)}, f32[32,3]{0,1:T(4,128)}, u32[]{:S(2)}) copy-start(f32[32,3]{0,1:T(4,128)} %param.29) | copy-start | bytes 1156
  12.5 100.6 %copy-start.7 = (f32[768]{0:T(1024)S(1)}, f32[768]{0:T(1024)}, u32[]{:S(2)}) copy-start(f32[768]{0:T(1024)} %param.35) | copy-start | bytes 9220
  12.5 100.6 %copy-start.8 = (f32[768]{0:T(1024)S(1)}, f32[768]{0:T(1024)}, u32[]{:S(2)}) copy-start(f32[768]{0:T(1024)} %param.30) | copy-start | bytes 9220
  12.5 100.6 %copy-start.9 = (f32[768]{0:T(1024)S(1)}, f32[768]{0:T(1024)}, u32[]{:S(2)}) copy-start(f32[768]{0:T(1024)} %param.24) | copy-start | bytes 9220
  12.5 101.4 %copy-start.6 = (s32[640]{0:T(1024)S(1)}, s32[640]{0:T(1024)}, u32[]{:S(2)}) copy-start(s32[640]{0:T(1024)} %param.23) | copy-start | bytes 7684
  12.5 101.6 %slice-start = ((s32[640]{0:T(1024)}), s32[321]{0:T(512)S(1)}, s32[]{:S(2)}) async-start(s32[640]{0:T(1024)} %param.23), calls=%async_computation | async-start | bytes 4096 | tf_op jit(solution)/shard_map/slice | solution.py:1062
  331.9 7.4 %copy-start.1 = (bf16[320,768]{1,0:T(8,128)(2,1)S(1)}, bf16[320,768]{1,0:T(8,128)(2,1)}, u32[]{:S(2)}) copy-start(bf16[320,768]{1,0:T(8,128)(2,1)} %get-tuple-element.136) | copy-start | bytes 1474564
  333.4 6.7 %copy-start = (bf16[512,768]{1,0:T(8,128)(2,1)S(1)}, bf16[512,768]{1,0:T(8,128)(2,1)}, u32[]{:S(2)}) copy-start(bf16[512,768]{1,0:T(8,128)(2,1)} %get-tuple-element.137) | copy-start | bytes 2359300

commit v3 on v2

v3 whole, which is shorter than its diff:
```python
import functools

import jax
import jax.numpy as jnp
from jax import lax
from jax.experimental import pallas as pl
from jax.experimental.pallas import tpu as pltpu
from jax.sharding import PartitionSpec as P

EPS = 1e-06
MASKED = -1e30
DH = 64
F32 = jnp.float32
BF16 = jnp.bfloat16
VMEM_BYTES = 62 << 20
ROOT = 0.7978845608028654
CUBE = 0.044715


def mm(a, b):
    return jnp.dot(a, b, preferred_element_type=F32)


def mm_nt(a, b):
    return lax.dot_general(a, b, (((1,), (1,)), ((), ())), preferred_element_type=F32)


def low(v):
    return v.astype(BF16)


def flip(v):
    return jnp.transpose(v.astype(F32)).astype(BF16)


def norm_rows(v, gain):
    root = lax.rsqrt(jnp.mean(v * v, axis=-1, keepdims=True) + EPS)
    unit = v * root
    return unit * gain, unit, root


def norm_back(grad, v, gain):
    _, unit, root = norm_rows(v, gain)
    scaled = grad * gain
    back = root * (scaled - unit * jnp.mean(scaled * unit, axis=-1, keepdims=True))
    return back, jnp.sum(grad * unit, axis=0, keepdims=True)


def block(w, i, j, start=0, stop=None):
    part = w[i, j, :, :, :, start:stop]
    return part.reshape(part.shape[0] * part.shape[1] * part.shape[2], part.shape[3])


def half_of_sequence(halves):
    return lax.rem(lax.axis_index("mp"), halves)


def chunks(rows, step):
    return [(r, min(step, rows - r)) for r in range(0, rows, step)]


MESH_ID = pl.DeviceIdType.MESH


def places():
    d = lax.axis_index("dp")
    z = lax.axis_index("mp")
    lo = lax.rem(d, 8)
    core = lax.rem(lo, 2)
    x = lax.rem(lax.div(lo, 2), 2)
    y = lax.div(lo, 4)
    d_core = d + 1 - 2 * core
    d_x = d + 2 - 4 * x
    d_y = d + 4 - 8 * y
    return d, z, core, x, y, d_core, d_x, d_y


def greet(z_parts):
    d, z, _, _, _, d_core, d_x, d_y = places()
    barrier = pltpu.get_barrier_semaphore()
    for who in (d_core, d_x, d_y):
        pl.semaphore_signal(barrier, inc=1, device_id=(who, z), device_id_type=MESH_ID)
    for step in range(1, z_parts):
        pl.semaphore_signal(
            barrier, inc=1, device_id=(d, lax.rem(z + step, z_parts)), device_id_type=MESH_ID
        )
    pl.semaphore_wait(barrier, 2 + z_parts)


def remote(src, dst, send, recv, who):
    return pltpu.make_async_remote_copy(
        src_ref=src, dst_ref=dst, send_sem=send, recv_sem=recv, device_id=who, device_id_type=MESH_ID
    )


class Gather:
    chunks = 8

    def __init__(self, packed, wg, z_send, z_recv, s_send, s_recv):
        self.packed, self.wg = packed, wg
        self.z_sems, self.s_sems = (z_send, z_recv), (s_send, s_recv)
        self.parts = wg.shape[1]
        self.place = places()

    def rows(self, k):
        half = self.wg.shape[4] // 2
        return k // 2, pl.ds((k % 2) * half, half)

    def z_copy(self, k, step):
        d, z, core, x, y, *_ = self.place
        yx = 2 * y + x
        g, rows = self.rows(k)
        return remote(
            self.packed.at[g, yx, core, rows],
            self.wg.at[g, self.parts - step, yx, core, rows],
            self.z_sems[0].at[k, step - 1],
            self.z_sems[1].at[k, step - 1],
            (d, lax.rem(z + step, self.parts)),
        )

    def s_copy(self, k, n):
        d, z, core, x, y, d_core, d_x, d_y = self.place
        rest = pl.ds(1, self.parts - 1)
        g, rows = self.rows(k)
        width = self.wg.shape[5]
        if n < 2:
            ref = self.wg.at[g, rest, 2 * y + x, core, rows]
            who = (d_x, d_y)[n]
        elif n == 2:
            ref = self.wg.at[g, rest, 2 * y + 1 - x, core, rows, pl.ds(0, width // 2)]
            who = d_y
        elif n == 3:
            ref = self.wg.at[g, rest, 2 * (1 - y) + x, core, rows, pl.ds(width // 2, width // 2)]
            who = d_x
        else:
            ref = self.wg.at[g, rest, :, core, rows]
            who = d_core
        return remote(ref, ref, self.s_sems[0].at[k, n], self.s_sems[1].at[k, n], (who, z))

    def z_start(self, k):
        for step in range(1, self.parts):
            self.z_copy(k, step).start()

    def tick(self, k):
        if 0 <= k - 2 < self.chunks:
            self.s_copy(k - 2, 2).wait_recv()
            self.s_copy(k - 2, 3).wait_recv()
            self.s_copy(k - 2, 4).start()
        if 0 <= k - 1 < self.chunks:
            self.s_copy(k - 1, 0).wait_recv()
            self.s_copy(k - 1, 2).start()
            self.s_copy(k - 1, 1).wait_recv()
            self.s_copy(k - 1, 3).start()
        if k < self.chunks:
            for step in range(1, self.parts):
                self.z_copy(k, step).wait_recv()
            self.s_copy(k, 0).start()
            self.s_copy(k, 1).start()
        if k + 2 < self.chunks:
            self.z_start(k + 2)

    def arrived(self, g):
        self.s_copy(2 * g, 4).wait_recv()
        self.s_copy(2 * g + 1, 4).wait_recv()

    def sent(self):
        for k in range(self.chunks):
            for step in range(1, self.parts):
                self.z_copy(k, step).wait_send()
            for n in range(5):
                self.s_copy(k, n).wait_send()


C_RING = 4
TICKS = 16


class Scatter:
    def __init__(self, bufs, sems, credit):
        (
            self.c_in, self.a_in, self.b_in, self.z_in,
            self.a_out, self.a_keep, self.b_out, self.b_keep, self.z_out, self.total,
        ) = bufs
        self.sems, self.credit = sems, credit
        self.parts = 4
        self.share = self.z_out.shape[1]
        self.place = places()

    def block(self, t):
        feed = 1 - lax.div(t, 8)
        r = feed * lax.div(t, 2) + (1 - feed) * lax.rem(t, 4)
        g = feed * (3 - lax.rem(t, 2)) + (1 - feed) * (3 - lax.div(t, 4))
        return g, r

    def copy(self, k, t, src, dst, who):
        return remote(src, dst, self.sems.at[0, k, t], self.sems.at[1, k, t], who)

    def c_copy(self, t, src):
        z, d_core = self.place[1], self.place[5]
        return self.copy(0, t, src, self.c_in.at[lax.rem(t, C_RING)], (d_core, z))

    def a_copy(self, t, q):
        _, z, *_, d_x, d_y = self.place
        src, dst = self.a_out.at[lax.rem(t, 2), q], self.a_in.at[t, q]
        return self.copy(1 + q, t, src, dst, ((d_x, d_y)[q], z))

    def b_copy(self, t, q):
        _, z, *_, d_x, d_y = self.place
        src, dst = self.b_out.at[lax.rem(t, 2), q], self.b_in.at[t, q]
        return self.copy(3 + q, t, src, dst, ((d_y, d_x)[q], z))

    def z_copy(self, t):
        d, z = self.place[:2]
        who = (d, lax.rem(z + self.block(t)[1], self.parts))
        return self.copy(5, t, self.z_out.at[lax.rem(t, 2)], self.z_in.at[t], who)

    def rows(self, q):
        return pl.ds(q * (self.share // 2), self.share // 2)

    def c_start(self, t, src):
        @pl.when(t >= C_RING)
        def _():
            pl.semaphore_wait(self.credit, 1)

        self.c_copy(t, src).start()

    def a_start(self, t, mine, src):
        _, z, _, x, y, d_core, *_ = self.place
        slot, ring = lax.rem(t, 2), lax.rem(t, C_RING)

        @pl.when(t >= 2)
        def _():
            self.a_copy(t - 2, 0).wait_send()
            self.a_copy(t - 2, 1).wait_send()

        self.c_copy(t, src).wait_recv()
        for q in range(2):
            rows = self.rows(q)
            for k in range(2):
                send = (2 * k + 1 - x, 2 * (1 - y) + k)[q]
                keep = (2 * k + x, 2 * y + k)[q]
                self.a_out[slot, q, k] = low(
                    mine[send, rows].astype(F32) + self.c_in[ring, send, rows].astype(F32)
                )
                self.a_keep[slot, q, k] = mine[keep, rows].astype(F32) + self.c_in[
                    ring, keep, rows
                ].astype(F32)
            self.a_copy(t, q).start()

        @pl.when(t < TICKS - C_RING)
        def _():
            pl.semaphore_signal(
                self.credit, inc=1, device_id=(d_core, z), device_id_type=MESH_ID
            )

    def b_start(self, t):
        _, _, _, x, y, *_ = self.place
        slot = lax.rem(t, 2)

        @pl.when(t >= 2)
        def _():
            self.b_copy(t - 2, 0).wait_send()
            self.b_copy(t - 2, 1).wait_send()

        for q in range(2):
            keep = (y, x)[q]
            send = 1 - keep
            self.a_copy(t, q).wait_recv()
            self.b_out[slot, q] = low(
                self.a_keep[slot, q, send] + self.a_in[t, q, send].astype(F32)
            )
            self.b_keep[slot, q] = self.a_keep[slot, q, keep] + self.a_in[t, q, keep].astype(F32)
            self.b_copy(t, q).start()

    def z_start(self, t):
        slot = lax.rem(t, 2)
        g, r = self.block(t)

        @pl.when((t >= 2) & (self.block(t - 2)[1] > 0))
        def _():
            self.z_copy(t - 2).wait_send()

        for q in range(2):
            self.b_copy(t, q).wait_recv()
            done = self.b_keep[slot, q] + self.b_in[t, q].astype(F32)

            @pl.when(r == 0)
            def _():
                self.total[g, self.rows(q)] = done

            @pl.when(r > 0)
            def _():
                self.z_out[slot, self.rows(q)] = low(done)

        @pl.when(r > 0)
        def _():
            self.z_copy(t).start()

    def step(self, t, mine, src):
        @pl.when((t >= 1) & (t < TICKS + 1))
        def _():
            self.a_start(t - 1, mine, src)

        @pl.when((t >= 2) & (t < TICKS + 2))
        def _():
            self.b_start(t - 2)

        @pl.when((t >= 3) & (t < TICKS + 3))
        def _():
            self.z_start(t - 3)

    def finish(self):
        def drain(t, carry):
            self.a_copy(t, 0).wait_send()
            self.a_copy(t, 1).wait_send()
            self.b_copy(t, 0).wait_send()
            self.b_copy(t, 1).wait_send()
            self.z_copy(t).wait_send()
            return carry

        lax.fori_loop(TICKS - 2, TICKS, drain, 0)

        def add(t, carry):
            g, r = self.block(t)

            @pl.when(r > 0)
            def _():
                self.z_copy(t).wait_recv()
                self.total[g] += self.z_in[t].astype(F32)

            return carry

        lax.fori_loop(0, TICKS, add, 0)


class Sum:
    def __init__(self, out, into, ring, send, recv):
        self.out, self.into, self.ring = out, into, ring
        self.send, self.recv = send, recv
        self.place = places()

    def pair(self, k):
        z, who = self.place[1], self.place[5 + k]
        return remote(
            self.out.at[k], self.into.at[k], self.send.at[k], self.recv.at[k], (who, z)
        )

    def along(self, step):
        d, z = self.place[:2]
        parts = self.ring.shape[0]
        return remote(
            self.ring.at[z], self.ring.at[z], self.send.at[2 + step], self.recv.at[2 + step],
            (d, lax.rem(z + step, parts)),
        )

    def start(self, value):
        self.out[0] = value
        self.pair(0).start()

    def turn(self, k):
        self.pair(k).wait()
        value = self.out[k] + self.into[k]
        if k < 2:
            self.out[k + 1] = value
            self.pair(k + 1).start()
            return
        self.ring[self.place[1]] = value
        for step in range(1, self.ring.shape[0]):
            self.along(step).start()

    def result(self):
        parts = self.ring.shape[0]
        z = self.place[1]
        for step in range(1, parts):
            self.along(step).wait_send()
            sender = lax.rem(z + parts - step, parts)
            remote(
                self.ring.at[sender], self.ring.at[sender],
                self.send.at[2 + step], self.recv.at[2 + step], (self.place[0], sender),
            ).wait_recv()
        value = self.ring[0]
        for k in range(1, parts):
            value = value + self.ring[k]
        return value


def forward_kernel(
    halves,
    len_ref,
    x_ref,
    enc_own,
    gains_ref,
    table_own,
    onehot_ref,
    packed,
    result_ref,
    w_hbm,
    xa_out,
    enc_out,
    n1_out,
    q1_out,
    kv1_out,
    p1_out,
    o1_out,
    l1_out,
    x1_out,
    n2_out,
    q2_out,
    kv2_out,
    p2_out,
    o2_out,
    l2_out,
    x2_out,
    n3_out,
    hid_out,
    slope_out,
    w,
    enc,
    diag,
    mask,
    s_buf,
    n1,
    q1,
    kv1,
    p1,
    o1,
    x1,
    n2,
    q2,
    kv2,
    p2,
    o2,
    x2,
    n3,
    hid,
    slope,
    l1,
    l2,
    acc,
    xa_ref,
    table_ref,
    w_sem,
    enc_sem,
    out_sem,
    z_send,
    z_recv,
    s_send,
    s_recv,
    e_send,
    e_recv,
):
    rows = x_ref.shape[0]
    parts = w.shape[1]
    half = half_of_sequence(halves)

    def fetch(g, r, src=w_hbm):
        src = packed.at[g] if src is packed else src.at[g, r]
        return pltpu.make_async_copy(src, w.at[g, r], w_sem.at[g, r])

    d, z_me = places()[:2]
    mate = z_me + 1 - 2 * half
    greet(parts)
    gather = Gather(packed, w_hbm, z_send, z_recv, s_send, s_recv)
    x_copy = remote(x_ref, xa_ref, e_send.at[0], e_recv.at[0], (d, mate))
    enc_copy = remote(enc_own, enc.at[half], e_send.at[1], e_recv.at[1], (d, mate))
    tables = [
        remote(
            table_own, table_ref.at[parts - step], e_send.at[1 + step], e_recv.at[1 + step],
            (d, lax.rem(z_me + step, parts)),
        )
        for step in range(1, parts)
    ]
    gather.z_start(0)
    for copy in tables:
        copy.start()
    x_copy.start()
    gather.z_start(1)
    enc_here = pltpu.make_async_copy(enc_own, enc.at[half], enc_sem)
    for g in range(4):
        fetch(g, 0, packed).start()
    enc_here.start()

    def take(g):
        gather.arrived(g)
        for r in range(1, parts):
            fetch(g, r).start()

    n1[rows : 2 * rows, :] = low(norm_rows(x_ref[...].astype(F32), gains_ref[0:1, :])[0])
    saves = []

    def save(src, dst):
        copy = pltpu.make_async_copy(src, dst, out_sem.at[len(saves)])
        copy.start()
        saves.append(copy)


    length = len_ref[0]
    i = lax.broadcasted_iota(jnp.int32, mask.shape, 0)
    c = lax.broadcasted_iota(jnp.int32, mask.shape, 1)
    own = c - rows
    limit = jnp.where(half > 0, length, 0)
    ok = ((own < 0) & (c < limit)) | ((own >= 0) & (own <= i) & (own + half * rows < length))
    mask[...] = jnp.where(ok, 0.0, MASKED)

    def heads(z, q, kv, p, o, l, keys, with_bias):
        outs = []
        for j in range(3):
            h = z * 3 + j
            q_h = q[z, :, DH * j : DH * (j + 1)]
            k_h = kv[z, :, DH * j : DH * (j + 1)]
            v_h = kv[z, :, DH * (3 + j) : DH * (4 + j)]
            s_buf[j % 2, :, 0:keys] = mm_nt(q_h, k_h)
            for r, n in chunks(rows, 32):
                s = s_buf[j % 2, r : r + n, 0:keys]
                if with_bias:
                    line = jnp.broadcast_to(diag[z, j : j + 1, :], (n, diag.shape[2]))
                    grid = pltpu.roll(line, r, 1, stride=1, stride_axis=0)
                    s = s + grid[:, 0:keys] + mask[r : r + n, :]
                top = jnp.max(s, axis=1, keepdims=True)
                p[h, r : r + n, :] = low(jnp.exp(s - top))
            wide = jnp.concatenate([v_h, jnp.ones_like(v_h)], axis=1)
            mixed = mm(p[h], wide)
            outs.append(low(mixed[:, 0:DH] / mixed[:, DH : 2 * DH]))
            l[z, :, 32 * j : 32 * (j + 1)] = mixed[:, DH : DH + 32]
        o[z] = jnp.concatenate(outs, axis=1)

    acc[...] = x_ref[...].astype(F32)
    gather.tick(0)
    enc_copy.start()
    gather.tick(1)
    for copy in tables:
        copy.wait()
    for r in range(parts):
        lines = table_own[...] if r == 0 else table_ref[r]
        diag[r] = jnp.dot(
            lines, onehot_ref[...], precision=lax.Precision.HIGHEST, preferred_element_type=F32
        )

    x_copy.wait()
    n1[0:rows, :] = low(norm_rows(xa_ref[...].astype(F32), gains_ref[0:1, :])[0])
    save(n1, n1_out)
    save(xa_ref, xa_out)
    gather.tick(2)
    gather.tick(3)
    take(0)

    def self_step(z, carry):
        fetch(0, z).wait()
        kv1[z] = low(mm(n1[...], block(w, 0, z, 0, 384)))
        q1[z] = low(mm(n1[rows : 2 * rows, :], block(w, 0, z, 384, 576)))
        heads(z, q1, kv1, p1, o1, l1, 2 * rows, True)
        acc[...] += mm_nt(o1[z], block(w, 0, z, 576, 768))

        @pl.when(z == 1)
        def _():
            gather.tick(4)

        return carry

    lax.fori_loop(0, parts, self_step, 0)
    for src, dst in ((q1, q1_out), (kv1, kv1_out), (p1, p1_out), (o1, o1_out), (l1, l1_out)):
        save(src, dst)
    x1[...] = acc[...]
    n2[...] = low(norm_rows(acc[...], gains_ref[1:2, :])[0])
    save(x1, x1_out)
    save(n2, n2_out)
    gather.tick(5)
    take(1)
    enc_copy.wait()
    enc_here.wait()
    save(enc, enc_out)
    keys = 2 * enc.shape[1]

    def cross_step(z, carry):
        fetch(1, z).wait()
        kv2[z] = low(mm(enc[...].reshape(keys, enc.shape[2]), block(w, 1, z, 0, 384)))
        q2[z] = low(mm(n2[...], block(w, 1, z, 384, 576)))
        heads(z, q2, kv2, p2, o2, l2, keys, False)
        acc[...] += mm_nt(o2[z], block(w, 1, z, 576, 768))

        @pl.when(z == 1)
        def _():
            gather.tick(6)

        return carry

    lax.fori_loop(0, parts, cross_step, 0)
    for src, dst in ((q2, q2_out), (kv2, kv2_out), (p2, p2_out), (o2, o2_out), (l2, l2_out)):
        save(src, dst)
    x2[...] = acc[...]
    n3[...] = low(norm_rows(acc[...], gains_ref[2:3, :])[0])
    save(x2, x2_out)
    save(n3, n3_out)
    gather.tick(7)
    take(2)

    def inner_step(z, carry):
        fetch(2, z).wait()
        for r, n in chunks(rows, 64):
            a = mm(n3[r : r + n, :], block(w, 2, z))
            sq = a * a
            t = jnp.tanh(a * (ROOT + ROOT * CUBE * sq))
            cdf = 0.5 + 0.5 * t
            hid[z, r : r + n, :] = low(a * cdf)
            slope[z, r : r + n, :] = low(
                cdf + 0.5 * a * (1.0 - t * t) * (ROOT + 3.0 * ROOT * CUBE * sq)
            )

        @pl.when(z == 1)
        def _():
            gather.tick(8)

        return carry

    lax.fori_loop(0, parts, inner_step, 0)
    save(hid, hid_out)
    save(slope, slope_out)
    gather.tick(9)
    take(3)

    def outer_step(z, carry):
        fetch(3, z).wait()
        acc[...] += mm_nt(hid[z], block(w, 3, z))
        return carry

    lax.fori_loop(0, parts, outer_step, 0)
    result_ref[...] = low(acc[...])
    for copy in saves:
        copy.wait()
    gather.sent()


def backward_kernel(
    x_ref, xa_ref, cot_ref, gains_ref, onehot_ref, enc_hbm, packed, w_hbm,
    n1_hbm, q1_hbm, kv1_hbm, p1_hbm, o1_hbm, l1_hbm, x1_hbm,
    n2_hbm, q2_hbm, kv2_hbm, p2_hbm, o2_hbm, l2_hbm, x2_hbm,
    n3_hbm, hid_hbm, slope_hbm,
    total_out, small_out, dx_out, denc_out,
    w, enc, nbuf, n2, q_in, kv_in, p_in, o_in, l_in, x_in, hid, slope,
    g_buf, rows_t, rows_t2, keys_t, dp_buf, ds_buf, dkv_t, dn, acc, enc_acc, diag_acc,
    dxa, dxa_in, denc, denc_in, small,
    c_in, a_in, b_in, z_in, a_out, a_keep, b_out, b_keep, z_out, s_out, s_in, s_ring,
    w_sem, one_sem, ring_sem,
    sems, credit, s_send, s_recv, e_send, e_recv,
):
    rows, width_all = x_ref.shape
    parts = w_hbm.shape[1]
    place = places()
    d, z_me, core = place[:3]
    half = lax.rem(z_me, 2)
    mate = z_me + 1 - 2 * half
    keys = 2 * enc.shape[1]
    own_keys = 2 * rows

    singles = [(n3_hbm, nbuf.at[0:rows]), (x2_hbm, x_in), (n2_hbm, n2), (enc_hbm, enc),
               (x1_hbm, x_in), (n1_hbm, nbuf)]

    def single(k):
        return pltpu.make_async_copy(*singles[k], one_sem.at[k])

    def streams(phase, r):
        slot = lax.rem(r, 2)
        if phase == 0:
            pairs = [(hid_hbm.at[r], hid.at[slot]), (slope_hbm.at[r], slope.at[slot])]
        else:
            q, kv, p, o, l = (
                (q2_hbm, kv2_hbm, p2_hbm, o2_hbm, l2_hbm),
                (q1_hbm, kv1_hbm, p1_hbm, o1_hbm, l1_hbm),
            )[phase - 1]
            n = (keys, own_keys)[phase - 1]
            pairs = [
                (q.at[r], q_in.at[slot]),
                (kv.at[r], kv_in.at[slot, 0:n]),
                (p.at[pl.ds(3 * r, 3)], p_in.at[slot, :, :, 0:n]),
                (o.at[r], o_in.at[slot]),
                (l.at[r], l_in.at[slot]),
            ]
        return [
            pltpu.make_async_copy(src, dst, ring_sem.at[k, slot])
            for k, (src, dst) in enumerate(pairs)
        ]

    def weight(g, r, k, src=None):
        slot = lax.rem(r, 2)
        src = w_hbm.at[g, r] if src is None else src.at[g]
        return pltpu.make_async_copy(src, w.at[slot, k], w_sem.at[slot, k])

    groups = ((3, 2), (1,), (0,))

    def prefetch(phase, r, first):
        for k, g in enumerate(groups[phase]):
            weight(g, r, k, packed if first else None).start()
        for copy in streams(phase, r):
            copy.start()

    def turn(phase, r):
        for k, g in enumerate(groups[phase]):
            weight(g, r, k).wait()
        for copy in streams(phase, r):
            copy.wait()

        @pl.when(r + 1 < parts)
        def _():
            prefetch(phase, r + 1, False)

        if phase < 2:

            @pl.when(r + 1 == parts)
            def _():
                prefetch(phase + 1, 0, True)

    prefetch(0, 0, True)
    for k in range(4):
        single(k).start()

    greet(parts)
    scatter = Scatter(
        (c_in, a_in, b_in, z_in, a_out, a_keep, b_out, b_keep, z_out, total_out), sems, credit
    )
    sums = Sum(s_out, s_in, s_ring, s_send, s_recv)
    dxa_copy = remote(dxa, dxa_in, e_send.at[0], e_recv.at[0], (d, mate))
    denc_copy = remote(denc.at[1 - half], denc_in, e_send.at[1], e_recv.at[1], (d, mate))

    def away(t):
        return g_buf.at[lax.rem(t, 2), :, 1 - core]

    def claim(t):
        @pl.when(t >= 2)
        def _():
            scatter.c_copy(t - 2, away(t)).wait_send()

    def put(t, value, start=0):
        shape = g_buf.shape[1:4] + (value.shape[1],)
        g_buf[lax.rem(t, 2), :, :, :, start : start + value.shape[1]] = value.reshape(shape)

    def release(t):
        scatter.c_start(t, away(t))
        scatter.step(t, g_buf.at[lax.rem(t + 1, 2), :, core], away(t + 1))

    rows_t[...] = flip(cot_ref[...])
    single(0).wait()
    rows_t2[...] = flip(nbuf[0:rows, :])
    acc[...] = jnp.zeros_like(acc)

    def feed_step(r, carry):
        turn(0, r)
        slot = lax.rem(r, 2)
        dh = low(mm(cot_ref[...], block(w, slot, 0)))
        claim(2 * r)
        put(2 * r, low(mm(rows_t[...], hid[slot])))
        release(2 * r)
        slope[slot] = low(dh.astype(F32) * slope[slot].astype(F32))
        claim(2 * r + 1)
        put(2 * r + 1, low(mm(rows_t2[...], slope[slot])))
        release(2 * r + 1)
        acc[...] += mm_nt(slope[slot], block(w, slot, 1))
        return carry

    lax.fori_loop(0, parts, feed_step, 0)
    single(1).wait()
    back, gain3 = norm_back(acc[...], x_in[...], gains_ref[2:3, :])
    dn[...] = cot_ref[...].astype(F32) + back
    single(4).start()
    single(5).start()
    small[...] = jnp.zeros_like(small)
    small[2:3, 0:width_all] = gain3

    def heads_back(r, do, n, with_diag):
        slot = lax.rem(r, 2)
        q, kv, o = q_in[slot], kv_in.at[slot], o_in[slot].astype(F32)
        do_all = []
        delta_all = []
        for j in range(3):
            do_h = do[:, DH * j : DH * (j + 1)]
            inv = 1.0 / l_in[slot, :, 32 * j : 32 * j + 1]
            o_h = o[:, DH * j : DH * (j + 1)]
            delta_all.append(jnp.sum(do_h * o_h * inv, axis=1, keepdims=True))
            do_all.append(do_h * inv)
        do_t = low(jnp.transpose(jnp.concatenate(do_all, axis=1)))
        q_t = flip(q)
        dq = []
        for j in range(3):
            p_h = p_in.at[slot, j]
            k_h = kv[0:n, DH * j : DH * (j + 1)]
            v_h = kv[0:n, DH * (3 + j) : DH * (4 + j)]
            dp_buf[j % 2, :, 0:n] = mm_nt(low(do_all[j]), v_h)
            total = None
            for s, m in chunks(rows, 32):
                ds = low(
                    p_h[s : s + m, 0:n].astype(F32)
                    * (dp_buf[j % 2, s : s + m, 0:n] - delta_all[j][s : s + m, :])
                )
                ds_buf[j % 2, s : s + m, 0:n] = ds
                if with_diag:
                    width = diag_acc.shape[2]
                    wide = jnp.concatenate([ds.astype(F32), jnp.zeros((m, width - n), F32)], axis=1)
                    for b in range(0, m, 8):
                        turned = pltpu.roll(wide[b : b + 8, :], (width - s - b) % width, 1)
                        total = turned if total is None else total + turned
            if with_diag:
                diag_acc[r * 3 + j] = total
            ds_h = ds_buf[j % 2, :, 0:n]
            dq.append(low(mm(ds_h, k_h)))
            dkv_t[DH * j : DH * (j + 1), 0:n] = mm(q_t[DH * j : DH * (j + 1), :], ds_h)
            dkv_t[DH * (3 + j) : DH * (4 + j), 0:n] = mm(
                do_t[DH * j : DH * (j + 1), :], p_h[:, 0:n]
            )
        return jnp.concatenate(dq, axis=1), low(jnp.transpose(dkv_t[:, 0:n]))

    def attention_step(phase, n, r):
        slot = lax.rem(r, 2)
        t = 4 + 4 * phase + r
        turn(phase, r)
        do = low(mm(low(dn[...]), block(w, slot, 0, 576, 768))).astype(F32)
        dq, dkv = heads_back(r, do, n, phase == 2)
        claim(t)
        put(t, low(mm(keys_t[:, 0:n], dkv)))
        both = [low(mm(rows_t2[...], dq)), low(mm(rows_t[...], o_in[slot]))]
        put(t, jnp.concatenate(both, axis=1), 384)
        release(t)
        acc[...] += mm_nt(dq, block(w, slot, 0, 384, 576))
        enc_acc[0:n, :] += mm_nt(dkv, block(w, slot, 0, 0, 384))

    rows_t[...] = flip(low(dn[...]))
    single(2).wait()
    single(3).wait()
    rows_t2[...] = flip(n2[...])
    keys_t[...] = flip(enc[...].reshape(keys, width_all))
    acc[...] = jnp.zeros_like(acc)
    enc_acc[...] = jnp.zeros_like(enc_acc)

    def cross_step(r, carry):
        attention_step(1, keys, r)
        return carry

    lax.fori_loop(0, parts, cross_step, 0)
    denc[...] = low(enc_acc[...]).reshape(denc.shape)
    denc_copy.start()
    single(4).wait()
    back, gain2 = norm_back(acc[...], x_in[...], gains_ref[1:2, :])
    dn[...] += back
    small[1:2, 0:width_all] = gain2

    rows_t[...] = flip(low(dn[...]))
    single(5).wait()
    rows_t2[...] = flip(nbuf[rows : 2 * rows, :])
    keys_t[:, 0:own_keys] = flip(nbuf[...])
    acc[...] = jnp.zeros_like(acc)
    enc_acc[0:own_keys, :] = jnp.zeros((own_keys, width_all), F32)

    def self_step(r, carry):
        attention_step(2, own_keys, r)
        return carry

    lax.fori_loop(0, parts, self_step, 0)
    gain = gains_ref[0:1, :]
    back, gain1a = norm_back(enc_acc[0:rows, :], xa_ref[...].astype(F32), gain)
    dxa[...] = low(back)

    @pl.when(half == 1)
    def _():
        dxa_copy.start()

    back, gain1 = norm_back(
        acc[...] + enc_acc[rows : 2 * rows, :], x_ref[...].astype(F32), gain
    )
    dn[...] += back
    small[0:1, 0:width_all] = gain1 + gain1a
    width = diag_acc.shape[2]
    lines = []
    for r in range(parts):
        for j in range(3):
            part = diag_acc[3 * r + j]
            line = part[0:1, :]
            for k in range(1, 8):
                line = line + pltpu.roll(part[k : k + 1, :], width - k, 1)
            lines.append(line)
    lines.append(jnp.zeros((16 - len(lines), width), F32))
    table = lax.dot_general(
        jnp.concatenate(lines, axis=0),
        onehot_ref[...],
        (((1,), (1,)), ((), ())),
        precision=lax.Precision.HIGHEST,
        preferred_element_type=F32,
    )
    for r in range(parts):
        at = lax.rem(z_me + r, parts)
        for p in range(parts):

            @pl.when(at == p)
            def _(r=r, p=p):
                small[3 + p : 4 + p, width_all : width_all + 128] = table[3 * r : 3 * r + 1]
                small[3 + p : 4 + p, width_all + 128 :] = table[3 * r + 1 : 3 * r + 2]
                small[3 + p : 4 + p, 0:128] = table[3 * r + 2 : 3 * r + 3]

    sums.start(small[...])

    def tail(t, carry):
        scatter.step(t, g_buf.at[lax.rem(t + 1, 2), :, core], away(t + 1))
        for k in range(3):

            @pl.when(t == TICKS + k)
            def _(k=k):
                sums.turn(k)

        return carry

    lax.fori_loop(TICKS, TICKS + 3, tail, 0)
    denc_copy.wait()
    denc_out[...] = low(denc[half].astype(F32) + denc_in[...].astype(F32))
    scatter.finish()
    small_out[...] = sums.result()

    @pl.when(half == 1)
    def _():
        dxa_copy.wait_send()
        dx_out[...] = low(dn[...])

    @pl.when(half == 0)
    def _():
        dxa_copy.wait_recv()
        dx_out[...] = low(dn[...] + dxa_in[...].astype(F32))

    for t in (TICKS - 2, TICKS - 1):
        scatter.c_copy(t, away(t)).wait_send()


def across_groups(summed, small, n_dp):
    groups = n_dp // 8
    d = lax.axis_index("dp")
    whole = lax.all_gather(summed, "dp", axis=0, tiled=False)
    share, width = summed.shape[1:]
    whole = whole.reshape(groups, 8, 4, share, width).sum(0)
    whole = jnp.transpose(whole, (1, 0, 2, 3)).reshape(4, 8 * share, width)
    rows = 8 * share // n_dp
    small = lax.all_gather(small, "dp", axis=0, tiled=False).reshape(groups, 8, *small.shape)[:, 0]
    return lax.dynamic_slice_in_dim(whole, d * rows, rows, 1), small.sum(0)


def body(
    inputs, encoded, cotangent, lengths, buckets,
    self_gain, self_query, self_key, self_value, self_output, bias_table,
    cross_gain, cross_query, cross_key, cross_value, cross_output,
    feed_gain, feed_inner, feed_output_weight,
):
    rows, width = inputs.shape
    parts = lax.axis_size("mp")
    n_dp = lax.axis_size("dp")
    halves = parts // lengths.shape[0]
    assert halves == 2 and buckets.shape[0] == 2 * rows and parts == 4
    z = lax.axis_index("mp")
    enc_rows = encoded.shape[0]
    vmem = pl.BlockSpec(memory_space=pltpu.VMEM)
    smem = pl.BlockSpec(memory_space=pltpu.SMEM)
    hbm = pl.BlockSpec(memory_space=pl.ANY)
    sds = jax.ShapeDtypeStruct

    share = width // 8
    packed = jnp.stack(
        [
            jnp.concatenate([self_key, self_value, self_query, self_output.T], axis=1),
            jnp.concatenate([cross_key, cross_value, cross_query, cross_output.T], axis=1),
            feed_inner,
            feed_output_weight.T,
        ]
    ).reshape(4, 4, 2, share, width)
    table_own = jnp.pad(bias_table.T, ((0, 8 - bias_table.shape[1]), (0, 128 - bias_table.shape[0])))
    length = lax.dynamic_slice_in_dim(lengths, lax.div(z, 2), 1)
    gains = jnp.concatenate(
        [jnp.stack([self_gain, cross_gain, feed_gain]), jnp.zeros((5, width), F32)]
    )
    diag = 1024
    line = jnp.concatenate(
        [
            buckets[0 : rows + 1][::-1],
            jnp.full((diag - 2 * rows,), -1, jnp.int32),
            buckets[rows + 1 :][::-1],
        ]
    )
    onehot = (line[None, :] == lax.iota(jnp.int32, 128)[:, None]).astype(F32)
    heads = 3 * parts
    keys = 2 * enc_rows
    saved = [
        ((2 * rows, width), BF16),
        ((parts, rows, 192), BF16),
        ((parts, 2 * rows, 384), BF16),
        ((heads, rows, 2 * rows), BF16),
        ((parts, rows, 192), BF16),
        ((parts, rows, 128), F32),
        ((rows, width), F32),
        ((rows, width), BF16),
        ((parts, rows, 192), BF16),
        ((parts, keys, 384), BF16),
        ((heads, rows, keys), BF16),
        ((parts, rows, 192), BF16),
        ((parts, rows, 128), F32),
        ((rows, width), F32),
        ((rows, width), BF16),
        ((parts, rows, width), BF16),
        ((parts, rows, width), BF16),
    ]
    n1s, q1s, kv1s, p1s, o1s, l1s, x1s, n2s, q2s, kv2s, p2s, o2s, l2s, x2s, n3s, hids, slopes = [
        pltpu.VMEM(*s) for s in saved
    ]
    result, weights, other, enc_all, *kept = pl.pallas_call(
        functools.partial(forward_kernel, halves),
        out_shape=[
            sds((rows, width), BF16),
            sds((4, parts, 4, 2, share, width), BF16),
            sds((rows, width), BF16),
            sds((2, enc_rows, width), BF16),
        ]
        + [sds(*s) for s in saved],
        in_specs=[smem, vmem, hbm, vmem, vmem, vmem, hbm],
        out_specs=[vmem] + [hbm] * (3 + len(saved)),
        scratch_shapes=[
            pltpu.VMEM((4, parts, 4, 2, share, width), BF16),
            pltpu.VMEM((2, enc_rows, width), BF16),
            pltpu.VMEM((parts, 8, diag), F32),
            pltpu.VMEM((rows, 2 * rows), F32),
            pltpu.VMEM((2, rows, keys), F32),
            n1s, q1s, kv1s, p1s, o1s, x1s, n2s, q2s, kv2s, p2s, o2s, x2s, n3s, hids, slopes,
            l1s, l2s,
            pltpu.VMEM((rows, width), F32),
            pltpu.VMEM((rows, width), BF16),
            pltpu.VMEM((parts, 8, 128), F32),
            pltpu.SemaphoreType.DMA((4, parts)),
            pltpu.SemaphoreType.DMA,
            pltpu.SemaphoreType.DMA((2 + len(saved),)),
            pltpu.SemaphoreType.DMA((8, parts - 1)),
            pltpu.SemaphoreType.DMA((8, parts - 1)),
            pltpu.SemaphoreType.DMA((8, 5)),
            pltpu.SemaphoreType.DMA((8, 5)),
            pltpu.SemaphoreType.DMA((5,)),
            pltpu.SemaphoreType.DMA((5,)),
        ],
        compiler_params=pltpu.CompilerParams(
            collective_id=1, has_side_effects=True, vmem_limit_bytes=VMEM_BYTES
        ),
        name="forward",
    )(length, inputs, encoded, gains, table_own, onehot, packed)

    half_share = share // 2
    summed, small, input_grad, encoder_grad = pl.pallas_call(
        backward_kernel,
        out_shape=[
            sds((4, share, width), F32),
            sds((8, diag), F32),
            sds((rows, width), BF16),
            sds((enc_rows, width), BF16),
        ],
        in_specs=[vmem] * 5 + [hbm] * 20,
        out_specs=[vmem] * 4,
        scratch_shapes=[
            pltpu.VMEM((2, 2, 4, 2, share, width), BF16),
            pltpu.VMEM((2, enc_rows, width), BF16),
            pltpu.VMEM((2 * rows, width), BF16),
            pltpu.VMEM((rows, width), BF16),
            pltpu.VMEM((2, rows, 192), BF16),
            pltpu.VMEM((2, keys, 384), BF16),
            pltpu.VMEM((2, 3, rows, keys), BF16),
            pltpu.VMEM((2, rows, 192), BF16),
            pltpu.VMEM((2, rows, 128), F32),
            pltpu.VMEM((rows, width), F32),
            pltpu.VMEM((2, rows, width), BF16),
            pltpu.VMEM((2, rows, width), BF16),
            pltpu.VMEM((2, 4, 2, share, width), BF16),
            pltpu.VMEM((width, rows), BF16),
            pltpu.VMEM((width, rows), BF16),
            pltpu.VMEM((width, keys), BF16),
            pltpu.VMEM((2, rows, keys), F32),
            pltpu.VMEM((2, rows, keys), BF16),
            pltpu.VMEM((384, keys), F32),
            pltpu.VMEM((rows, width), F32),
            pltpu.VMEM((rows, width), F32),
            pltpu.VMEM((keys, width), F32),
            pltpu.VMEM((heads, 8, diag), F32),
            pltpu.VMEM((rows, width), BF16),
            pltpu.VMEM((rows, width), BF16),
            pltpu.VMEM((2, enc_rows, width), BF16),
            pltpu.VMEM((enc_rows, width), BF16),
            pltpu.VMEM((8, diag), F32),
            pltpu.VMEM((C_RING, 4, share, width), BF16),
            pltpu.VMEM((TICKS, 2, 2, half_share, width), BF16),
            pltpu.VMEM((TICKS, 2, half_share, width), BF16),
            pltpu.VMEM((TICKS, share, width), BF16),
            pltpu.VMEM((2, 2, 2, half_share, width), BF16),
            pltpu.VMEM((2, 2, 2, half_share, width), F32),
            pltpu.VMEM((2, 2, half_share, width), BF16),
            pltpu.VMEM((2, 2, half_share, width), F32),
            pltpu.VMEM((2, share, width), BF16),
            pltpu.VMEM((3, 8, diag), F32),
            pltpu.VMEM((3, 8, diag), F32),
            pltpu.VMEM((parts, 8, diag), F32),
            pltpu.SemaphoreType.DMA((2, 2)),
            pltpu.SemaphoreType.DMA((6,)),
            pltpu.SemaphoreType.DMA((5, 2)),
            pltpu.SemaphoreType.DMA((2, 6, TICKS)),
            pltpu.SemaphoreType.REGULAR,
            pltpu.SemaphoreType.DMA((6,)),
            pltpu.SemaphoreType.DMA((6,)),
            pltpu.SemaphoreType.DMA((2,)),
            pltpu.SemaphoreType.DMA((2,)),
        ],
        compiler_params=pltpu.CompilerParams(
            collective_id=2, has_side_effects=True, vmem_limit_bytes=VMEM_BYTES
        ),
        name="backward",
    )(inputs, other, cotangent, gains, onehot, enc_all, packed, weights, *kept)
    if n_dp > 8:
        summed, small = across_groups(summed, small, n_dp)
    buckets_here = bias_table.shape[0]
    mine = lax.dynamic_slice_in_dim(small, 3 + z, 1, 0)[0]
    table_mine = jnp.stack(
        [mine[width : width + buckets_here], mine[width + 128 :][:buckets_here], mine[:buckets_here]],
        axis=1,
    )
    gs, gc = summed[0], summed[1]
    return (
        result,
        low(input_grad),
        low(encoder_grad),
        small[0, :width],
        gs[:, 384:576],
        gs[:, 0:192],
        gs[:, 192:384],
        gs[:, 576:768].T,
        table_mine,
        small[1, :width],
        gc[:, 384:576],
        gc[:, 0:192],
        gc[:, 192:384],
        gc[:, 576:768].T,
        small[2, :width],
        summed[2],
        summed[3].T,
    )


def solution(mesh):
    rows = P(("dp", "mp"), None)
    across, down = P(None, "mp"), P("mp", None)
    return jax.shard_map(
        body,
        mesh=mesh,
        in_specs=(
            rows, rows, rows, P("dp"), P(),
            P(), across, across, across, down, across,
            P(), across, across, across, down,
            P(), across, down,
        ),
        out_specs=(
            rows, rows, rows,
            P(), P("dp", "mp"), P("dp", "mp"), P("dp", "mp"), P("mp", "dp"), P(None, "mp"),
            P(), P("dp", "mp"), P("dp", "mp"), P("dp", "mp"), P("mp", "dp"),
            P(), P("dp", "mp"), P("mp", "dp"),
        ),
        check_vma=False,
    )
```

time: 341 us -> 259 us (0.76)
  Pallas kernels: 317 us -> 230 us
  local copies, waits for them, and re-layouts: 14.7 us -> 19.6 us
    pallas_call x3 -> x1, Pallas kernels: 278 us -> 119 us  [body(): pl.pallas_call(backward_kernel, out_shape=[sds((4, share, width), F32), s...]
    pallas_call x1, Pallas kernels: 38.9 us -> 111 us  [body(): pl.pallas_call(functools.partial(forward_kernel, halves), out_shape=[sds(...]
where the time goes in v3:
time: 259 us; the launch traced here: 258 us
  Pallas kernels  230 us (89%)
  local copies, waits for them, and re-layouts  19.6 us (8%)
  other arithmetic  8.13 us (3%)
    pallas_call x1, Pallas kernels, body(): pl.pallas_call(backward_kernel, out_shape=[sds((4, share, width), F32), s...  119 us
    pallas_call x1, Pallas kernels, body(): pl.pallas_call(functools.partial(forward_kernel, halves), out_shape=[sds(...  111 us

profile of v3, /device:TPU:0, one launch (start us, length us, event | category | flops | bytes accessed | tf_op | source)
XLA Modules:
  0.0 258.0 jit_solution(11847694157653879630)
XLA Ops:
  0.7 1.3 dynamic_slice.6.len_ref
  2.0 0.7 stack.38
  2.7 0.7 stack.37
  3.4 0.7 stack.36
  4.2 0.7 maximum_maximum_fusion.gains_ref
  4.9 1.3 pad.4.table_own
  6.1 0.8 slice.67
  7.1 0.7 slice.66
  8.0 0.9 fusion.onehot_ref
  8.9 1.6 copy.38
  11.2 2.3 pad_maximum_fusion.1
  13.5 1.6 copy.36
  15.1 3.5 %pad_maximum_fusion.packed = bf16[4,4,2,96,768]{4,3,2,1,0:T(8,128)(2,1)} fusion(bf16[1,4,2,96,768]{4,3,2,1,0:T(8,128)(2,1)S(1)} %bitcast.30, bf16[1,4,2,96,768]{4,3,2,1,0:T(8,128)(2,1)} %bitcast.33, bf16[1,4,2,96,768]{4,3,2,1,0:T(8,128)(2,1)S(1)} %bitcast.31, bf16[1,4,2,96,768]{4,3,2,1,0:T(8,128)(2,1)S(1)} %bitcast.32), kind=kLoop, calls=%fused_computation | loop fusion | flops 7077888 | bytes 9437184 | tf_op jit(solution)/shard_map/stack | solution.py:959
  18.6 110.7 %forward.1 = (bf16[320,768]{1,0:T(8,128)(2,1)}, bf16[4,4,4,2,96,768]{5,4,3,2,1,0:T(8,128)(2,1)}, bf16[320,768]{1,0:T(8,128)(2,1)}, bf16[2,512,768]{2,1,0:T(8,128...) custom-call(s32[1]{0:T(128)} %dynamic_slice.6.len_ref, ...), custom_call_target="tpu_custom_call" | custom-call | tf_op jit(solution)/shard_map/forward/pallas_call | solution.py:1005
  129.4 118.8 %backward.1 = (f32[4,96,768]{2,1,0:T(8,128)}, f32[8,1024]{1,0:T(8,128)}, bf16[320,768]{1,0:T(8,128)(2,1)}, bf16[512,768]{1,0:T(8,128)(2,1)}) custom-call(bf16[320,768]{1,0:T(8,128)(2,1)} %x_ref.3, bf16[320,768]{1,0:T(8,128)(2,1)} %get-tuple-element.43.xa_ref, bf16[320,768]{1,0:T(8,128)(2,1)} %cot_ref.1, f32[8,768]{1,0:T(8,128)} %maximum_maximum_fusion.gains_ref, ...), custom_call_target="tpu_custom_call" | custom-call | tf_op jit(solution)/shard_map/backward/pallas_call | solution.py:1044
  248.2 1.5 slice_reduce_fusion
  249.7 2.2 slice_bitcast_fusion
  251.9 0.9 slice_bitcast_fusion.4
  252.7 0.7 copy.39
  253.5 0.8 dynamic-slice_bitcast_fusion.2
  254.9 0.7 copy.40
  255.6 0.8 copy.44
  256.4 0.8 copy.45
  257.2 0.9 copy.46
  (25 shorter events, 1.8 us)
Async XLA Ops:
  0.7 9.8 %copy-start.3 = (bf16[192,768]{1,0:T(8,128)(2,1)S(1)}, bf16[192,768]{1,0:T(8,128)(2,1)}, u32[]{:S(2)}) copy-start(bf16[192,768]{1,0:T(8,128)(2,1)} %param.34) | copy-start | bytes 884740
  0.7 9.8 %copy-start.4 = (bf16[768,192]{0,1:T(8,128)(2,1)S(1)}, bf16[768,192]{0,1:T(8,128)(2,1)}, u32[]{:S(2)}) copy-start(bf16[768,192]{0,1:T(8,128)(2,1)} %param.31) | copy-start | bytes 884740
  0.7 9.8 %copy-start.5 = (bf16[768,192]{0,1:T(8,128)(2,1)S(1)}, bf16[768,192]{0,1:T(8,128)(2,1)}, u32[]{:S(2)}) copy-start(bf16[768,192]{0,1:T(8,128)(2,1)} %param.33) | copy-start | bytes 884740
  0.7 9.8 %copy-start.6 = (bf16[768,192]{0,1:T(8,128)(2,1)S(1)}, bf16[768,192]{0,1:T(8,128)(2,1)}, u32[]{:S(2)}) copy-start(bf16[768,192]{0,1:T(8,128)(2,1)} %param.32) | copy-start | bytes 884740
  249.7 5.9 %copy-start.1 = (bf16[320,768]{1,0:T(8,128)(2,1)S(1)}, bf16[320,768]{1,0:T(8,128)(2,1)}, u32[]{:S(2)}) copy-start(bf16[320,768]{1,0:T(8,128)(2,1)} %get-tuple-element.123) | copy-start | bytes 1474564
  251.9 4.5 %copy-start.2 = (bf16[320,768]{1,0:T(8,128)(2,1)S(1)}, bf16[320,768]{1,0:T(8,128)(2,1)}, u32[]{:S(2)}) copy-start(bf16[320,768]{1,0:T(8,128)(2,1)} %get-tuple-element.124) | copy-start | bytes 1474564
  251.9 5.3 %copy-start = (bf16[512,768]{1,0:T(8,128)(2,1)S(1)}, bf16[512,768]{1,0:T(8,128)(2,1)}, u32[]{:S(2)}) copy-start(bf16[512,768]{1,0:T(8,128)(2,1)} %get-tuple-element.125) | copy-start | bytes 2359300

commit v4 on v3

v4 whole, which is shorter than its diff:
```python
import functools

import jax
import jax.numpy as jnp
from jax import lax
from jax.experimental import pallas as pl
from jax.experimental.pallas import tpu as pltpu
from jax.sharding import PartitionSpec as P

EPS = 1e-06
MASKED = -1e30
DH = 64
F32 = jnp.float32
BF16 = jnp.bfloat16
VMEM_BYTES = 62 << 20
ROOT = 0.7978845608028654
CUBE = 0.044715


def mm(a, b):
    return jnp.dot(a, b, preferred_element_type=F32)


def mm_nt(a, b):
    return lax.dot_general(a, b, (((1,), (1,)), ((), ())), preferred_element_type=F32)


def line_of(ref):
    return ref[...].reshape(1, ref.shape[0])


def low(v):
    return v.astype(BF16)


def flip(v):
    return jnp.transpose(v.astype(F32)).astype(BF16)


def norm_rows(v, gain):
    root = lax.rsqrt(jnp.mean(v * v, axis=-1, keepdims=True) + EPS)
    unit = v * root
    return unit * gain, unit, root


def norm_back(grad, v, gain):
    _, unit, root = norm_rows(v, gain)
    scaled = grad * gain
    back = root * (scaled - unit * jnp.mean(scaled * unit, axis=-1, keepdims=True))
    return back, jnp.sum(grad * unit, axis=0, keepdims=True)


def block(w, i, j, start=0, stop=None):
    part = w[i, j]
    part = part.reshape(part.shape[0] * part.shape[1] * part.shape[2], part.shape[3])
    return part[start:stop]


def half_of_sequence(halves):
    return lax.rem(lax.axis_index("mp"), halves)


def chunks(rows, step):
    return [(r, min(step, rows - r)) for r in range(0, rows, step)]


MESH_ID = pl.DeviceIdType.MESH


def places():
    d = lax.axis_index("dp")
    z = lax.axis_index("mp")
    lo = lax.rem(d, 8)
    core = lax.rem(lo, 2)
    x = lax.rem(lax.div(lo, 2), 2)
    y = lax.div(lo, 4)
    d_core = d + 1 - 2 * core
    d_x = d + 2 - 4 * x
    d_y = d + 4 - 8 * y
    return d, z, core, x, y, d_core, d_x, d_y


def peer(k):
    d = lax.axis_index("dp")
    lo = lax.rem(d, 8)
    return d - lo + lax.rem(lo + k, 8)


def greet(z_parts, everyone):
    d, z, _, _, _, d_core, d_x, d_y = places()
    barrier = pltpu.get_barrier_semaphore()
    near = [peer(k) for k in range(1, 8)] if everyone else [d_core, d_x, d_y]
    for who in near:
        pl.semaphore_signal(barrier, inc=1, device_id=(who, z), device_id_type=MESH_ID)
    for step in range(1, z_parts):
        pl.semaphore_signal(
            barrier, inc=1, device_id=(d, lax.rem(z + step, z_parts)), device_id_type=MESH_ID
        )
    return lambda: pl.semaphore_wait(barrier, len(near) + z_parts - 1)


def remote(src, dst, send, recv, who):
    return pltpu.make_async_remote_copy(
        src_ref=src, dst_ref=dst, send_sem=send, recv_sem=recv, device_id=who, device_id_type=MESH_ID
    )


class Gather:
    parts_of_group = 3
    chunks = 12
    ahead = 6

    def __init__(self, mine, wg, z_send, z_recv, s_send, s_recv):
        self.mine, self.wg = mine, wg
        self.z_sems, self.s_sems = (z_send, z_recv), (s_send, s_recv)
        self.parts = wg.shape[1]
        self.place = places()

    def rows(self, k):
        some = self.wg.shape[4] // self.parts_of_group
        return k // self.parts_of_group, pl.ds((k % self.parts_of_group) * some, some)

    def z_copy(self, k, step):
        d, z, core, x, y, *_ = self.place
        yx = 2 * y + x
        g, rows = self.rows(k)
        return remote(
            self.mine.at[g, 0, yx, core, rows],
            self.wg.at[g, self.parts - step, yx, core, rows],
            self.z_sems[0].at[k, step - 1],
            self.z_sems[1].at[k, step - 1],
            (d, lax.rem(z + step, self.parts)),
        )

    def s_copy(self, k, n):
        d, z, core, x, y, d_core, d_x, d_y = self.place
        rest = pl.ds(1, self.parts - 1)
        g, rows = self.rows(k)
        width = self.wg.shape[5]
        if n < 2:
            ref = self.wg.at[g, rest, 2 * y + x, core, rows]
            who = (d_x, d_y)[n]
        elif n == 2:
            ref = self.wg.at[g, rest, 2 * y + 1 - x, core, rows, pl.ds(0, width // 2)]
            who = d_y
        elif n == 3:
            ref = self.wg.at[g, rest, 2 * (1 - y) + x, core, rows, pl.ds(width // 2, width // 2)]
            who = d_x
        else:
            ref = self.wg.at[g, rest, :, core, rows]
            who = d_core
        return remote(ref, ref, self.s_sems[0].at[k, n], self.s_sems[1].at[k, n], (who, z))

    def z_start(self, k):
        for step in range(1, self.parts):
            self.z_copy(k, step).start()

    def tick(self, k):
        if k < self.chunks:
            for step in range(1, self.parts):
                self.z_copy(k, step).wait_recv()
            self.s_copy(k, 0).start()
            self.s_copy(k, 1).start()
            if k + self.ahead < self.chunks:
                self.z_start(k + self.ahead)
        if 0 <= k - 1 < self.chunks:
            self.s_copy(k - 1, 0).wait_recv()
            self.s_copy(k - 1, 2).start()
            self.s_copy(k - 1, 1).wait_recv()
            self.s_copy(k - 1, 3).start()
        if 0 <= k - 2 < self.chunks:
            self.s_copy(k - 2, 2).wait_recv()
            self.s_copy(k - 2, 3).wait_recv()
            self.s_copy(k - 2, 4).start()

    def arrived(self, g):
        for k in range(self.parts_of_group * g, self.parts_of_group * (g + 1)):
            self.s_copy(k, 4).wait_recv()

    def sent(self):
        for k in range(self.chunks):
            for step in range(1, self.parts):
                self.z_copy(k, step).wait_send()
            for n in range(5):
                self.s_copy(k, n).wait_send()


C_RING = 4
KEEP = 4
Z_RING = 6
TICKS = 16


class Scatter:
    def __init__(self, bufs, sems, credit):
        (
            self.c_in, self.a_in, self.b_in, self.z_in,
            self.a_out, self.a_keep, self.b_out, self.b_keep, self.z_out, self.total,
        ) = bufs
        self.sems, self.credit = sems, credit
        self.parts = 4
        self.share = self.z_out.shape[1]
        self.place = places()

    def block(self, t):
        if t < 6:
            return 3 - t % 2, 1 + t // 2
        if t < 14:
            return 1 - (t - 6) // 4, (t - 5) % 4
        return 17 - t, 0

    def copy(self, k, t, src, dst, who):
        return remote(src, dst, self.sems.at[0, k, t], self.sems.at[1, k, t], who)

    def c_copy(self, t, src):
        z, d_core = self.place[1], self.place[5]
        return self.copy(0, t, src, self.c_in.at[t % C_RING], (d_core, z))

    def a_copy(self, t, q):
        _, z, *_, d_x, d_y = self.place
        src, dst = self.a_out.at[t % 2, q], self.a_in.at[t, q]
        return self.copy(1 + q, t, src, dst, ((d_x, d_y)[q], z))

    def b_copy(self, t, q):
        _, z, *_, d_x, d_y = self.place
        src, dst = self.b_out.at[t % 2, q], self.b_in.at[t, q]
        return self.copy(3 + q, t, src, dst, ((d_y, d_x)[q], z))

    def z_copy(self, t):
        d, z = self.place[:2]
        who = (d, lax.rem(z + self.block(t)[1], self.parts))
        return self.copy(5, t, self.z_out.at[t % Z_RING], self.z_in.at[t], who)

    def rows(self, q):
        return pl.ds(q * (self.share // 2), self.share // 2)

    def c_start(self, t, src):
        if t >= C_RING:
            pl.semaphore_wait(self.credit, 1)
        self.c_copy(t, src).start()

    def a_start(self, t, mine, src):
        _, z, _, x, y, d_core, *_ = self.place
        slot, ring, held = t % 2, t % C_RING, t % KEEP
        if t >= 2:
            self.a_copy(t - 2, 0).wait_send()
            self.a_copy(t - 2, 1).wait_send()
        self.c_copy(t, src).wait_recv()
        for q in range(2):
            rows = self.rows(q)
            for k in range(2):
                send = (2 * k + 1 - x, 2 * (1 - y) + k)[q]
                self.a_out[slot, q, k] = low(
                    mine[send, rows].astype(F32) + self.c_in[ring, send, rows].astype(F32)
                )
            self.a_copy(t, q).start()
        for q in range(2):
            rows = self.rows(q)
            for k in range(2):
                keep = (2 * k + x, 2 * y + k)[q]
                self.a_keep[held, q, k] = low(
                    mine[keep, rows].astype(F32) + self.c_in[ring, keep, rows].astype(F32)
                )
        if t < TICKS - C_RING:
            pl.semaphore_signal(
                self.credit, inc=1, device_id=(d_core, z), device_id_type=MESH_ID
            )

    def b_start(self, t):
        _, _, _, x, y, *_ = self.place
        slot, held = t % 2, t % KEEP
        if t >= 2:
            self.b_copy(t - 2, 0).wait_send()
            self.b_copy(t - 2, 1).wait_send()
        for q in range(2):
            keep = (y, x)[q]
            send = 1 - keep
            self.a_copy(t, q).wait_recv()
            self.b_out[slot, q] = low(
                self.a_keep[held, q, send].astype(F32) + self.a_in[t, q, send].astype(F32)
            )
            self.b_copy(t, q).start()
            self.b_keep[held, q] = self.a_keep[held, q, keep].astype(F32) + self.a_in[
                t, q, keep
            ].astype(F32)

    def z_start(self, t):
        slot, held = t % Z_RING, t % KEEP
        g, r = self.block(t)
        if t >= Z_RING and self.block(t - Z_RING)[1] > 0:
            self.z_copy(t - Z_RING).wait_send()
        for q in range(2):
            self.b_copy(t, q).wait_recv()
            done = self.b_keep[held, q] + self.b_in[t, q].astype(F32)
            if r == 0:
                self.total[g, self.rows(q)] = done
            else:
                self.z_out[slot, self.rows(q)] = low(done)
        if r > 0:
            self.z_copy(t).start()

    def finish(self):
        for t in range(TICKS - 2, TICKS):
            for q in range(2):
                self.a_copy(t, q).wait_send()
                self.b_copy(t, q).wait_send()
        for t in range(TICKS):
            g, r = self.block(t)
            if r > 0:
                if t >= TICKS - Z_RING:
                    self.z_copy(t).wait_send()
                self.z_copy(t).wait_recv()
                self.total[g] += self.z_in[t].astype(F32)


class Sum:
    def __init__(self, near, far, send, recv):
        self.near, self.far = near, far
        self.send, self.recv = send, recv
        self.place = places()
        self.lo = lax.rem(self.place[0], 8)

    def near_copy(self, k):
        ref = self.near.at[self.lo]
        return remote(
            ref, ref, self.send.at[k - 1], self.recv.at[k - 1], (peer(k), self.place[1])
        )

    def far_copy(self, k):
        d, z = self.place[:2]
        ref = self.far.at[z]
        who = (d, lax.rem(z + k, self.far.shape[0]))
        return remote(ref, ref, self.send.at[6 + k], self.recv.at[6 + k], who)

    def start(self, value):
        self.near[self.lo] = value
        for k in range(1, 8):
            self.near_copy(k).start()

    def turn(self):
        for k in range(1, 8):
            self.near_copy(k).wait_send()
            sender = lax.rem(self.lo + 8 - k, 8)
            ref = self.near.at[sender]
            remote(
                ref, ref, self.send.at[k - 1], self.recv.at[k - 1], (peer(8 - k), self.place[1])
            ).wait_recv()
        value = self.near[0]
        for k in range(1, 8):
            value = value + self.near[k]
        self.far[self.place[1]] = value
        for k in range(1, self.far.shape[0]):
            self.far_copy(k).start()

    def result(self):
        d, z = self.place[:2]
        parts = self.far.shape[0]
        for k in range(1, parts):
            self.far_copy(k).wait_send()
            sender = lax.rem(z + parts - k, parts)
            ref = self.far.at[sender]
            remote(
                ref, ref, self.send.at[6 + k], self.recv.at[6 + k], (d, sender)
            ).wait_recv()
        value = self.far[0]
        for k in range(1, parts):
            value = value + self.far[k]
        return value


def forward_kernel(
    halves,
    len_ref, x_ref, enc_own, gain1, gain2, gain3, buckets_ref, table_in,
    sk, sv, sq, so, ck, cv, cq, co, fi, fo,
    result_ref, w_hbm, xa_out, enc_out, onehot_out,
    n1_out, q1_out, kv1_out, p1_out, o1_out, l1_out, x1_out,
    n2_out, q2_out, kv2_out, p2_out, o2_out, l2_out, x2_out,
    n3_out, hid_out, slope_out,
    w, enc, diag, mask, s_buf,
    n1, q1, kv1, p_buf, o1, x1, n2, q2, kv2, o2, x2, n3, hid, slope, l1, l2,
    acc, xa, table_own, table_far,
    w_sem, in_sem, own_sem, out_sem, p_sem,
    z_send, z_recv, s_send, s_recv, e_send, e_recv,
):
    rows, width = x_ref.shape
    parts = w.shape[1]
    half = half_of_sequence(halves)
    d, z_me = places()[:2]
    mate = z_me + 1 - 2 * half
    entered = greet(parts, False)

    def fetch(g, r):
        return pltpu.make_async_copy(w_hbm.at[g, r], w.at[g, r], w_sem.at[g, r])

    enc_here = pltpu.make_async_copy(enc_own, enc.at[half], in_sem.at[4])

    def own(g):
        if g == 2:
            return [pltpu.make_async_copy(fi, w.at[2, 0], in_sem.at[2])]
        if g == 3:
            return [pltpu.make_async_copy(fo, w.at[3, 0], in_sem.at[3])]
        refs = ((sk, sv, sq, so), (ck, cv, cq, co))[g]
        return [
            pltpu.make_async_copy(ref, w.at[g, 0, k], own_sem.at[g, k])
            for k, ref in enumerate(refs)
        ]

    for g in range(4):
        for copy in own(g):
            copy.start()
    enc_here.start()

    saves = []

    def saving(k):
        src, dst = saves[k]()
        return pltpu.make_async_copy(src, dst, out_sem.at[k])

    def save(src, dst):
        saves.append((lambda: (src, dst)) if not callable(src) else lambda: (src(), dst()))
        saving(len(saves) - 1).start()

    def pack(g):
        for copy in own(g):
            copy.wait()
        save(lambda: w.at[g, 0], lambda: w_hbm.at[g, 0])

    pack(0)
    entered()
    gather = Gather(w, w_hbm, z_send, z_recv, s_send, s_recv)
    x_copy = remote(x_ref, xa, e_send.at[0], e_recv.at[0], (d, mate))
    enc_copy = remote(enc_own, enc.at[half], e_send.at[1], e_recv.at[1], (d, mate))
    tables = [
        remote(
            table_own, table_far.at[parts - step], e_send.at[1 + step], e_recv.at[1 + step],
            (d, lax.rem(z_me + step, parts)),
        )
        for step in range(1, parts)
    ]
    gather.z_start(0)
    gather.z_start(1)

    @pl.when(half == 0)
    def _():
        x_copy.start()

    gather.z_start(2)
    table_own[...] = jnp.zeros_like(table_own)
    table_own[0 : table_in.shape[0], 0 : table_in.shape[1]] = table_in[...]
    for copy in tables:
        copy.start()
    pack(1)
    pack(2)
    pack(3)
    for k in range(3, gather.ahead):
        gather.z_start(k)

    n1[rows : 2 * rows, :] = low(norm_rows(x_ref[...].astype(F32), line_of(gain1))[0])
    gather.tick(0)

    slots = buckets_ref.shape[0]
    span = onehot_out.shape[1]
    here = jnp.concatenate(
        [line_of(buckets_ref), jnp.full((1, span - slots), -1, jnp.int32)], axis=1
    )
    kinds = onehot_out.shape[0]
    which = lax.broadcasted_iota(jnp.int32, (kinds, span), 0) == here
    plain = jnp.where(which, 1.0, 0.0).astype(BF16)
    for start in range(0, span, 128):
        offset = lax.broadcasted_iota(jnp.int32, (span, 128), 0)
        column = lax.broadcasted_iota(jnp.int32, (span, 128), 1) + start
        turn = (offset + column == rows) | (offset + column == rows + span)
        onehot_out[:, start : start + 128] = mm(plain, jnp.where(turn, 1.0, 0.0).astype(BF16))

    length = len_ref[lax.div(z_me, halves)]
    i = lax.broadcasted_iota(jnp.int32, mask.shape, 0)
    c = lax.broadcasted_iota(jnp.int32, mask.shape, 1)
    own = c - rows
    limit = jnp.where(half > 0, length, 0)
    ok = ((own < 0) & (c < limit)) | ((own >= 0) & (own <= i) & (own + half * rows < length))
    mask[...] = jnp.where(ok, 0.0, MASKED)
    gather.tick(1)
    enc_copy.start()
    for copy in tables:
        copy.wait()
    for r in range(parts):
        table = table_own[...] if r == 0 else table_far[r]
        diag[r] = jnp.dot(
            table[:, 0 : onehot_out.shape[0]],
            onehot_out[...],
            precision=lax.Precision.HIGHEST,
            preferred_element_type=F32,
        )

    @pl.when(half == 0)
    def _():
        x_copy.wait_send()
        xa[...] = x_ref[...]

    @pl.when(half == 1)
    def _():
        x_copy.wait_recv()

    n1[0:rows, :] = low(norm_rows(xa[...].astype(F32), line_of(gain1))[0])
    save(n1, n1_out)
    save(xa, xa_out)

    def take(g):
        gather.arrived(g)
        for r in range(1, parts):
            fetch(g, r).start()

    def ready(g, r):
        @pl.when(r > 0)
        def _():
            fetch(g, r).wait()

    def after(r, **hooks):
        for name, hook in hooks.items():
            pl.when(r == int(name[1:]))(hook)

    p_outs = (p1_out, p2_out)
    p_keys = (2 * rows, 2 * enc.shape[1])

    def p_save(phase, r):
        slot = lax.rem(r, 2)
        return pltpu.make_async_copy(
            p_buf.at[slot, :, :, 0 : p_keys[phase]],
            p_outs[phase].at[pl.ds(3 * r, 3)],
            p_sem.at[phase, slot],
        )

    def heads(phase, r, q, kv, o, l):
        keys = p_keys[phase]
        slot = lax.rem(r, 2)

        @pl.when(r >= 2)
        def _():
            p_save(phase, r - 2).wait()

        if phase == 1:

            @pl.when(r < 2)
            def _():
                p_save(0, r + 2).wait()

        outs = []
        for j in range(3):
            q_h = q[r, :, DH * j : DH * (j + 1)]
            k_h = kv[r, :, DH * j : DH * (j + 1)]
            v_h = kv[r, :, DH * (3 + j) : DH * (4 + j)]
            s_buf[j % 2, :, 0:keys] = mm_nt(q_h, k_h)
            for a, n in chunks(rows, 32):
                s = s_buf[j % 2, a : a + n, 0:keys]
                if phase == 0:
                    line = jnp.broadcast_to(diag[r, j : j + 1, :], (n, diag.shape[2]))
                    grid = pltpu.roll(line, a, 1, stride=1, stride_axis=0)
                    s = s + grid[:, 0:keys] + mask[a : a + n, :]
                top = jnp.max(s, axis=1, keepdims=True)
                p_buf[slot, j, a : a + n, 0:keys] = low(jnp.exp(s - top))
            wide = jnp.concatenate([v_h, jnp.ones_like(v_h)], axis=1)
            mixed = mm(p_buf[slot, j, :, 0:keys], wide)
            outs.append(low(mixed[:, 0:DH] / mixed[:, DH : 2 * DH]))
            l[r, :, 32 * j : 32 * (j + 1)] = mixed[:, DH : DH + 32]
        o[r] = jnp.concatenate(outs, axis=1)
        p_save(phase, r).start()

    acc[...] = x_ref[...].astype(F32)

    def self_step(r, carry):
        ready(0, r)
        kv1[r] = low(mm_nt(n1[...], block(w, 0, r, 0, 384)))
        q1[r] = low(mm_nt(n1[rows : 2 * rows, :], block(w, 0, r, 384, 576)))
        heads(0, r, q1, kv1, o1, l1)
        acc[...] += mm(o1[r], block(w, 0, r, 576, 768))

        def first():
            for k in (2, 3, 4):
                gather.tick(k)
            take(0)

        after(r, r0=first, r1=lambda: gather.tick(5), r2=lambda: gather.tick(6), r3=lambda: gather.tick(7))
        return carry

    lax.fori_loop(0, parts, self_step, 0)
    for src, dst in ((q1, q1_out), (kv1, kv1_out), (o1, o1_out), (l1, l1_out)):
        save(src, dst)
    x1[...] = acc[...]
    n2[...] = low(norm_rows(acc[...], line_of(gain2))[0])
    save(x1, x1_out)
    save(n2, n2_out)
    enc_copy.wait()
    enc_here.wait()
    save(enc, enc_out)
    keys = 2 * enc.shape[1]

    def cross_step(r, carry):
        ready(1, r)
        kv2[r] = low(mm_nt(enc[...].reshape(keys, width), block(w, 1, r, 0, 384)))
        q2[r] = low(mm_nt(n2[...], block(w, 1, r, 384, 576)))
        heads(1, r, q2, kv2, o2, l2)
        acc[...] += mm(o2[r], block(w, 1, r, 576, 768))

        def first():
            gather.tick(8)
            take(1)

        after(r, r0=first, r1=lambda: gather.tick(9), r2=lambda: gather.tick(10), r3=lambda: gather.tick(11))
        return carry

    lax.fori_loop(0, parts, cross_step, 0)
    for src, dst in ((q2, q2_out), (kv2, kv2_out), (o2, o2_out), (l2, l2_out)):
        save(src, dst)
    x2[...] = acc[...]
    n3[...] = low(norm_rows(acc[...], line_of(gain3))[0])
    save(x2, x2_out)
    save(n3, n3_out)

    def inner_step(r, carry):
        ready(2, r)
        for a, n in chunks(rows, 64):
            v = mm(n3[a : a + n, :], block(w, 2, r))
            sq = v * v
            t = jnp.tanh(v * (ROOT + ROOT * CUBE * sq))
            cdf = 0.5 + 0.5 * t
            hid[r, a : a + n, :] = low(v * cdf)
            slope[r, a : a + n, :] = low(
                cdf + 0.5 * v * (1.0 - t * t) * (ROOT + 3.0 * ROOT * CUBE * sq)
            )
        after(r, r0=lambda: take(2), r1=lambda: gather.tick(12), r3=lambda: gather.tick(13))
        return carry

    lax.fori_loop(0, parts, inner_step, 0)
    save(hid, hid_out)
    save(slope, slope_out)

    def outer_step(r, carry):
        ready(3, r)
        acc[...] += mm(hid[r], block(w, 3, r))
        after(r, r0=lambda: take(3))
        return carry

    lax.fori_loop(0, parts, outer_step, 0)
    result_ref[...] = low(acc[...])
    for k in range(len(saves)):
        saving(k).wait()
    for r in (parts - 2, parts - 1):
        p_save(1, r).wait()
    gather.sent()


def backward_kernel(
    x_ref, xa_ref, cot_ref, gain1, gain2, gain3, onehot_ref, enc_hbm, w_hbm,
    n1_hbm, q1_hbm, kv1_hbm, p1_hbm, o1_hbm, l1_hbm, x1_hbm,
    n2_hbm, q2_hbm, kv2_hbm, p2_hbm, o2_hbm, l2_hbm, x2_hbm,
    n3_hbm, hid_hbm, slope_hbm,
    total_out, small_out, dx_out, denc_out, g_hbm,
    w, enc, nbuf, n2, q_in, kv_in, p_in, o_in, l_in, x_in, hid, slope,
    g_buf, l_buf, rows_t, rows_t2, keys_t, dp_buf, ds_buf, dkv_t, dn, acc, enc_acc, diag_acc,
    dxa, dxa_in, denc, denc_in, small,
    c_in, a_in, b_in, z_in, a_out, a_keep, b_out, b_keep, z_out, s_near, s_far,
    w_sem, one_sem, ring_sem, store_sem, load_sem,
    sems, credit, s_send, s_recv, e_send, e_recv,
):
    rows, width_all = x_ref.shape
    parts = w_hbm.shape[1]
    place = places()
    d, z_me, core = place[:3]
    half = lax.rem(z_me, 2)
    mate = z_me + 1 - 2 * half
    keys = 2 * enc.shape[1]
    own_keys = 2 * rows

    singles = [(n3_hbm, nbuf.at[0:rows]), (x2_hbm, x_in), (n2_hbm, n2), (enc_hbm, enc),
               (x1_hbm, x_in), (n1_hbm, nbuf)]

    def single(k):
        return pltpu.make_async_copy(*singles[k], one_sem.at[k])

    def which(i):
        return lax.rem(i + 1, parts)

    def streams(phase, i):
        slot, r = lax.rem(i, 2), which(i)
        if phase == 0:
            pairs = [(hid_hbm.at[r], hid.at[slot]), (slope_hbm.at[r], slope.at[slot])]
        else:
            q, kv, p, o, l = (
                (q2_hbm, kv2_hbm, p2_hbm, o2_hbm, l2_hbm),
                (q1_hbm, kv1_hbm, p1_hbm, o1_hbm, l1_hbm),
            )[phase - 1]
            n = (keys, own_keys)[phase - 1]
            pairs = [
                (q.at[r], q_in.at[slot]),
                (kv.at[r], kv_in.at[slot, 0:n]),
                (p.at[pl.ds(3 * r, 3)], p_in.at[slot, :, :, 0:n]),
                (o.at[r], o_in.at[slot]),
                (l.at[r], l_in.at[slot]),
            ]
        return [
            pltpu.make_async_copy(src, dst, ring_sem.at[k, slot])
            for k, (src, dst) in enumerate(pairs)
        ]

    def weight(g, i, k):
        slot = lax.rem(i, 2)
        return pltpu.make_async_copy(w_hbm.at[g, which(i)], w.at[slot, k], w_sem.at[slot, k])

    groups = ((3, 2), (1,), (0,))

    def prefetch(phase, r):
        for k, g in enumerate(groups[phase]):
            weight(g, r, k).start()
        for copy in streams(phase, r):
            copy.start()

    def turn(phase, r):
        for k, g in enumerate(groups[phase]):
            weight(g, r, k).wait()
        for copy in streams(phase, r):
            copy.wait()

        @pl.when(r + 1 < parts)
        def _():
            prefetch(phase, r + 1)

        if phase < 2:

            @pl.when(r + 1 == parts)
            def _():
                prefetch(phase + 1, 0)

    entered = greet(parts, True)
    prefetch(0, 0)
    for k in range(4):
        single(k).start()

    scatter = Scatter(
        (c_in, a_in, b_in, z_in, a_out, a_keep, b_out, b_keep, z_out, total_out), sems, credit
    )
    sums = Sum(s_near, s_far, s_send, s_recv)
    dxa_copy = remote(dxa, dxa_in, e_send.at[0], e_recv.at[0], (d, mate))
    denc_copy = remote(denc.at[1 - half], denc_in, e_send.at[1], e_recv.at[1], (d, mate))

    def put(t, value, start=0):
        shape = g_buf.shape[1:4] + (value.shape[1],)
        g_buf[lax.rem(t, 2), :, :, :, start : start + value.shape[1]] = value.reshape(shape)

    def store(t):
        slot = lax.rem(t, 2)
        return pltpu.make_async_copy(g_buf.at[slot], g_hbm.at[t], store_sem.at[slot])

    def away(t):
        return g_hbm.at[t, :, 1 - core]

    def load(t):
        slot = t % 2
        return pltpu.make_async_copy(g_hbm.at[t, :, core], l_buf.at[slot], load_sem.at[slot])

    def leave(t):
        if t < TICKS:
            scatter.c_start(t, away(t))
            load(t).start()
        if t >= 1:
            load(t - 1).wait()
            scatter.a_start(t - 1, l_buf.at[(t - 1) % 2], away(t - 1))

    def tick(t):
        leave(t)
        if t >= 3:
            scatter.b_start(t - 3)
        if t >= 5:
            scatter.z_start(t - 5)

    b, z = scatter.b_start, scatter.z_start

    def at(i, step, *moves):
        @pl.when(i == step)
        def _():
            for move, t in moves:
                move(t)

    def keep_sum(g, value):
        part = width_all // 2
        small[2 * g : 2 * g + 1, :] = value[:, 0:part]
        small[2 * g + 1 : 2 * g + 2, :] = value[:, part:]

    rows_t[...] = flip(cot_ref[...])
    single(0).wait()
    rows_t2[...] = flip(nbuf[0:rows, :])
    acc[...] = jnp.zeros_like(acc)

    def feed_step(i, carry):
        turn(0, i)
        slot = lax.rem(i, 2)
        t = 2 * i + 8 * lax.div(i, 3)
        put(t, low(mm(rows_t[...], hid[slot])))
        store(t).start()
        dh = low(mm_nt(cot_ref[...], block(w, slot, 0)))
        slope[slot] = low(dh.astype(F32) * slope[slot].astype(F32))
        store(t).wait()

        @pl.when(i == 0)
        def _():
            entered()
            tick(0)

        put(t + 1, low(mm(rows_t2[...], slope[slot])))
        store(t + 1).start()
        acc[...] += mm_nt(slope[slot], block(w, slot, 1))
        store(t + 1).wait()
        at(i, 1, (tick, 1))
        at(i, 2, (tick, 2))
        at(i, 3, (tick, 3))
        return carry

    lax.fori_loop(0, parts, feed_step, 0)
    single(1).wait()
    back, sum3 = norm_back(acc[...], x_in[...], line_of(gain3))
    dn[...] = cot_ref[...].astype(F32) + back
    single(4).start()
    single(5).start()
    small[...] = jnp.zeros_like(small)
    keep_sum(2, sum3)

    def heads_back(r, do, n, with_diag, between):
        slot = lax.rem(r, 2)
        q, kv, o = q_in[slot], kv_in.at[slot], o_in[slot].astype(F32)
        do_all = []
        delta_all = []
        for j in range(3):
            do_h = do[:, DH * j : DH * (j + 1)]
            inv = 1.0 / l_in[slot, :, 32 * j : 32 * j + 1]
            o_h = o[:, DH * j : DH * (j + 1)]
            delta_all.append(jnp.sum(do_h * o_h * inv, axis=1, keepdims=True))
            do_all.append(do_h * inv)
        do_t = low(jnp.transpose(jnp.concatenate(do_all, axis=1)))
        q_t = flip(q)
        dq = []
        for j in range(3):
            p_h = p_in.at[slot, j]
            k_h = kv[0:n, DH * j : DH * (j + 1)]
            v_h = kv[0:n, DH * (3 + j) : DH * (4 + j)]
            dp_buf[j % 2, :, 0:n] = mm_nt(low(do_all[j]), v_h)
            total = None
            for s, m in chunks(rows, 32):
                ds = low(
                    p_h[s : s + m, 0:n].astype(F32)
                    * (dp_buf[j % 2, s : s + m, 0:n] - delta_all[j][s : s + m, :])
                )
                ds_buf[j % 2, s : s + m, 0:n] = ds
                if with_diag:
                    width = diag_acc.shape[2]
                    wide = jnp.concatenate([ds.astype(F32), jnp.zeros((m, width - n), F32)], axis=1)
                    for b in range(0, m, 8):
                        turned = pltpu.roll(wide[b : b + 8, :], (width - s - b) % width, 1)
                        total = turned if total is None else total + turned
            if with_diag:
                diag_acc[which(r) * 3 + j] = total
            ds_h = ds_buf[j % 2, :, 0:n]
            dq.append(low(mm(ds_h, k_h)))
            dkv_t[DH * j : DH * (j + 1), 0:n] = mm(q_t[DH * j : DH * (j + 1), :], ds_h)
            dkv_t[DH * (3 + j) : DH * (4 + j), 0:n] = mm(
                do_t[DH * j : DH * (j + 1), :], p_h[:, 0:n]
            )
            if j == 1:
                between()
        return jnp.concatenate(dq, axis=1), low(jnp.transpose(dkv_t[:, 0:n]))

    def attention_step(phase, n, r, middle):
        slot = lax.rem(r, 2)
        t = 2 + 4 * phase + r
        turn(phase, r)
        do = low(mm_nt(low(dn[...]), block(w, slot, 0, 576, 768))).astype(F32)
        dq, dkv = heads_back(r, do, n, phase == 2, lambda: middle(r))
        put(t, low(mm(keys_t[:, 0:n], dkv)))
        both = [low(mm(rows_t2[...], dq)), low(mm(rows_t[...], o_in[slot]))]
        put(t, jnp.concatenate(both, axis=1), 384)
        store(t).start()
        acc[...] += mm(dq, block(w, slot, 0, 384, 576))
        enc_acc[0:n, :] += mm(dkv, block(w, slot, 0, 0, 384))
        store(t).wait()

    rows_t[...] = flip(low(dn[...]))
    single(2).wait()
    single(3).wait()
    rows_t2[...] = flip(n2[...])
    keys_t[...] = flip(enc[...].reshape(keys, width_all))
    acc[...] = jnp.zeros_like(acc)
    enc_acc[...] = jnp.zeros_like(enc_acc)

    def cross_step(r, carry):
        def middle(r):
            at(r, 0, (tick, 4))
            at(r, 3, (tick, 8))

        attention_step(1, keys, r, middle)
        at(r, 0, (tick, 5))
        at(r, 1, (tick, 6))
        at(r, 2, (tick, 7))
        at(r, 3, (tick, 9))
        return carry

    lax.fori_loop(0, parts, cross_step, 0)
    denc[...] = low(enc_acc[...]).reshape(denc.shape)
    denc_copy.start()
    single(4).wait()
    back, sum2 = norm_back(acc[...], x_in[...], line_of(gain2))
    dn[...] += back
    keep_sum(1, sum2)

    rows_t[...] = flip(low(dn[...]))
    single(5).wait()
    rows_t2[...] = flip(nbuf[rows : 2 * rows, :])
    keys_t[:, 0:own_keys] = flip(nbuf[...])
    acc[...] = jnp.zeros_like(acc)
    enc_acc[0:own_keys, :] = jnp.zeros((own_keys, width_all), F32)

    def self_step(r, carry):
        def middle(r):
            at(r, 1, (b, 8), (z, 6))
            at(r, 2, (z, 8))

        attention_step(2, own_keys, r, middle)
        at(r, 0, (tick, 10))
        at(r, 1, (leave, 11), (b, 9), (z, 7))
        at(r, 2, (leave, 12), (b, 10), (z, 9))
        at(r, 3, (leave, 13), (b, 11), (z, 10))
        return carry

    lax.fori_loop(0, parts, self_step, 0)
    gain = line_of(gain1)
    back, sum1a = norm_back(enc_acc[0:rows, :], xa_ref[...].astype(F32), gain)
    dxa[...] = low(back)

    @pl.when(half == 1)
    def _():
        dxa_copy.start()

    leave(14)
    b(12)
    z(11)
    back, sum1 = norm_back(
        acc[...] + enc_acc[rows : 2 * rows, :], x_ref[...].astype(F32), gain
    )
    dn[...] += back
    keep_sum(0, sum1 + sum1a)
    width = diag_acc.shape[2]
    lines = []
    for r in range(parts):
        for j in range(3):
            part = diag_acc[3 * r + j]
            line = part[0:1, :]
            for k in range(1, 8):
                line = line + pltpu.roll(part[k : k + 1, :], width - k, 1)
            lines.append(line)
    lines.append(jnp.zeros((16 - len(lines), width), F32))
    table = lax.dot_general(
        jnp.concatenate(lines, axis=0),
        onehot_ref[...],
        (((1,), (1,)), ((), ())),
        precision=lax.Precision.HIGHEST,
        preferred_element_type=F32,
    )
    kinds = onehot_ref.shape[0]
    for r in range(parts):
        at = lax.rem(z_me + r, parts)
        for p in range(parts):

            @pl.when(at == p)
            def _(r=r, p=p):
                for j in range(3):
                    lane = kinds * (3 * p + j)
                    small[6:7, lane : lane + kinds] = table[3 * r + j : 3 * r + j + 1]

    leave(15)
    b(13)
    z(12)
    sums.start(small[...])
    leave(16)
    b(14)
    z(13)
    sums.turn()
    b(15)
    z(14)
    z(15)
    denc_copy.wait()
    denc_out[...] = low(denc[half].astype(F32) + denc_in[...].astype(F32))
    scatter.finish()
    small_out[...] = sums.result()

    @pl.when(half == 1)
    def _():
        dxa_copy.wait_send()
        dx_out[...] = low(dn[...])

    @pl.when(half == 0)
    def _():
        dxa_copy.wait_recv()
        dx_out[...] = low(dn[...] + dxa_in[...].astype(F32))

    for t in range(TICKS):
        scatter.c_copy(t, away(t)).wait_send()


def finish_kernel(
    result_in, dx, denc, total, small,
    result, input_grad, encoder_grad,
    g_gain1, gsq, gsk, gsv, gso, g_gain2, gcq, gck, gcv, gco, g_gain3, gfi, gfo, lines,
):
    result[...] = result_in[...]
    input_grad[...] = dx[...]
    encoder_grad[...] = denc[...]
    width = result.shape[1]
    for g, (k, v, q, o) in enumerate(((gsk, gsv, gsq, gso), (gck, gcv, gcq, gco))):
        k[...] = total[g, :, 0:192]
        v[...] = total[g, :, 192:384]
        q[...] = total[g, :, 384:576]
        o[...] = jnp.transpose(total[g, :, 576:768])
    gfi[...] = total[2]
    gfo[...] = total[3]
    for row, gain in enumerate((g_gain1, g_gain2, g_gain3)):
        part = small[2 * row : 2 * row + 2, :]
        gain[...] = jnp.concatenate([part[0:1], part[1:2]], axis=1).reshape(width)
    z = lax.axis_index("mp")
    for p in range(4):

        @pl.when(z == p)
        def _(p=p):
            kinds = lines.shape[1]
            for j in range(3):
                lane = kinds * (3 * p + j)
                lines[j : j + 1, :] = small[6:7, lane : lane + kinds]


def across(value, axis, n_dp):
    groups = n_dp // 8
    whole = lax.all_gather(value, "dp", axis=0, tiled=False)
    whole = whole.reshape(groups, 8, *value.shape).sum(0)
    whole = jnp.concatenate([whole[k] for k in range(8)], axis=axis)
    share = whole.shape[axis] // n_dp
    return lax.dynamic_slice_in_dim(whole, lax.axis_index("dp") * share, share, axis)


def across_small(value, n_dp):
    whole = lax.all_gather(value, "dp", axis=0, tiled=False)
    return whole.reshape(n_dp // 8, 8, *value.shape)[:, 0].sum(0)


def body(
    inputs, encoded, cotangent, lengths, buckets,
    self_gain, self_query, self_key, self_value, self_output, bias_table,
    cross_gain, cross_query, cross_key, cross_value, cross_output,
    feed_gain, feed_inner, feed_output_weight,
):
    rows, width = inputs.shape
    parts = lax.axis_size("mp")
    n_dp = lax.axis_size("dp")
    halves = parts // lengths.shape[0]
    assert halves == 2 and buckets.shape[0] == 2 * rows and parts == 4
    z = lax.axis_index("mp")
    enc_rows = encoded.shape[0]
    vmem = pl.BlockSpec(memory_space=pltpu.VMEM)
    smem = pl.BlockSpec(memory_space=pltpu.SMEM)
    hbm = pl.BlockSpec(memory_space=pl.ANY)
    sds = jax.ShapeDtypeStruct

    share = width // 8
    diag = 1024
    heads = 3 * parts
    keys = 2 * enc_rows
    gains = [self_gain, cross_gain, feed_gain]
    split = lambda v: v.reshape(2, share, width)
    whole = lambda v: v.reshape(4, 2, share, width)
    kinds = bias_table.shape[0]
    saved = [
        ((2 * rows, width), BF16),
        ((parts, rows, 192), BF16),
        ((parts, 2 * rows, 384), BF16),
        ((heads, rows, 2 * rows), BF16),
        ((parts, rows, 192), BF16),
        ((parts, rows, 128), F32),
        ((rows, width), F32),
        ((rows, width), BF16),
        ((parts, rows, 192), BF16),
        ((parts, keys, 384), BF16),
        ((heads, rows, keys), BF16),
        ((parts, rows, 192), BF16),
        ((parts, rows, 128), F32),
        ((rows, width), F32),
        ((rows, width), BF16),
        ((parts, rows, width), BF16),
        ((parts, rows, width), BF16),
    ]
    n1s, q1s, kv1s, p1s, o1s, l1s, x1s, n2s, q2s, kv2s, p2s, o2s, l2s, x2s, n3s, hids, slopes = [
        pltpu.VMEM(*s) for s in saved
    ]
    result, weights, other, enc_all, onehot, *kept = pl.pallas_call(
        functools.partial(forward_kernel, halves),
        out_shape=[
            sds((rows, width), BF16),
            sds((4, parts, 4, 2, share, width), BF16),
            sds((rows, width), BF16),
            sds((2, enc_rows, width), BF16),
            sds((kinds, diag), F32),
        ]
        + [sds(*s) for s in saved],
        in_specs=[smem, vmem, hbm] + [vmem] * 5 + [hbm] * 10,
        out_specs=[vmem, hbm, hbm, hbm, vmem] + [hbm] * len(saved),
        scratch_shapes=[
            pltpu.VMEM((4, parts, 4, 2, share, width), BF16),
            pltpu.VMEM((2, enc_rows, width), BF16),
            pltpu.VMEM((parts, 8, diag), F32),
            pltpu.VMEM((rows, 2 * rows), F32),
            pltpu.VMEM((2, rows, keys), F32),
            n1s, q1s, kv1s, pltpu.VMEM((2, 3, rows, keys), BF16), o1s, x1s,
            n2s, q2s, kv2s, o2s, x2s, n3s, hids, slopes,
            l1s, l2s,
            pltpu.VMEM((rows, width), F32),
            pltpu.VMEM((rows, width), BF16),
            pltpu.VMEM((8, 128), F32),
            pltpu.VMEM((parts, 8, 128), F32),
            pltpu.SemaphoreType.DMA((4, parts)),
            pltpu.SemaphoreType.DMA((5,)),
            pltpu.SemaphoreType.DMA((2, 4)),
            pltpu.SemaphoreType.DMA((6 + len(saved),)),
            pltpu.SemaphoreType.DMA((2, 2)),
            pltpu.SemaphoreType.DMA((Gather.chunks, parts - 1)),
            pltpu.SemaphoreType.DMA((Gather.chunks, parts - 1)),
            pltpu.SemaphoreType.DMA((Gather.chunks, 5)),
            pltpu.SemaphoreType.DMA((Gather.chunks, 5)),
            pltpu.SemaphoreType.DMA((5,)),
            pltpu.SemaphoreType.DMA((5,)),
        ],
        compiler_params=pltpu.CompilerParams(
            collective_id=1, has_side_effects=True, vmem_limit_bytes=VMEM_BYTES
        ),
        name="forward",
    )(
        lengths, inputs, encoded, *gains, buckets, bias_table.T,
        split(self_key.T), split(self_value.T), split(self_query.T), split(self_output),
        split(cross_key.T), split(cross_value.T), split(cross_query.T), split(cross_output),
        whole(feed_inner), whole(feed_output_weight),
    )

    half_share = share // 2
    summed, small, input_grad, encoder_grad, _ = pl.pallas_call(
        backward_kernel,
        out_shape=[
            sds((4, share, width), F32),
            sds((8, width // 2), F32),
            sds((rows, width), BF16),
            sds((enc_rows, width), BF16),
            sds((TICKS, 4, 2, share, width), BF16),
        ],
        in_specs=[vmem] * 7 + [hbm] * 19,
        out_specs=[vmem] * 4 + [hbm],
        scratch_shapes=[
            pltpu.VMEM((2, 2, 4, 2, share, width), BF16),
            pltpu.VMEM((2, enc_rows, width), BF16),
            pltpu.VMEM((2 * rows, width), BF16),
            pltpu.VMEM((rows, width), BF16),
            pltpu.VMEM((2, rows, 192), BF16),
            pltpu.VMEM((2, keys, 384), BF16),
            pltpu.VMEM((2, 3, rows, keys), BF16),
            pltpu.VMEM((2, rows, 192), BF16),
            pltpu.VMEM((2, rows, 128), F32),
            pltpu.VMEM((rows, width), F32),
            pltpu.VMEM((2, rows, width), BF16),
            pltpu.VMEM((2, rows, width), BF16),
            pltpu.VMEM((2, 4, 2, share, width), BF16),
            pltpu.VMEM((2, 4, share, width), BF16),
            pltpu.VMEM((width, rows), BF16),
            pltpu.VMEM((width, rows), BF16),
            pltpu.VMEM((width, keys), BF16),
            pltpu.VMEM((2, rows, keys), F32),
            pltpu.VMEM((2, rows, keys), BF16),
            pltpu.VMEM((384, keys), F32),
            pltpu.VMEM((rows, width), F32),
            pltpu.VMEM((rows, width), F32),
            pltpu.VMEM((keys, width), F32),
            pltpu.VMEM((heads, 8, diag), F32),
            pltpu.VMEM((rows, width), BF16),
            pltpu.VMEM((rows, width), BF16),
            pltpu.VMEM((2, enc_rows, width), BF16),
            pltpu.VMEM((enc_rows, width), BF16),
            pltpu.VMEM((8, width // 2), F32),
            pltpu.VMEM((C_RING, 4, share, width), BF16),
            pltpu.VMEM((TICKS, 2, 2, half_share, width), BF16),
            pltpu.VMEM((TICKS, 2, half_share, width), BF16),
            pltpu.VMEM((TICKS, share, width), BF16),
            pltpu.VMEM((2, 2, 2, half_share, width), BF16),
            pltpu.VMEM((KEEP, 2, 2, half_share, width), BF16),
            pltpu.VMEM((2, 2, half_share, width), BF16),
            pltpu.VMEM((KEEP, 2, half_share, width), F32),
            pltpu.VMEM((Z_RING, share, width), BF16),
            pltpu.VMEM((8, 8, width // 2), F32),
            pltpu.VMEM((parts, 8, width // 2), F32),
            pltpu.SemaphoreType.DMA((2, 2)),
            pltpu.SemaphoreType.DMA((6,)),
            pltpu.SemaphoreType.DMA((5, 2)),
            pltpu.SemaphoreType.DMA((2,)),
            pltpu.SemaphoreType.DMA((2,)),
            pltpu.SemaphoreType.DMA((2, 6, TICKS)),
            pltpu.SemaphoreType.REGULAR,
            pltpu.SemaphoreType.DMA((10,)),
            pltpu.SemaphoreType.DMA((10,)),
            pltpu.SemaphoreType.DMA((2,)),
            pltpu.SemaphoreType.DMA((2,)),
        ],
        compiler_params=pltpu.CompilerParams(
            collective_id=2, has_side_effects=True, vmem_limit_bytes=VMEM_BYTES
        ),
        name="backward",
    )(inputs, other, cotangent, *gains, onehot, enc_all, weights, *kept)

    f32 = lambda *shape: sds(shape, F32)
    outs = pl.pallas_call(
        finish_kernel,
        out_shape=[
            sds((rows, width), BF16), sds((rows, width), BF16), sds((enc_rows, width), BF16),
            f32(width), f32(share, 192), f32(share, 192), f32(share, 192), f32(192, share),
            f32(width), f32(share, 192), f32(share, 192), f32(share, 192), f32(192, share),
            f32(width), f32(share, width), f32(share, width), f32(3, kinds),
        ],
        in_specs=[vmem] * 5,
        out_specs=[vmem] * 17,
        name="finish",
    )(result, input_grad, encoder_grad, summed, small)
    result, input_grad, encoder_grad, *grads, lines = outs
    if n_dp > 8:
        axes = (None, 0, 0, 0, 1, None, 0, 0, 0, 1, None, 0, 0)
        grads = [
            across_small(value, n_dp) if axis is None else across(value, axis, n_dp)
            for value, axis in zip(grads, axes)
        ]
        lines = across_small(lines, n_dp)
    return (result, input_grad, encoder_grad, *grads[0:5], lines.T, *grads[5:-1], grads[-1].T)


def solution(mesh):
    rows = P(("dp", "mp"), None)
    across, down = P(None, "mp"), P("mp", None)
    return jax.shard_map(
        body,
        mesh=mesh,
        in_specs=(
            rows, rows, rows, P("dp"), P(),
            P(), across, across, across, down, across,
            P(), across, across, across, down,
            P(), across, down,
        ),
        out_specs=(
            rows, rows, rows,
            P(), P("dp", "mp"), P("dp", "mp"), P("dp", "mp"), P("mp", "dp"), P(None, "mp"),
            P(), P("dp", "mp"), P("dp", "mp"), P("dp", "mp"), P("mp", "dp"),
            P(), P("dp", "mp"), P("mp", "dp"),
        ),
        check_vma=False,
    )
```

time: 259 us -> 217 us (0.84)
  local copies, waits for them, and re-layouts: 19.6 us -> 0 us
  Pallas kernels: 230 us -> 216 us
  other arithmetic: 8.13 us -> 0 us
    pallas_call x1, Pallas kernels: 111 us -> 100 us  [body(): pl.pallas_call(functools.partial(forward_kernel, halves), out_shape=[sds(...]
    pallas_call x1, Pallas kernels: 119 us -> 112 us  [body(): pl.pallas_call(backward_kernel, out_shape=[sds((4, share, width), F32), s...]
    transpose x3 -> x0, local copies, waits for them, and re-layouts: 4.61 us -> none  [the longest x1 2.17 us: body(): summed[3]]
    unnamed x23 -> x0, local copies, waits for them, and re-layouts: 4.29 us -> none
    another operation x2 -> x0, other arithmetic: 4.11 us -> none  [the longest x1 3.52 us: body(): jnp.stack([jnp.concatenate([self_key, self_value, self_query, self_output...]
    pallas_call x0 -> x1, Pallas kernels: none -> 3.92 us  [body(): pl.pallas_call(finish_kernel, out_shape=[sds((rows, width), BF16), sds((r...]
    concatenate x4 -> x0, other arithmetic: 3.17 us -> none  [the longest x1 2.33 us: body(): jnp.concatenate([self_key, self_value, self_query, self_output.T], axis=1)]
    slice x3 -> x0, local copies, waits for them, and re-layouts: 2.93 us -> none  [the longest x1 1.48 us: body(): small[2, :width]]
where the time goes in v4:
time: 217 us
  Pallas kernels  216 us (100%)
    pallas_call x1, Pallas kernels, body(): pl.pallas_call(backward_kernel, out_shape=[sds((4, share, width), F32), s...  112 us
    pallas_call x1, Pallas kernels, body(): pl.pallas_call(functools.partial(forward_kernel, halves), out_shape=[sds(...  100 us

profile of v4, /device:TPU:0, one launch (start us, length us, event | category | flops | bytes accessed | tf_op | source)
XLA Modules:
  0.0 217.2 jit_solution(17245631145267635236)
XLA Ops:
  0.7 100.3 %forward.1 = (bf16[320,768]{1,0:T(8,128)(2,1)}, bf16[4,4,4,2,96,768]{5,4,3,2,1,0:T(8,128)(2,1)}, bf16[320,768]{1,0:T(8,128)(2,1)}, bf16[2,512,768]{2,1,0:T(8,128...) custom-call(s32[2]{0:T(128)} %len_ref.1, ...), custom_call_target="tpu_custom_call" | custom-call | tf_op jit(solution)/shard_map/forward/pallas_call | solution.py:1098
  101.0 112.2 %backward.1 = (f32[4,96,768]{2,1,0:T(8,128)}, f32[8,384]{1,0:T(8,128)}, bf16[320,768]{1,0:T(8,128)(2,1)}, bf16[512,768]{1,0:T(8,128)(2,1)}, bf16[16,4,2,96,768]{4,3,2,1,0:T(8,128)(2,1)}) custom-call(bf16[320,768]{1,0:T(8,128)(2,1)} %x_ref.3, bf16[320,768]{1,0:T(8,128)(2,1)} %get-tuple-element.61.xa_ref, bf16[320,768]{1,0:T(8,128)(2,1)} %cot_ref.1, ...), custom_call_target="tpu_custom_call" | custom-call | tf_op jit(solution)/shard_map/backward/pallas_call | solution.py:1147
  213.2 3.9 %finish.1 = (bf16[320,768]{1,0:T(8,128)(2,1)}, bf16[320,768]{1,0:T(8,128)(2,1)}, bf16[512,768]{1,0:T(8,128)(2,1)}, f32[768]{0:T(1024)}, f32[96,192]{1,0:T(8,128)...) custom-call(bf16[320,768]{1,0:T(8,128)(2,1)} %get-tuple-element.60.r, ...), custom_call_target="tpu_custom_call" | custom-call | tf_op jit(solution)/shard_map/finish/pallas_call | solution.py:1218

commit v5 on v4

v5 whole, which is shorter than its diff:
```python
import functools

import jax
import jax.numpy as jnp
from jax import lax
from jax.experimental import pallas as pl
from jax.experimental.pallas import tpu as pltpu
from jax.sharding import PartitionSpec as P

EPS = 1e-06
MASKED = -1e30
DH = 64
F32 = jnp.float32
BF16 = jnp.bfloat16
VMEM_BYTES = 62 << 20
ROOT = 0.7978845608028654
CUBE = 0.044715


def mm(a, b):
    return jnp.dot(a, b, preferred_element_type=F32)


def mm_nt(a, b):
    return lax.dot_general(a, b, (((1,), (1,)), ((), ())), preferred_element_type=F32)


def line_of(ref):
    return ref[...].reshape(1, ref.shape[0])


def low(v):
    return v.astype(BF16)


def flip(v):
    return jnp.transpose(v.astype(F32)).astype(BF16)


def norm_rows(v, gain):
    root = lax.rsqrt(jnp.mean(v * v, axis=-1, keepdims=True) + EPS)
    unit = v * root
    return unit * gain, unit, root


def norm_back(grad, v, gain):
    _, unit, root = norm_rows(v, gain)
    scaled = grad * gain
    back = root * (scaled - unit * jnp.mean(scaled * unit, axis=-1, keepdims=True))
    return back, jnp.sum(grad * unit, axis=0, keepdims=True)


def block(w, i, j, start=0, stop=None):
    part = w[i, j]
    part = part.reshape(part.shape[0] * part.shape[1] * part.shape[2], part.shape[3])
    return part[start:stop]


def half_of_sequence(halves):
    return lax.rem(lax.axis_index("mp"), halves)


def chunks(rows, step):
    return [(r, min(step, rows - r)) for r in range(0, rows, step)]


MESH_ID = pl.DeviceIdType.MESH


def places():
    d = lax.axis_index("dp")
    z = lax.axis_index("mp")
    lo = lax.rem(d, 8)
    core = lax.rem(lo, 2)
    x = lax.rem(lax.div(lo, 2), 2)
    y = lax.div(lo, 4)
    d_core = d + 1 - 2 * core
    d_x = d + 2 - 4 * x
    d_y = d + 4 - 8 * y
    return d, z, core, x, y, d_core, d_x, d_y


def peer(k):
    d = lax.axis_index("dp")
    lo = lax.rem(d, 8)
    return d - lo + lax.rem(lo + k, 8)


def greet(z_parts, everyone):
    d, z, _, _, _, d_core, d_x, d_y = places()
    barrier = pltpu.get_barrier_semaphore()
    near = [peer(k) for k in range(1, 8)] if everyone else [d_core, d_x, d_y]
    for who in near:
        pl.semaphore_signal(barrier, inc=1, device_id=(who, z), device_id_type=MESH_ID)
    for step in range(1, z_parts):
        pl.semaphore_signal(
            barrier, inc=1, device_id=(d, lax.rem(z + step, z_parts)), device_id_type=MESH_ID
        )
    return lambda: pl.semaphore_wait(barrier, len(near) + z_parts - 1)


def remote(src, dst, send, recv, who):
    return pltpu.make_async_remote_copy(
        src_ref=src, dst_ref=dst, send_sem=send, recv_sem=recv, device_id=who, device_id_type=MESH_ID
    )


class Gather:
    parts_of_group = 3
    chunks = 12
    ahead = 6

    def __init__(self, mine, wg, z_send, z_recv, s_send, s_recv):
        self.mine, self.wg = mine, wg
        self.z_sems, self.s_sems = (z_send, z_recv), (s_send, s_recv)
        self.parts = wg.shape[1]
        self.place = places()

    def rows(self, k):
        some = self.wg.shape[4] // self.parts_of_group
        return k // self.parts_of_group, pl.ds((k % self.parts_of_group) * some, some)

    def z_copy(self, k, step, part=0):
        d, z, core, x, y, *_ = self.place
        yx = 2 * y + x
        g, rows = self.rows(k)
        mine = self.mine[g]
        src = mine[part].at[core, rows] if isinstance(mine, tuple) else mine.at[yx, core, rows]
        return remote(
            src,
            self.wg.at[g, self.parts - step, yx, core, rows],
            self.z_sems[0].at[k, step - 1],
            self.z_sems[1].at[k, step - 1],
            (d, lax.rem(z + step, self.parts)),
        )

    def s_copy(self, k, n):
        d, z, core, x, y, d_core, d_x, d_y = self.place
        rest = pl.ds(1, self.parts - 1)
        g, rows = self.rows(k)
        width = self.wg.shape[5]
        if n < 2:
            ref = self.wg.at[g, rest, 2 * y + x, core, rows]
            who = (d_x, d_y)[n]
        elif n == 2:
            ref = self.wg.at[g, rest, 2 * y + 1 - x, core, rows, pl.ds(0, width // 2)]
            who = d_y
        elif n == 3:
            ref = self.wg.at[g, rest, 2 * (1 - y) + x, core, rows, pl.ds(width // 2, width // 2)]
            who = d_x
        else:
            ref = self.wg.at[g, rest, :, core, rows]
            who = d_core
        return remote(ref, ref, self.s_sems[0].at[k, n], self.s_sems[1].at[k, n], (who, z))

    def z_start(self, k):
        _, _, _, x, y, *_ = self.place
        if isinstance(self.mine[self.rows(k)[0]], tuple):
            for part in range(4):

                @pl.when(2 * y + x == part)
                def _(part=part):
                    for step in range(1, self.parts):
                        self.z_copy(k, step, part).start()

        else:
            for step in range(1, self.parts):
                self.z_copy(k, step).start()

    def tick(self, k):
        if k < self.chunks:
            for step in range(1, self.parts):
                self.z_copy(k, step).wait_recv()
            self.s_copy(k, 0).start()
            self.s_copy(k, 1).start()
            if k + self.ahead < self.chunks:
                self.z_start(k + self.ahead)
        if 0 <= k - 1 < self.chunks:
            self.s_copy(k - 1, 0).wait_recv()
            self.s_copy(k - 1, 2).start()
            self.s_copy(k - 1, 1).wait_recv()
            self.s_copy(k - 1, 3).start()
        if 0 <= k - 2 < self.chunks:
            self.s_copy(k - 2, 2).wait_recv()
            self.s_copy(k - 2, 3).wait_recv()
            self.s_copy(k - 2, 4).start()

    def arrived(self, g):
        for k in range(self.parts_of_group * g, self.parts_of_group * (g + 1)):
            self.s_copy(k, 4).wait_recv()

    def sent(self):
        for k in range(self.chunks):
            for step in range(1, self.parts):
                self.z_copy(k, step).wait_send()
            for n in range(5):
                self.s_copy(k, n).wait_send()


C_RING = 4
KEEP = 4
A_RING = 6
B_RING = 6
Z_RING = 6
TICKS = 16


class Scatter:
    def __init__(self, bufs, sems, credit):
        (
            self.c_in, self.a_in, self.b_in, self.z_in,
            self.a_out, self.a_keep, self.b_out, self.b_keep, self.z_out, self.total,
        ) = bufs
        self.sems, self.credit = sems, credit
        self.parts = 4
        self.share = self.z_out.shape[1]
        self.place = places()

    def block(self, t):
        if t < 8:
            return 3 - t // 4, t % 4
        return 3 - t // 4, (t + 1) % 4

    def copy(self, k, t, src, dst, who):
        return remote(src, dst, self.sems.at[0, k, t], self.sems.at[1, k, t], who)

    def c_copy(self, t, src):
        z, d_core = self.place[1], self.place[5]
        return self.copy(0, t, src, self.c_in.at[t % C_RING], (d_core, z))

    def a_copy(self, t, q):
        _, z, *_, d_x, d_y = self.place
        src, dst = self.a_out.at[t % 2, q], self.a_in.at[t % A_RING, q]
        return self.copy(1 + q, t, src, dst, ((d_x, d_y)[q], z))

    def b_copy(self, t, q):
        _, z, *_, d_x, d_y = self.place
        src, dst = self.b_out.at[t % 2, q], self.b_in.at[t % B_RING, q]
        return self.copy(3 + q, t, src, dst, ((d_y, d_x)[q], z))

    def z_copy(self, t):
        d, z = self.place[:2]
        who = (d, lax.rem(z + self.block(t)[1], self.parts))
        return self.copy(5, t, self.z_out.at[t % Z_RING], self.z_in.at[t], who)

    def rows(self, q):
        return pl.ds(q * (self.share // 2), self.share // 2)

    def c_start(self, t, src):
        if t >= C_RING:
            pl.semaphore_wait(self.credit.at[0], 1)
        self.c_copy(t, src).start()

    def a_start(self, t, mine, src):
        _, _, _, x, y, d_core, *_ = self.place
        slot, ring, held = t % 2, t % C_RING, t % KEEP
        if t >= 2:
            self.a_copy(t - 2, 0).wait_send()
            self.a_copy(t - 2, 1).wait_send()
        self.c_copy(t, src).wait_recv()
        for q in range(2):
            rows = self.rows(q)
            for k in range(2):
                send = (2 * k + 1 - x, 2 * (1 - y) + k)[q]
                self.a_out[slot, q, k] = mine[send, rows] + self.c_in[ring, send, rows]
            if t >= A_RING:
                pl.semaphore_wait(self.credit.at[1 + q], 1)
            self.a_copy(t, q).start()
        for q in range(2):
            rows = self.rows(q)
            for k in range(2):
                keep = (2 * k + x, 2 * y + k)[q]
                self.a_keep[held, q, k] = mine[keep, rows] + self.c_in[ring, keep, rows]
        if t < TICKS - C_RING:
            self.free(0, d_core)

    def free(self, k, who):
        pl.semaphore_signal(
            self.credit.at[k], inc=1, device_id=(who, self.place[1]), device_id_type=MESH_ID
        )

    def b_start(self, t):
        _, _, _, x, y, _, d_x, d_y = self.place
        slot, held, ring = t % 2, t % KEEP, t % A_RING
        if t >= 2:
            self.b_copy(t - 2, 0).wait_send()
            self.b_copy(t - 2, 1).wait_send()
        for q in range(2):
            keep = (y, x)[q]
            send = 1 - keep
            self.a_copy(t, q).wait_recv()
            self.b_out[slot, q] = self.a_keep[held, q, send] + self.a_in[ring, q, send]
            if t >= B_RING:
                pl.semaphore_wait(self.credit.at[3 + q], 1)
            self.b_copy(t, q).start()
            self.b_keep[held, q] = self.a_keep[held, q, keep].astype(F32) + self.a_in[
                ring, q, keep
            ].astype(F32)
            if t < TICKS - A_RING:
                self.free(1 + q, (d_x, d_y)[q])

    def z_start(self, t):
        slot, held = t % Z_RING, t % KEEP
        g, r = self.block(t)
        if t >= Z_RING and self.block(t - Z_RING)[1] > 0:
            self.z_copy(t - Z_RING).wait_send()
        for q in range(2):
            self.b_copy(t, q).wait_recv()
            done = self.b_keep[held, q] + self.b_in[t % B_RING, q].astype(F32)
            if r == 0:
                self.total[g, self.rows(q)] = done
            else:
                self.z_out[slot, self.rows(q)] = low(done)
            if t < TICKS - B_RING:
                self.free(3 + q, self.place[7 - q])
        if r > 0:
            self.z_copy(t).start()

    def finish(self):
        for t in range(TICKS - 2, TICKS):
            for q in range(2):
                self.a_copy(t, q).wait_send()
                self.b_copy(t, q).wait_send()
        for t in range(TICKS):
            g, r = self.block(t)
            if r > 0:
                if t >= TICKS - Z_RING:
                    self.z_copy(t).wait_send()
                self.z_copy(t).wait_recv()
                self.total[g] += self.z_in[t].astype(F32)


class Sum:
    def __init__(self, near, far, send, recv):
        self.near, self.far = near, far
        self.send, self.recv = send, recv
        self.place = places()
        self.lo = lax.rem(self.place[0], 8)

    def near_copy(self, k):
        ref = self.near.at[self.lo]
        return remote(
            ref, ref, self.send.at[k - 1], self.recv.at[k - 1], (peer(k), self.place[1])
        )

    def far_copy(self, k):
        d, z = self.place[:2]
        ref = self.far.at[z]
        who = (d, lax.rem(z + k, self.far.shape[0]))
        return remote(ref, ref, self.send.at[6 + k], self.recv.at[6 + k], who)

    def start(self, value):
        self.near[self.lo] = value
        for k in range(1, 8):
            self.near_copy(k).start()

    def turn(self):
        for k in range(1, 8):
            self.near_copy(k).wait_send()
            sender = lax.rem(self.lo + 8 - k, 8)
            ref = self.near.at[sender]
            remote(
                ref, ref, self.send.at[k - 1], self.recv.at[k - 1], (peer(8 - k), self.place[1])
            ).wait_recv()
        value = self.near[0]
        for k in range(1, 8):
            value = value + self.near[k]
        self.far[self.place[1]] = value
        for k in range(1, self.far.shape[0]):
            self.far_copy(k).start()

    def result(self):
        d, z = self.place[:2]
        parts = self.far.shape[0]
        for k in range(1, parts):
            self.far_copy(k).wait_send()
            sender = lax.rem(z + parts - k, parts)
            ref = self.far.at[sender]
            remote(
                ref, ref, self.send.at[6 + k], self.recv.at[6 + k], (d, sender)
            ).wait_recv()
        value = self.far[0]
        for k in range(1, parts):
            value = value + self.far[k]
        return value


def layer_kernel(
    halves,
    len_ref, x_ref, cot_ref, enc_own, gain1, gain2, gain3, buckets_ref, table_in,
    sk, sv, sq, so, ck, cv, cq, co, fi, fo,
    result_ref, total_out, small_out, dx_out, denc_out,
    w_hbm, g_hbm, q1_hbm, kv1_hbm, p1_hbm, o1_hbm, l1_hbm, q2_hbm, kv2_hbm, p2_hbm, o2_hbm, l2_hbm,
    w, enc, diag, mask, onehot, spread, xa, table_own, table_far,
    nbuf, n2, n3, q_in, kv_in, p_in, o_in, l_in, x1, x2, hid, slope, acc, dn,
    g_buf, l_buf, rows_t, rows_t2, keys_t, dp_buf, ds_buf, dkv_t, enc_acc, diag_acc,
    dxa_in, denc_in, small,
    c_in, a_in, b_in, z_in, a_out, a_keep, b_out, b_keep, z_out, s_near, s_far,
    w_sem, own_sem, in_sem, ring_sem, keep_sem, store_sem, load_sem, out_sem,
    z_send, z_recv, s_send, s_recv, e_send, e_recv,
    sems, credit, n_send, n_recv,
):
    rows, width_all = x_ref.shape
    width = width_all
    parts = w_hbm.shape[1]
    place = places()
    d, z_me, core = place[:3]
    half = half_of_sequence(halves)
    mate = z_me + 1 - 2 * half
    keys = 2 * enc.shape[1]
    own_keys = 2 * rows
    all_keys = (own_keys, keys)
    entered = greet(parts, True)

    mine = ((sk, sv, sq, so), (ck, cv, cq, co), fi, fo)

    def own_copies(g, k):
        if g >= 2:
            return [pltpu.make_async_copy(mine[g], w.at[0, k], own_sem.at[k, 0])]
        return [
            pltpu.make_async_copy(ref, w.at[0, k, part], own_sem.at[k, part])
            for part, ref in enumerate(mine[g])
        ]

    def own_start(g, k):
        for copy in own_copies(g, k):
            copy.start()

    def far_copy(g, r, slot, k):
        return pltpu.make_async_copy(w_hbm.at[g, r], w.at[slot, k], w_sem.at[slot, k])

    def own_in_slot_one(g, k):
        if g >= 2:
            return [pltpu.make_async_copy(mine[g], w.at[1, k], own_sem.at[k, 0])]
        return [
            pltpu.make_async_copy(ref, w.at[1, k, part], own_sem.at[k, part])
            for part, ref in enumerate(mine[g])
        ]

    def w_wait(g, r, k):
        @pl.when(r == 0)
        def _():
            for copy in own_copies(g, k):
                copy.wait()

        @pl.when(r > 0)
        def _():
            far_copy(g, r, lax.rem(r, 2), k).wait()

    def w_next(g, r, k):
        @pl.when((r > 0) & (r + 1 < parts))
        def _():
            far_copy(g, r + 1, lax.rem(r + 1, 2), k).start()

    def which(i):
        return lax.rem(i + 1, parts)

    kept = (
        (q1_hbm, kv1_hbm, p1_hbm, o1_hbm, l1_hbm),
        (q2_hbm, kv2_hbm, p2_hbm, o2_hbm, l2_hbm),
    )

    def ring(phase, r, slot):
        n = all_keys[phase]
        q, kv, p, o, l = kept[phase]
        return [
            (q.at[r], q_in.at[slot]),
            (kv.at[r], kv_in.at[slot, 0:n]),
            (p.at[pl.ds(3 * r, 3)], p_in.at[slot, :, :, 0:n]),
            (o.at[r], o_in.at[slot]),
            (l.at[r], l_in.at[slot]),
        ]

    def keeps(phase, r):
        slot = lax.rem(r, 2)
        return [
            pltpu.make_async_copy(dst, src, keep_sem.at[k, slot])
            for k, (src, dst) in enumerate(ring(phase, r, slot))
        ]

    def keep_wait(phase, r):
        for copy in keeps(phase, r):
            copy.wait()

    def streams(phase, i):
        slot = lax.rem(i, 2)
        return [
            pltpu.make_async_copy(src, dst, ring_sem.at[k, slot])
            for k, (src, dst) in enumerate(ring(phase, which(i), slot))
        ]

    def back_prefetch(phase, i):
        @pl.when(i < parts - 1)
        def _():
            far_copy(phase, which(i), lax.rem(i, 2), 0).start()

        @pl.when(i == parts - 1)
        def _():
            for copy in own_in_slot_one(phase, 0):
                copy.start()

        for copy in streams(phase, i):
            copy.start()

    def back_wait(phase, i):
        @pl.when(i < parts - 1)
        def _():
            far_copy(phase, which(i), lax.rem(i, 2), 0).wait()

        @pl.when(i == parts - 1)
        def _():
            for copy in own_in_slot_one(phase, 0):
                copy.wait()

        for copy in streams(phase, i):
            copy.wait()

    enc_here = pltpu.make_async_copy(enc_own, enc.at[half], in_sem)
    own_start(0, 0)
    enc_here.start()
    entered()

    gather = Gather(mine, w_hbm, z_send, z_recv, s_send, s_recv)
    scatter = Scatter(
        (c_in, a_in, b_in, z_in, a_out, a_keep, b_out, b_keep, z_out, total_out), sems, credit
    )
    sums = Sum(s_near, s_far, n_send, n_recv)
    x_copy = remote(x_ref, xa, e_send.at[0], e_recv.at[0], (d, mate))
    enc_copy = remote(enc_own, enc.at[half], e_send.at[1], e_recv.at[1], (d, mate))
    dxa_copy = remote(n2, dxa_in, e_send.at[2], e_recv.at[2], (d, mate))
    denc_copy = remote(enc.at[1 - half], denc_in, e_send.at[3], e_recv.at[3], (d, mate))
    tables = [
        remote(
            table_own, table_far.at[parts - step], e_send.at[3 + step], e_recv.at[3 + step],
            (d, lax.rem(z_me + step, parts)),
        )
        for step in range(1, parts)
    ]

    def put(t, value, start=0):
        shape = g_buf.shape[1:4] + (value.shape[1],)
        g_buf[lax.rem(t, 2), :, :, :, start : start + value.shape[1]] = value.reshape(shape)

    def store(t):
        slot = lax.rem(t, 2)
        return pltpu.make_async_copy(g_buf.at[slot], g_hbm.at[t], store_sem.at[slot])

    def away(t):
        return g_hbm.at[t, :, 1 - core]

    def load(t):
        slot = t % 2
        return pltpu.make_async_copy(g_hbm.at[t, :, core], l_buf.at[slot], load_sem.at[slot])

    def leave(t):
        if t < TICKS:
            scatter.c_start(t, away(t))
            load(t).start()
        if t >= 1:
            load(t - 1).wait()
            scatter.a_start(t - 1, l_buf.at[(t - 1) % 2], away(t - 1))

    b, z, tick = scatter.b_start, scatter.z_start, gather.tick

    def at(i, step, *moves):
        @pl.when(i == step)
        def _():
            for move, *args in moves:
                move(*args)

    gather.z_start(0)
    gather.z_start(1)

    @pl.when(half == 0)
    def _():
        x_copy.start()

    gather.z_start(2)
    table_own[...] = jnp.zeros_like(table_own)
    table_own[0 : table_in.shape[0], 0 : table_in.shape[1]] = table_in[...]
    for copy in tables:
        copy.start()
    for k in range(3, gather.ahead):
        gather.z_start(k)

    nbuf[rows : 2 * rows, :] = low(norm_rows(x_ref[...].astype(F32), line_of(gain1))[0])
    tick(0)

    slots = buckets_ref.shape[0]
    span = onehot.shape[1]
    here = jnp.concatenate(
        [line_of(buckets_ref), jnp.full((1, span - slots), -1, jnp.int32)], axis=1
    )
    kinds = onehot.shape[0]
    hit = lax.broadcasted_iota(jnp.int32, (kinds, span), 0) == here
    plain = jnp.where(hit, 1.0, 0.0).astype(BF16)
    for start in range(0, span, 128):
        offset = lax.broadcasted_iota(jnp.int32, (span, 128), 0)
        column = lax.broadcasted_iota(jnp.int32, (span, 128), 1) + start
        turn = (offset + column == rows) | (offset + column == rows + span)
        onehot[:, start : start + 128] = mm(plain, jnp.where(turn, 1.0, 0.0).astype(BF16))

    turns = [onehot[...]] + [pltpu.roll(onehot[...], k, 1) for k in range(1, 8)]
    spread[...] = jnp.transpose(jnp.concatenate(turns, axis=0))

    length = len_ref[lax.div(z_me, halves)]
    i = lax.broadcasted_iota(jnp.int32, mask.shape, 0)
    c = lax.broadcasted_iota(jnp.int32, mask.shape, 1)
    own = c - rows
    limit = jnp.where(half > 0, length, 0)
    ok = ((own < 0) & (c < limit)) | ((own >= 0) & (own <= i) & (own + half * rows < length))
    mask[...] = jnp.where(ok, 0.0, MASKED)
    tick(1)
    enc_copy.start()
    for copy in tables:
        copy.wait()
    for r in range(parts):
        table = table_own[...] if r == 0 else table_far[r]
        diag[r] = jnp.dot(
            table[:, 0 : onehot.shape[0]],
            onehot[...],
            precision=lax.Precision.HIGHEST,
            preferred_element_type=F32,
        )

    @pl.when(half == 0)
    def _():
        x_copy.wait_send()
        xa[...] = x_ref[...]

    @pl.when(half == 1)
    def _():
        x_copy.wait_recv()

    nbuf[0:rows, :] = low(norm_rows(xa[...].astype(F32), line_of(gain1))[0])

    def heads(phase, r):
        n = all_keys[phase]
        slot = lax.rem(r, 2)
        outs = []
        for j in range(3):
            q_h = q_in[slot, :, DH * j : DH * (j + 1)]
            k_h = kv_in[slot, 0:n, DH * j : DH * (j + 1)]
            v_h = kv_in[slot, 0:n, DH * (3 + j) : DH * (4 + j)]
            dp_buf[j % 2, :, 0:n] = mm_nt(q_h, k_h)
            for a, m in chunks(rows, 32):
                s = dp_buf[j % 2, a : a + m, 0:n]
                if phase == 0:
                    line = jnp.broadcast_to(diag[r, j : j + 1, :], (m, diag.shape[2]))
                    grid = pltpu.roll(line, a, 1, stride=1, stride_axis=0)
                    s = s + grid[:, 0:n] + mask[a : a + m, :]
                top = jnp.max(s, axis=1, keepdims=True)
                p_in[slot, j, a : a + m, 0:n] = low(jnp.exp(s - top))
            wide = jnp.concatenate([v_h, jnp.ones_like(v_h)], axis=1)
            mixed = mm(p_in[slot, j, :, 0:n], wide)
            outs.append(low(mixed[:, 0:DH] / mixed[:, DH : 2 * DH]))
            l_in[slot, :, 32 * j : 32 * (j + 1)] = mixed[:, DH : DH + 32]
        o_in[slot] = jnp.concatenate(outs, axis=1)

    def attention(phase, r, key_rows, query_rows):
        slot = lax.rem(r, 2)
        w_wait(phase, r, 0)
        w_next(phase, r, 0)

        @pl.when(r >= 2)
        def _():
            keep_wait(phase, r - 2)

        if phase == 1:

            @pl.when(r < 2)
            def _():
                keep_wait(0, r + 2)

        kv_in[slot, 0 : all_keys[phase]] = low(mm_nt(key_rows, block(w, slot, 0, 0, 384)))
        q_in[slot] = low(mm_nt(query_rows, block(w, slot, 0, 384, 576)))
        heads(phase, r)
        acc[...] += mm(o_in[slot], block(w, slot, 0, 576, 768))
        for copy in keeps(phase, r):
            copy.start()

    def take(g, k):
        gather.arrived(g)
        far_copy(g, 1, 1, k).start()

    acc[...] = x_ref[...].astype(F32)

    def self_step(r, carry):
        attention(0, r, nbuf[...], nbuf[rows : 2 * rows, :])
        at(r, 0, (tick, 2), (tick, 3), (tick, 4), (take, 0, 0))
        at(r, 1, (tick, 5))
        at(r, 2, (tick, 6), (own_start, 1, 0))
        at(r, 3, (tick, 7))
        return carry

    lax.fori_loop(0, parts, self_step, 0)
    x1[...] = acc[...]
    n2[...] = low(norm_rows(acc[...], line_of(gain2))[0])

    enc_copy.wait()
    enc_here.wait()

    def cross_step(r, carry):
        attention(1, r, enc[...].reshape(keys, width), n2[...])
        at(r, 0, (tick, 8), (take, 1, 0))
        at(r, 1, (tick, 9))
        at(r, 2, (tick, 10), (own_start, 2, 0))
        at(r, 3, (tick, 11))
        return carry

    lax.fori_loop(0, parts, cross_step, 0)
    x2[...] = acc[...]
    n3[...] = low(norm_rows(acc[...], line_of(gain3))[0])

    own_start(3, 1)
    rows_t[...] = flip(cot_ref[...])

    def inner_step(r, carry):
        slot = lax.rem(r, 2)
        w_wait(2, r, 0)
        w_next(2, r, 0)
        for a, n in chunks(rows, 64):
            v = mm(n3[a : a + n, :], block(w, slot, 0))
            sq = v * v
            t = jnp.tanh(v * (ROOT + ROOT * CUBE * sq))
            cdf = 0.5 + 0.5 * t
            hid[r, a : a + n, :] = low(v * cdf)
            slope[r, a : a + n, :] = low(
                cdf + 0.5 * v * (1.0 - t * t) * (ROOT + 3.0 * ROOT * CUBE * sq)
            )
        put(r, low(mm(rows_t[...], hid[r])))
        store(r).start()
        at(r, 0, (take, 2, 0))
        at(r, 1, (tick, 12))
        at(r, 2, (own_start, 2, 0))
        at(r, 3, (tick, 13))
        store(r).wait()
        at(r, 2, (leave, 0))
        at(r, 3, (leave, 1))
        return carry

    lax.fori_loop(0, parts, inner_step, 0)
    for r in (parts - 2, parts - 1):
        keep_wait(1, r)
    rows_t2[...] = flip(n3[...])
    dn[...] = jnp.zeros_like(dn)
    leave(2)

    def outer_step(r, carry):
        slot = lax.rem(r, 2)
        w_wait(3, r, 1)
        w_next(3, r, 1)
        w_wait(2, r, 0)

        @pl.when(r + 1 < parts)
        def _():
            far_copy(2, r + 1, lax.rem(r + 1, 2), 0).start()

        @pl.when(r + 1 == parts)
        def _():
            back_prefetch(1, jnp.int32(0))

        dh = low(mm_nt(cot_ref[...], block(w, slot, 1)))
        slope[r] = low(dh.astype(F32) * slope[r].astype(F32))
        put(4 + r, low(mm(rows_t2[...], slope[r])))
        store(4 + r).start()
        dn[...] += mm_nt(slope[r], block(w, slot, 0))
        store(4 + r).wait()
        at(r, 0, (leave, 3), (b, 0), (take, 3, 1))
        at(r, 1, (leave, 4), (b, 1), (z, 0))
        at(r, 2, (leave, 5), (b, 2), (z, 1))
        return carry

    lax.fori_loop(0, parts, outer_step, 0)
    def keep_sum(g, value):
        part = width_all // 2
        small[2 * g : 2 * g + 1, :] = value[:, 0:part]
        small[2 * g + 1 : 2 * g + 2, :] = value[:, part:]

    small[...] = jnp.zeros_like(small)
    back, sum3 = norm_back(dn[...], x2[...], line_of(gain3))
    dn[...] = cot_ref[...].astype(F32) + back
    keep_sum(2, sum3)
    leave(6)
    b(3)
    z(2)

    def heads_back(r, do, n, with_diag, between):
        slot = lax.rem(r, 2)
        q, kv, o = q_in[slot], kv_in.at[slot], o_in[slot].astype(F32)
        do_all = []
        delta_all = []
        for j in range(3):
            do_h = do[:, DH * j : DH * (j + 1)]
            inv = 1.0 / l_in[slot, :, 32 * j : 32 * j + 1]
            o_h = o[:, DH * j : DH * (j + 1)]
            delta_all.append(jnp.sum(do_h * o_h * inv, axis=1, keepdims=True))
            do_all.append(do_h * inv)
        do_t = low(jnp.transpose(jnp.concatenate(do_all, axis=1)))
        q_t = flip(q)
        dq = []
        for j in range(3):
            p_h = p_in.at[slot, j]
            k_h = kv[0:n, DH * j : DH * (j + 1)]
            v_h = kv[0:n, DH * (3 + j) : DH * (4 + j)]
            dp_buf[j % 2, :, 0:n] = mm_nt(low(do_all[j]), v_h)
            total = None
            for s, m in chunks(rows, 32):
                ds = low(
                    p_h[s : s + m, 0:n].astype(F32)
                    * (dp_buf[j % 2, s : s + m, 0:n] - delta_all[j][s : s + m, :])
                )
                ds_buf[j % 2, s : s + m, 0:n] = ds
                if with_diag:
                    width = diag_acc.shape[2]
                    wide = jnp.concatenate([ds.astype(F32), jnp.zeros((m, width - n), F32)], axis=1)
                    for b in range(0, m, 8):
                        turned = pltpu.roll(wide[b : b + 8, :], (width - s - b) % width, 1)
                        total = turned if total is None else total + turned
            if with_diag:
                diag_acc[which(r) * 3 + j] = total
            ds_h = ds_buf[j % 2, :, 0:n]
            dq.append(low(mm(ds_h, k_h)))
            dkv_t[DH * j : DH * (j + 1), 0:n] = mm(q_t[DH * j : DH * (j + 1), :], ds_h)
            dkv_t[DH * (3 + j) : DH * (4 + j), 0:n] = mm(
                do_t[DH * j : DH * (j + 1), :], p_h[:, 0:n]
            )
            if j == 1:
                between()
        return jnp.concatenate(dq, axis=1), low(jnp.transpose(dkv_t[:, 0:n]))

    def attention_step(phase, i, middle):
        slot = lax.rem(i, 2)
        n = all_keys[phase]
        t = 12 - 4 * phase + i
        back_wait(phase, i)

        @pl.when(i + 1 < parts)
        def _():
            back_prefetch(phase, i + 1)

        if phase == 1:

            @pl.when(i + 1 == parts)
            def _():
                back_prefetch(0, jnp.int32(0))

        do = low(mm_nt(low(dn[...]), block(w, slot, 0, 576, 768))).astype(F32)
        dq, dkv = heads_back(i, do, n, phase == 0, lambda: middle(i))
        put(t, low(mm(keys_t[:, 0:n], dkv)))
        both = [low(mm(rows_t2[...], dq)), low(mm(rows_t[...], o_in[slot]))]
        put(t, jnp.concatenate(both, axis=1), 384)
        store(t).start()
        acc[...] += mm(dq, block(w, slot, 0, 384, 576))
        enc_acc[0:n, :] += mm(dkv, block(w, slot, 0, 0, 384))
        store(t).wait()

    rows_t[...] = flip(low(dn[...]))
    rows_t2[...] = flip(n2[...])
    keys_t[...] = flip(enc[...].reshape(keys, width_all))
    acc[...] = jnp.zeros_like(acc)
    enc_acc[...] = jnp.zeros_like(enc_acc)

    def cross_back_step(i, carry):
        def middle(i):
            at(i, 0, (leave, 7), (b, 4), (z, 3))
            at(i, 1, (leave, 8), (b, 6), (z, 5))
            at(i, 2, (b, 7), (z, 6))
            at(i, 3, (leave, 10), (b, 8), (z, 7))

        attention_step(1, i, middle)
        at(i, 0, (b, 5), (z, 4))
        at(i, 1, (leave, 9))
        at(i, 3, (leave, 11))
        return carry

    lax.fori_loop(0, parts, cross_back_step, 0)
    enc[...] = low(enc_acc[...]).reshape(enc.shape)
    denc_copy.start()
    back, sum2 = norm_back(acc[...], x1[...], line_of(gain2))
    dn[...] += back
    keep_sum(1, sum2)
    b(9)
    z(8)

    own_start(3, 1)
    far_copy(3, 1, 1, 1).start()
    rows_t[...] = flip(low(dn[...]))
    rows_t2[...] = flip(nbuf[rows : 2 * rows, :])
    keys_t[:, 0:own_keys] = flip(nbuf[...])
    acc[...] = jnp.zeros_like(acc)
    enc_acc[0:own_keys, :] = jnp.zeros((own_keys, width_all), F32)

    def self_back_step(i, carry):
        def middle(i):
            at(i, 0, (b, 10), (z, 9))
            at(i, 1, (z, 10))
            at(i, 2, (z, 11))

        attention_step(0, i, middle)
        at(i, 0, (leave, 12))
        at(i, 1, (leave, 13), (b, 11))
        at(i, 2, (leave, 14), (b, 12))
        at(i, 3, (leave, 15), (b, 13), (z, 12))
        return carry

    lax.fori_loop(0, parts, self_back_step, 0)
    for r in (2, 3):
        far_copy(3, r, r - 2, 0).start()
    gain = line_of(gain1)
    back, sum1a = norm_back(enc_acc[0:rows, :], xa[...].astype(F32), gain)
    n2[...] = low(back)

    @pl.when(half == 1)
    def _():
        dxa_copy.start()

    leave(16)
    back, sum1 = norm_back(
        acc[...] + enc_acc[rows : 2 * rows, :], x_ref[...].astype(F32), gain
    )
    dn[...] += back
    keep_sum(0, sum1 + sum1a)
    count = 8 * diag_acc.shape[0]
    turned = jnp.dot(
        diag_acc[...].reshape(count, diag_acc.shape[2]),
        spread[...],
        precision=lax.Precision.HIGHEST,
        preferred_element_type=F32,
    )
    kinds = onehot.shape[0]
    row = lax.rem(lax.broadcasted_iota(jnp.int32, turned.shape, 0), 8)
    place_of = lax.div(lax.broadcasted_iota(jnp.int32, turned.shape, 1), kinds)
    turned = jnp.where(row == place_of, turned, 0.0)
    turned = jnp.sum(turned.reshape(count // 8, 8, turned.shape[1]), axis=1)
    table = turned[:, 0:kinds]
    for k in range(1, 8):
        table = table + turned[:, kinds * k : kinds * (k + 1)]
    for r in range(parts):
        at = lax.rem(z_me + r, parts)
        for p in range(parts):

            @pl.when(at == p)
            def _(r=r, p=p):
                for j in range(3):
                    lane = kinds * (3 * p + j)
                    small[6:7, lane : lane + kinds] = table[3 * r + j : 3 * r + j + 1]

    sums.start(small[...])
    for copy in own_copies(3, 1):
        copy.wait()
    x2[...] += mm(hid[0], block(w, 0, 1))
    b(14)
    z(13)
    far_copy(3, 1, 1, 1).wait()
    x2[...] += mm(hid[1], block(w, 1, 1))
    sums.turn()
    b(15)
    z(14)
    for r in (2, 3):
        far_copy(3, r, r - 2, 0).wait()
        x2[...] += mm(hid[r], block(w, r - 2, 0))
    result_ref[...] = low(x2[...])
    denc_copy.wait()
    enc[half] = low(enc[half].astype(F32) + denc_in[...].astype(F32))
    denc_done = pltpu.make_async_copy(enc.at[half], denc_out, out_sem.at[0])
    denc_done.start()
    z(15)

    @pl.when(half == 1)
    def _():
        dxa_copy.wait_send()
        n3[...] = low(dn[...])

    @pl.when(half == 0)
    def _():
        dxa_copy.wait_recv()
        n3[...] = low(dn[...] + dxa_in[...].astype(F32))

    dx_done = pltpu.make_async_copy(n3, dx_out, out_sem.at[1])
    dx_done.start()
    scatter.finish()
    small_out[...] = sums.result()
    for t in range(TICKS):
        scatter.c_copy(t, away(t)).wait_send()
    gather.sent()
    denc_done.wait()
    dx_done.wait()


def finish_kernel(
    result_in, dx, denc, total, small,
    result, input_grad, encoder_grad,
    g_gain1, gsq, gsk, gsv, gso, g_gain2, gcq, gck, gcv, gco, g_gain3, gfi, gfo, lines,
):
    result[...] = result_in[...]
    input_grad[...] = dx[...]
    encoder_grad[...] = denc[...]
    width = result.shape[1]
    for g, (k, v, q, o) in enumerate(((gsk, gsv, gsq, gso), (gck, gcv, gcq, gco))):
        k[...] = total[g, :, 0:192]
        v[...] = total[g, :, 192:384]
        q[...] = total[g, :, 384:576]
        o[...] = jnp.transpose(total[g, :, 576:768])
    gfi[...] = total[2]
    gfo[...] = total[3]
    for row, gain in enumerate((g_gain1, g_gain2, g_gain3)):
        part = small[2 * row : 2 * row + 2, :]
        gain[...] = jnp.concatenate([part[0:1], part[1:2]], axis=1).reshape(width)
    z = lax.axis_index("mp")
    for p in range(4):

        @pl.when(z == p)
        def _(p=p):
            kinds = lines.shape[1]
            for j in range(3):
                lane = kinds * (3 * p + j)
                lines[j : j + 1, :] = small[6:7, lane : lane + kinds]


def across(value, axis, n_dp):
    groups = n_dp // 8
    whole = lax.all_gather(value, "dp", axis=0, tiled=False)
    whole = whole.reshape(groups, 8, *value.shape).sum(0)
    whole = jnp.concatenate([whole[k] for k in range(8)], axis=axis)
    share = whole.shape[axis] // n_dp
    return lax.dynamic_slice_in_dim(whole, lax.axis_index("dp") * share, share, axis)


def across_small(value, n_dp):
    whole = lax.all_gather(value, "dp", axis=0, tiled=False)
    return whole.reshape(n_dp // 8, 8, *value.shape)[:, 0].sum(0)


def body(
    inputs, encoded, cotangent, lengths, buckets,
    self_gain, self_query, self_key, self_value, self_output, bias_table,
    cross_gain, cross_query, cross_key, cross_value, cross_output,
    feed_gain, feed_inner, feed_output_weight,
):
    rows, width = inputs.shape
    parts = lax.axis_size("mp")
    n_dp = lax.axis_size("dp")
    halves = parts // lengths.shape[0]
    assert halves == 2 and buckets.shape[0] == 2 * rows and parts == 4
    z = lax.axis_index("mp")
    enc_rows = encoded.shape[0]
    vmem = pl.BlockSpec(memory_space=pltpu.VMEM)
    smem = pl.BlockSpec(memory_space=pltpu.SMEM)
    hbm = pl.BlockSpec(memory_space=pl.ANY)
    sds = jax.ShapeDtypeStruct

    share = width // 8
    diag = 1024
    heads = 3 * parts
    keys = 2 * enc_rows
    gains = [self_gain, cross_gain, feed_gain]
    split = lambda v: v.reshape(2, share, width)
    whole = lambda v: v.reshape(4, 2, share, width)
    kinds = bias_table.shape[0]
    kept = [
        kind
        for n in (2 * rows, keys)
        for kind in (
            sds((parts, rows, 192), BF16),
            sds((parts, n, 384), BF16),
            sds((heads, rows, n), BF16),
            sds((parts, rows, 192), BF16),
            sds((parts, rows, 128), F32),
        )
    ]
    half_share = share // 2
    bf, ff = (lambda *shape: pltpu.VMEM(shape, BF16)), (lambda *shape: pltpu.VMEM(shape, F32))
    dma = lambda *shape: pltpu.SemaphoreType.DMA(shape)
    result, summed, small, input_grad, encoder_grad, *_ = pl.pallas_call(
        functools.partial(layer_kernel, halves),
        out_shape=[
            sds((rows, width), BF16),
            sds((4, share, width), F32),
            sds((8, width // 2), F32),
            sds((rows, width), BF16),
            sds((enc_rows, width), BF16),
            sds((4, parts, 4, 2, share, width), BF16),
            sds((TICKS, 4, 2, share, width), BF16),
            *kept,
        ],
        in_specs=[smem, vmem, vmem, hbm] + [vmem] * 5 + [hbm] * 10,
        out_specs=[vmem] * 3 + [hbm] * (4 + len(kept)),
        scratch_shapes=[
            bf(2, 2, 4, 2, share, width), bf(2, enc_rows, width), ff(parts, 8, diag),
            ff(rows, 2 * rows), ff(kinds, diag), ff(diag, 8 * kinds), bf(rows, width), ff(8, 128), ff(parts, 8, 128),
            bf(2 * rows, width), bf(rows, width), bf(rows, width),
            bf(2, rows, 192), bf(2, keys, 384), bf(2, 3, rows, keys), bf(2, rows, 192),
            ff(2, rows, 128), ff(rows, width), ff(rows, width),
            bf(parts, rows, width), bf(parts, rows, width), ff(rows, width), ff(rows, width),
            bf(2, 4, 2, share, width), bf(2, 4, share, width),
            bf(width, rows), bf(width, rows), bf(width, keys),
            ff(2, rows, keys), bf(2, rows, keys), ff(384, keys), ff(keys, width),
            ff(heads, 8, diag),
            bf(rows, width), bf(enc_rows, width), ff(8, width // 2),
            bf(C_RING, 4, share, width), bf(A_RING, 2, 2, half_share, width),
            bf(B_RING, 2, half_share, width), bf(TICKS, share, width),
            bf(2, 2, 2, half_share, width), bf(KEEP, 2, 2, half_share, width),
            bf(2, 2, half_share, width), ff(KEEP, 2, half_share, width),
            bf(Z_RING, share, width), ff(8, 8, width // 2), ff(parts, 8, width // 2),
            dma(2, 2), dma(2, 4), pltpu.SemaphoreType.DMA, dma(5, 2), dma(5, 2), dma(2), dma(2),
            dma(2),
            dma(Gather.chunks, parts - 1), dma(Gather.chunks, parts - 1),
            dma(Gather.chunks, 5), dma(Gather.chunks, 5), dma(7), dma(7),
            dma(2, 6, TICKS), pltpu.SemaphoreType.REGULAR((5,)), dma(10), dma(10),
        ],
        compiler_params=pltpu.CompilerParams(
            collective_id=1, has_side_effects=True, vmem_limit_bytes=VMEM_BYTES
        ),
        name="layer",
    )(
        lengths, inputs, cotangent, encoded, *gains, buckets, bias_table.T,
        split(self_key.T), split(self_value.T), split(self_query.T), split(self_output),
        split(cross_key.T), split(cross_value.T), split(cross_query.T), split(cross_output),
        whole(feed_inner), whole(feed_output_weight),
    )

    f32 = lambda *shape: sds(shape, F32)
    outs = pl.pallas_call(
        finish_kernel,
        out_shape=[
            sds((rows, width), BF16), sds((rows, width), BF16), sds((enc_rows, width), BF16),
            f32(width), f32(share, 192), f32(share, 192), f32(share, 192), f32(192, share),
            f32(width), f32(share, 192), f32(share, 192), f32(share, 192), f32(192, share),
            f32(width), f32(share, width), f32(share, width), f32(3, kinds),
        ],
        in_specs=[vmem] * 5,
        out_specs=[vmem] * 17,
        name="finish",
    )(result, input_grad, encoder_grad, summed, small)
    result, input_grad, encoder_grad, *grads, lines = outs
    if n_dp > 8:
        axes = (None, 0, 0, 0, 1, None, 0, 0, 0, 1, None, 0, 0)
        grads = [
            across_small(value, n_dp) if axis is None else across(value, axis, n_dp)
            for value, axis in zip(grads, axes)
        ]
        lines = across_small(lines, n_dp)
    return (result, input_grad, encoder_grad, *grads[0:5], lines.T, *grads[5:-1], grads[-1].T)


def solution(mesh):
    rows = P(("dp", "mp"), None)
    across, down = P(None, "mp"), P("mp", None)
    return jax.shard_map(
        body,
        mesh=mesh,
        in_specs=(
            rows, rows, rows, P("dp"), P(),
            P(), across, across, across, down, across,
            P(), across, across, across, down,
            P(), across, down,
        ),
        out_specs=(
            rows, rows, rows,
            P(), P("dp", "mp"), P("dp", "mp"), P("dp", "mp"), P("mp", "dp"), P(None, "mp"),
            P(), P("dp", "mp"), P("dp", "mp"), P("dp", "mp"), P("mp", "dp"),
            P(), P("dp", "mp"), P("mp", "dp"),
        ),
        check_vma=False,
    )
```

time: 217 us -> 211 us (0.972)
  Pallas kernels: 216 us -> 210 us
    pallas_call x2 -> x1, Pallas kernels: 213 us -> 206 us  [body(): pl.pallas_call(functools.partial(layer_kernel, halves), out_shape=[sds((r...]
where the time goes in v5:
time: 211 us
  Pallas kernels  210 us (100%)
    pallas_call x1, Pallas kernels, body(): pl.pallas_call(functools.partial(layer_kernel, halves), out_shape=[sds((r...  206 us

profile of v5, /device:TPU:0, one launch (start us, length us, event | category | flops | bytes accessed | tf_op | source)
XLA Modules:
  0.0 210.6 jit_solution(2885192181423044484)
XLA Ops:
  0.7 205.9 %layer.1 = (bf16[320,768]{1,0:T(8,128)(2,1)}, f32[4,96,768]{2,1,0:T(8,128)}, f32[8,384]{1,0:T(8,128)}, bf16[320,768]{1,0:T(8,128)(2,1)}, bf16[512,768]{1,0:T(8,1...) custom-call(s32[2]{0:T(128)} %len_ref.1, ...), custom_call_target="tpu_custom_call" | custom-call | tf_op jit(solution)/shard_map/layer/pallas_call | solution.py:1075
  206.6 3.9 %finish.1 = (bf16[320,768]{1,0:T(8,128)(2,1)}, bf16[320,768]{1,0:T(8,128)(2,1)}, bf16[512,768]{1,0:T(8,128)(2,1)}, f32[768]{0:T(1024)}, f32[96,192]{1,0:T(8,128)...) custom-call(bf16[320,768]{1,0:T(8,128)(2,1)} %get-tuple-element.39.r, ...), custom_call_target="tpu_custom_call" | custom-call | tf_op jit(solution)/shard_map/finish/pallas_call | solution.py:1124

commit v6 on v5

--- a/solution.py
+++ b/solution.py
@@ -199,6 +199,7 @@
 
 C_RING = 4
 KEEP = 4
+OUT_RING = 4
 A_RING = 6
 B_RING = 6
 Z_RING = 6
@@ -230,12 +231,12 @@
 
     def a_copy(self, t, q):
         _, z, *_, d_x, d_y = self.place
-        src, dst = self.a_out.at[t % 2, q], self.a_in.at[t % A_RING, q]
+        src, dst = self.a_out.at[t % OUT_RING, q], self.a_in.at[t % A_RING, q]
         return self.copy(1 + q, t, src, dst, ((d_x, d_y)[q], z))
 
     def b_copy(self, t, q):
         _, z, *_, d_x, d_y = self.place
-        src, dst = self.b_out.at[t % 2, q], self.b_in.at[t % B_RING, q]
+        src, dst = self.b_out.at[t % OUT_RING, q], self.b_in.at[t % B_RING, q]
         return self.copy(3 + q, t, src, dst, ((d_y, d_x)[q], z))
 
     def z_copy(self, t):
@@ -253,10 +254,10 @@
 
     def a_start(self, t, mine, src):
         _, _, _, x, y, d_core, *_ = self.place
-        slot, ring, held = t % 2, t % C_RING, t % KEEP
-        if t >= 2:
-            self.a_copy(t - 2, 0).wait_send()
-            self.a_copy(t - 2, 1).wait_send()
+        slot, ring, held = t % OUT_RING, t % C_RING, t % KEEP
+        if t >= OUT_RING:
+            self.a_copy(t - OUT_RING, 0).wait_send()
+            self.a_copy(t - OUT_RING, 1).wait_send()
         self.c_copy(t, src).wait_recv()
         for q in range(2):
             rows = self.rows(q)
@@ -281,10 +282,10 @@
 
     def b_start(self, t):
         _, _, _, x, y, _, d_x, d_y = self.place
-        slot, held, ring = t % 2, t % KEEP, t % A_RING
-        if t >= 2:
-            self.b_copy(t - 2, 0).wait_send()
-            self.b_copy(t - 2, 1).wait_send()
+        slot, held, ring = t % OUT_RING, t % KEEP, t % A_RING
+        if t >= OUT_RING:
+            self.b_copy(t - OUT_RING, 0).wait_send()
+            self.b_copy(t - OUT_RING, 1).wait_send()
         for q in range(2):
             keep = (y, x)[q]
             send = 1 - keep
@@ -317,7 +318,7 @@
             self.z_copy(t).start()
 
     def finish(self):
-        for t in range(TICKS - 2, TICKS):
+        for t in range(TICKS - OUT_RING, TICKS):
             for q in range(2):
                 self.a_copy(t, q).wait_send()
                 self.b_copy(t, q).wait_send()
@@ -552,13 +553,18 @@
         slot = t % 2
         return pltpu.make_async_copy(g_hbm.at[t, :, core], l_buf.at[slot], load_sem.at[slot])
 
+    def c(t):
+        scatter.c_start(t, away(t))
+        load(t).start()
+
+    def a(t):
+        load(t).wait()
+        scatter.a_start(t, l_buf.at[t % 2], away(t))
+
     def leave(t):
-        if t < TICKS:
-            scatter.c_start(t, away(t))
-            load(t).start()
+        c(t)
         if t >= 1:
-            load(t - 1).wait()
-            scatter.a_start(t - 1, l_buf.at[(t - 1) % 2], away(t - 1))
+            a(t - 1)
 
     b, z, tick = scatter.b_start, scatter.z_start, gather.tick
 
@@ -569,17 +575,17 @@
                 move(*args)
 
     gather.z_start(0)
-    gather.z_start(1)
-
-    @pl.when(half == 0)
-    def _():
-        x_copy.start()
-
-    gather.z_start(2)
     table_own[...] = jnp.zeros_like(table_own)
     table_own[0 : table_in.shape[0], 0 : table_in.shape[1]] = table_in[...]
     for copy in tables:
         copy.start()
+    gather.z_start(1)
+
+    @pl.when(half == 0)
+    def _():
+        x_copy.start()
+
+    gather.z_start(2)
     for k in range(3, gather.ahead):
         gather.z_start(k)
 
@@ -600,15 +606,12 @@
         turn = (offset + column == rows) | (offset + column == rows + span)
         onehot[:, start : start + 128] = mm(plain, jnp.where(turn, 1.0, 0.0).astype(BF16))
 
-    turns = [onehot[...]] + [pltpu.roll(onehot[...], k, 1) for k in range(1, 8)]
-    spread[...] = jnp.transpose(jnp.concatenate(turns, axis=0))
-
     length = len_ref[lax.div(z_me, halves)]
     i = lax.broadcasted_iota(jnp.int32, mask.shape, 0)
-    c = lax.broadcasted_iota(jnp.int32, mask.shape, 1)
-    own = c - rows
+    column = lax.broadcasted_iota(jnp.int32, mask.shape, 1)
+    own = column - rows
     limit = jnp.where(half > 0, length, 0)
-    ok = ((own < 0) & (c < limit)) | ((own >= 0) & (own <= i) & (own + half * rows < length))
+    ok = ((own < 0) & (column < limit)) | ((own >= 0) & (own <= i) & (own + half * rows < length))
     mask[...] = jnp.where(ok, 0.0, MASKED)
     tick(1)
     enc_copy.start()
@@ -696,6 +699,9 @@
     lax.fori_loop(0, parts, self_step, 0)
     x1[...] = acc[...]
     n2[...] = low(norm_rows(acc[...], line_of(gain2))[0])
+
+    turns = [onehot[...]] + [pltpu.roll(onehot[...], k, 1) for k in range(1, 8)]
+    spread[...] = jnp.transpose(jnp.concatenate(turns, axis=0))
 
     enc_copy.wait()
     enc_here.wait()
@@ -893,15 +899,16 @@
 
     def self_back_step(i, carry):
         def middle(i):
-            at(i, 0, (b, 10), (z, 9))
-            at(i, 1, (z, 10))
-            at(i, 2, (z, 11))
+            at(i, 0, (a, 11), (b, 10), (z, 9))
+            at(i, 1, (a, 12), (b, 11), (z, 10))
+            at(i, 2, (a, 13), (b, 12), (z, 11))
+            at(i, 3, (a, 14), (b, 13), (z, 12))
 
         attention_step(0, i, middle)
-        at(i, 0, (leave, 12))
-        at(i, 1, (leave, 13), (b, 11))
-        at(i, 2, (leave, 14), (b, 12))
-        at(i, 3, (leave, 15), (b, 13), (z, 12))
+        at(i, 0, (c, 12))
+        at(i, 1, (c, 13))
+        at(i, 2, (c, 14))
+        at(i, 3, (c, 15))
         return carry
 
     lax.fori_loop(0, parts, self_back_step, 0)
@@ -915,7 +922,9 @@
     def _():
         dxa_copy.start()
 
-    leave(16)
+    a(15)
+    b(14)
+    z(13)
     back, sum1 = norm_back(
         acc[...] + enc_acc[rows : 2 * rows, :], x_ref[...].astype(F32), gain
     )
@@ -950,8 +959,6 @@
     for copy in own_copies(3, 1):
         copy.wait()
     x2[...] += mm(hid[0], block(w, 0, 1))
-    b(14)
-    z(13)
     far_copy(3, 1, 1, 1).wait()
     x2[...] += mm(hid[1], block(w, 1, 1))
     sums.turn()
@@ -1100,8 +1107,8 @@
             bf(rows, width), bf(enc_rows, width), ff(8, width // 2),
             bf(C_RING, 4, share, width), bf(A_RING, 2, 2, half_share, width),
             bf(B_RING, 2, half_share, width), bf(TICKS, share, width),
-            bf(2, 2, 2, half_share, width), bf(KEEP, 2, 2, half_share, width),
-            bf(2, 2, half_share, width), ff(KEEP, 2, half_share, width),
+            bf(OUT_RING, 2, 2, half_share, width), bf(KEEP, 2, 2, half_share, width),
+            bf(OUT_RING, 2, half_share, width), ff(KEEP, 2, half_share, width),
             bf(Z_RING, share, width), ff(8, 8, width // 2), ff(parts, 8, width // 2),
             dma(2, 2), dma(2, 4), pltpu.SemaphoreType.DMA, dma(5, 2), dma(5, 2), dma(2), dma(2),
             dma(2),

time: 211 us -> 207 us (0.981)
  Pallas kernels: 210 us -> 206 us
    pallas_call x1, Pallas kernels: 206 us -> 202 us  [body(): pl.pallas_call(functools.partial(layer_kernel, halves), out_shape=[sds((r...]
where the time goes in v6:
time: 207 us
  Pallas kernels  206 us (100%)
    pallas_call x1, Pallas kernels, body(): pl.pallas_call(functools.partial(layer_kernel, halves), out_shape=[sds((r...  202 us

profile of v6, /device:TPU:0, one launch (start us, length us, event | category | flops | bytes accessed | tf_op | source)
XLA Modules:
  0.0 206.6 jit_solution(5673143724333530134)
XLA Ops:
  0.7 202.0 %layer.1 = (bf16[320,768]{1,0:T(8,128)(2,1)}, f32[4,96,768]{2,1,0:T(8,128)}, f32[8,384]{1,0:T(8,128)}, bf16[320,768]{1,0:T(8,128)(2,1)}, bf16[512,768]{1,0:T(8,1...) custom-call(s32[2]{0:T(128)} %len_ref.1, ...), custom_call_target="tpu_custom_call" | custom-call | tf_op jit(solution)/shard_map/layer/pallas_call | solution.py:1082
  202.6 3.9 %finish.1 = (bf16[320,768]{1,0:T(8,128)(2,1)}, bf16[320,768]{1,0:T(8,128)(2,1)}, bf16[512,768]{1,0:T(8,128)(2,1)}, f32[768]{0:T(1024)}, f32[96,192]{1,0:T(8,128)...) custom-call(bf16[320,768]{1,0:T(8,128)(2,1)} %get-tuple-element.39.r, ...), custom_call_target="tpu_custom_call" | custom-call | tf_op jit(solution)/shard_map/finish/pallas_call | solution.py:1131

commit v7 on v6

--- a/solution.py
+++ b/solution.py
@@ -870,14 +870,15 @@
     def cross_back_step(i, carry):
         def middle(i):
             at(i, 0, (leave, 7), (b, 4), (z, 3))
-            at(i, 1, (leave, 8), (b, 6), (z, 5))
-            at(i, 2, (b, 7), (z, 6))
-            at(i, 3, (leave, 10), (b, 8), (z, 7))
+            at(i, 1, (a, 7), (b, 6), (z, 5))
+            at(i, 2, (a, 9), (b, 7), (z, 6))
+            at(i, 3, (a, 10), (b, 8), (z, 7))
 
         attention_step(1, i, middle)
-        at(i, 0, (b, 5), (z, 4))
-        at(i, 1, (leave, 9))
-        at(i, 3, (leave, 11))
+        at(i, 0, (c, 8), (b, 5), (z, 4))
+        at(i, 1, (a, 8), (c, 9))
+        at(i, 2, (c, 10))
+        at(i, 3, (c, 11))
         return carry
 
     lax.fori_loop(0, parts, cross_back_step, 0)

time: 207 us -> 210 us (1.014)
  Pallas kernels: 206 us -> 209 us
    pallas_call x1, Pallas kernels: 202 us -> 205 us  [body(): pl.pallas_call(functools.partial(layer_kernel, halves), out_shape=[sds((r...]
where the time goes in v7:
time: 210 us
  Pallas kernels  209 us (100%)
    pallas_call x1, Pallas kernels, body(): pl.pallas_call(functools.partial(layer_kernel, halves), out_shape=[sds((r...  205 us

profile of v7, /device:TPU:0, one launch (start us, length us, event | category | flops | bytes accessed | tf_op | source)
XLA Modules:
  0.0 209.6 jit_solution(17778854870172616323)
XLA Ops:
  0.7 204.9 %layer.1 = (bf16[320,768]{1,0:T(8,128)(2,1)}, f32[4,96,768]{2,1,0:T(8,128)}, f32[8,384]{1,0:T(8,128)}, bf16[320,768]{1,0:T(8,128)(2,1)}, bf16[512,768]{1,0:T(8,1...) custom-call(s32[2]{0:T(128)} %len_ref.1, ...), custom_call_target="tpu_custom_call" | custom-call | tf_op jit(solution)/shard_map/layer/pallas_call | solution.py:1083
  205.6 3.9 %finish.1 = (bf16[320,768]{1,0:T(8,128)(2,1)}, bf16[320,768]{1,0:T(8,128)(2,1)}, bf16[512,768]{1,0:T(8,128)(2,1)}, f32[768]{0:T(1024)}, f32[96,192]{1,0:T(8,128)...) custom-call(bf16[320,768]{1,0:T(8,128)(2,1)} %get-tuple-element.39.r, ...), custom_call_target="tpu_custom_call" | custom-call | tf_op jit(solution)/shard_map/finish/pallas_call | solution.py:1132
